TPU v7x, 256 devices: a whole 4x4x8 slice. The times are simulated.
256 devices in a mesh: dp: 4 (over y), frame: 4 (over x), height: 16 (over z, core).
Axes of the slice: x: 4, y: 4, z: 8, core: 2. Of those that a mesh axis runs over, the one named last changes fastest.
Arguments:
- clip_latents: bfloat16 [4, 8, 32, 64, 384], P('dp', 'frame', 'height'), may hold values from -6 to 6
- conv_one: bfloat16 [3, 3, 3, 384, 384], replicated, may hold values from -0.0625 to 0.0625
- conv_two: bfloat16 [3, 3, 384, 192], replicated, may hold values from -0.109375 to 0.109375
- cotangent: bfloat16 [4, 8, 64, 128, 192], P('dp', 'frame', 'height'), may hold values from -6 to 6
Outputs:
- grad_latents: bfloat16 [4, 8, 32, 64, 384], P('dp', 'frame', 'height')
- grad_conv_one: float32 [3, 3, 3, 384, 384], P(None, None, None, ('dp', 'frame'), 'height')
- grad_conv_two: float32 [3, 3, 384, 192], P(None, None, ('dp', 'frame'), 'height')
All inputs are finite; a program needn't handle non-finite values.
Results may differ from a plain program's by a relative error of at most 0.0049.
Values may be sent and summed in bfloat16 or wider, within the bound.
No kernel may reach another device: no remote copies, remote signals or barrier semaphores. Data moves between devices by JAX's collectives and lax.ppermute only.
A program may use at most 128 MiB of HBM per device.

v0:
```python
import jax
import jax.numpy as jnp
from jax import lax
from jax.sharding import PartitionSpec as P


def shifted(value, axis, steps):
    count = lax.axis_size(axis)
    initial, last = (max(0, -steps), min(count, count - steps))
    return lax.ppermute(value, axis, [(source, source + steps) for source in range(initial, last)])


def extended(value, sides, width):
    for axis, dim in sides:
        size, length = (lax.axis_size(axis), value.shape[dim])
        up = [(i, (i + 1) % size) for i in range(size - 1)]
        down = [(j, i) for i, j in up]
        last = lax.slice_in_dim(value, length - width, length, axis=dim)
        initial = lax.slice_in_dim(value, 0, width, axis=dim)
        before = lax.ppermute(last, axis, up)
        after = lax.ppermute(initial, axis, down)
        value = jnp.concatenate([before, value, after], axis=dim)
    return value


def forward_taps(padded, weight, shape_out):
    frames_n, rows_n, cols_n = shape_out
    summed = jnp.zeros((frames_n, rows_n, cols_n, weight.shape[4]), jnp.float32)
    for frame_tap in range(3):
        for row_tap in range(3):
            for column_tap in range(3):
                window = padded[
                    frame_tap : frame_tap + frames_n,
                    row_tap : row_tap + rows_n,
                    column_tap : column_tap + cols_n,
                ]
                summed = summed + jnp.einsum(
                    "frwc,cd->frwd",
                    window,
                    weight[frame_tap, row_tap, column_tap],
                    preferred_element_type=jnp.float32,
                )
    return summed


def backward_taps(padded, weight, shape_out):
    frames_n, rows_n, cols_n = shape_out
    summed = jnp.zeros((frames_n, rows_n, cols_n, weight.shape[3]), jnp.float32)
    for frame_tap in range(3):
        for row_tap in range(3):
            for column_tap in range(3):
                window = padded[
                    2 - frame_tap : 2 - frame_tap + frames_n,
                    2 - row_tap : 2 - row_tap + rows_n,
                    2 - column_tap : 2 - column_tap + cols_n,
                ]
                summed = summed + jnp.einsum(
                    "frwd,cd->frwc",
                    window,
                    weight[frame_tap, row_tap, column_tap],
                    preferred_element_type=jnp.float32,
                )
    return summed


def weight_taps(padded, grad_out):
    frames_n, rows_n, cols_n = grad_out.shape[:3]
    taps_list = []
    for frame_tap in range(3):
        for row_tap in range(3):
            for column_tap in range(3):
                window = padded[
                    frame_tap : frame_tap + frames_n,
                    row_tap : row_tap + rows_n,
                    column_tap : column_tap + cols_n,
                ]
                taps_list.append(
                    jnp.einsum(
                        "frwc,frwd->cd", window, grad_out, preferred_element_type=jnp.float32
                    )
                )
    stacked = jnp.stack(taps_list)
    return stacked.reshape((3, 3, 3) + stacked.shape[1:])


def plane_backward(padded, weight, shape_out):
    frames_n, rows_n, cols_n = shape_out
    summed = jnp.zeros((frames_n, rows_n, cols_n, weight.shape[2]), jnp.float32)
    for row_tap in range(3):
        for column_tap in range(3):
            window = padded[
                :, 2 - row_tap : 2 - row_tap + rows_n, 2 - column_tap : 2 - column_tap + cols_n
            ]
            summed = summed + jnp.einsum(
                "frwd,cd->frwc",
                window,
                weight[row_tap, column_tap],
                preferred_element_type=jnp.float32,
            )
    return summed


def plane_weight(padded, grad_out):
    frames_n, rows_n, cols_n = grad_out.shape[:3]
    taps_list = []
    for row_tap in range(3):
        for column_tap in range(3):
            window = padded[:, row_tap : row_tap + rows_n, column_tap : column_tap + cols_n]
            taps_list.append(
                jnp.einsum("frwc,frwd->cd", window, grad_out, preferred_element_type=jnp.float32)
            )
    stacked = jnp.stack(taps_list)
    return stacked.reshape((3, 3) + stacked.shape[1:])


def pad_columns(field):
    return jnp.pad(field, ((0, 0), (0, 0), (1, 1), (0, 0)))


def pad_plane(field):
    return jnp.pad(field, ((0, 0), (1, 1), (1, 1), (0, 0)))


def local(clip_latents, conv_one, conv_two, cotangent):
    latents = clip_latents[0]
    upstream = cotangent[0]
    frames_n, rows_n, cols_n = latents.shape[:3]
    band = lax.axis_index("height")
    gathered = lax.all_gather(latents, "height", axis=1, tiled=True)
    latent_prev = shifted(gathered, "frame", 1)
    full_in = pad_plane(jnp.concatenate([latent_prev, gathered], axis=0))
    padded_in = lax.dynamic_slice_in_dim(full_in, band * rows_n, rows_n + 2, 1)
    preact = forward_taps(padded_in, conv_one, (frames_n, rows_n, cols_n))
    hidden = jax.nn.silu(preact).astype(jnp.bfloat16)
    hidden_all = lax.all_gather(hidden, "height", axis=1, tiled=True)
    padded_up = pad_plane(jnp.repeat(jnp.repeat(hidden_all, 2, axis=1), 2, axis=2))
    upstream_cols = lax.all_to_all(upstream, "height", split_axis=3, concat_axis=1, tiled=True)
    grad_two = plane_weight(padded_up, upstream_cols)
    upstream_ext = extended(upstream, (("height", 1),), 1)
    padded_cot = pad_columns(upstream_ext)
    grad_larger = plane_backward(padded_cot, conv_two, (frames_n, 2 * rows_n, 2 * cols_n))
    grad_hidden = grad_larger.reshape(frames_n, rows_n, 2, cols_n, 2, -1).sum(axis=(2, 4))
    sigma = jax.nn.sigmoid(preact)
    grad_pre = (grad_hidden * sigma * (1.0 + preact * (1.0 - sigma))).astype(jnp.bfloat16)
    pregrad_cols = lax.all_to_all(grad_pre, "height", split_axis=3, concat_axis=1, tiled=True)
    grad_one = weight_taps(full_in, pregrad_cols)
    pregrad_ext = extended(grad_pre, (("height", 1),), 1)
    pregrad_next_block = shifted(pregrad_ext, "frame", -1)
    padded_grad = pad_columns(jnp.concatenate([pregrad_ext, pregrad_next_block], axis=0))
    grad_in = backward_taps(padded_grad, conv_one, (frames_n, rows_n, cols_n)).astype(jnp.bfloat16)
    share_one, share_two = (
        lax.psum_scatter(grad_one, "dp", scatter_dimension=3, tiled=True),
        lax.psum_scatter(grad_two, "dp", scatter_dimension=2, tiled=True),
    )
    final_one, final_two = (
        lax.psum_scatter(share_one, "frame", scatter_dimension=3, tiled=True),
        lax.psum_scatter(share_two, "frame", scatter_dimension=2, tiled=True),
    )
    return (grad_in[None], final_one, final_two)


def solution(mesh):
    placed = (
        P("dp", "frame", "height", None, None),
        P(),
        P(),
        P("dp", "frame", "height", None, None),
    )
    return jax.shard_map(
        local,
        mesh=mesh,
        in_specs=placed,
        out_specs=(
            P("dp", "frame", "height", None, None),
            P(None, None, None, ("dp", "frame"), "height"),
            P(None, None, ("dp", "frame"), "height"),
        ),
        check_vma=False,
    )
```

profile of v0, /device:TPU:8, one launch (start us, length us, event | category | flops | bytes accessed | tf_op | source)
XLA Modules:
  0.0 360.3 jit_solution(5364764246763198460)
XLA Ops:
  7.9 45.9 %all-gather.6.cloned.1.call-done = bf16[1,2,32,64,384]{4,3,2,1,0:T(8,128)(2,1)} async-done(((bf16[1,2,2,64,384]{4,3,2,1,0:T(8,128)(2,1)}), bf16[1,2,32,64,384]{4,3,2,1,0:T(8,128)(2,1)}) %all-gather.6.cloned.1.call-update) | async-done | bytes 3145744 | tf_op jit(solution)/shard_map/all_gather | solution.py:129
  53.8 5.1 %collective-permute-start.2 = (bf16[2,32,64,384]{3,2,1,0:T(8,128)(2,1)}, bf16[2,32,64,384]{3,2,1,0:T(8,128)(2,1)}, u32[]{:S(2)}, u32[]{:S(2)}) collective-permute-start(bf16[2,32,64,384]{3,2,1,0:T(8,128)(2,1)} %bitcast.704), channel_id=1, source_target_pairs={{0,16},{16,32},{32,48},{1,17},{17,33},{33,49},{2,18},{18,34},{34,5... | collective-permute-start | bytes 9437192 | tf_op jit(solution)/shard_map/ppermute | solution.py:10
  59.8 1.9 collective-permute-start
  61.7 1.3 collective-permute-start.1
  63.0 2.1 copy.19
  65.1 8.1 %all-to-all-start.1 = ((bf16[2,4,128,192]{2,1,0,3:T(4,128)(2,1)}), bf16[2,4,128,192]{2,1,0,3:T(4,128)(2,1)}, u32[]{:S(2)}, u32[]{:S(2)}) async-start(bf16[2,4,128,192]{2,1,0,3:T(4,128)(2,1)} %copy.19), calls=%async_computation.3 | async-start | bytes 786432 | tf_op jit(solution)/shard_map/all_to_all | solution.py:137
  73.2 2.7 fusion.539
  75.9 1.6 fusion.115
  77.5 1.4 fusion.318
  82.4 3.1 add_add_fusion
  85.5 3.5 reshape.21
  89.0 3.3 reduce_sum.9
  92.2 33.0 %collective-permute-done.2 = bf16[2,32,64,384]{3,2,1,0:T(8,128)(2,1)} collective-permute-done((bf16[2,32,64,384]{3,2,1,0:T(8,128)(2,1)}, bf16[2,32,64,384]{3,2,1,0:T(8,128)(2,1)}, u32[]{:S(2)}, u32[]{:S(2)}) %collective-permute-start.2) | collective-permute-done | bytes 3145760 | tf_op jit(solution)/shard_map/ppermute | solution.py:10
  125.2 2.6 pad_maximum_fusion
  127.8 1.6 fusion.346
  129.5 3.1 fusion.352
  140.9 1.6 multiply_convert_fusion
  143.6 1.9 reshape.104
  145.5 4.5 %all-to-all-start = ((bf16[16,2,3072]{2,1,0:T(2,128)(2,1)}), bf16[16,2,3072]{2,1,0:T(2,128)(2,1)}, u32[]{:S(2)}, u32[]{:S(2)}) async-start(bf16[16,2,3072]{2,1,0:T(2,128)(2,1)} %reshape.104), calls=%async_computation | async-start | bytes 393216 | tf_op jit(solution)/shard_map/all_to_all | solution.py:145
  152.1 3.0 collective-permute-start.3
  156.4 2.0 copy.21
  159.3 1.5 collective-permute-start.5
  160.8 2.0 reshape.105
  164.0 3.0 fusion.121
  169.5 2.5 fusion.263
  178.5 2.0 fusion.264
  192.2 4.6 %copy.18 = f32[3,3,3,384,24]{4,3,2,1,0:T(8,128)} copy(f32[3,3,3,384,24]{3,4,2,1,0:T(8,128)} %bitcast.727) | data formatting | bytes 1990656 | tf_op jit(solution)/shard_map/reshape | solution.py:83
  198.5 1.3 fusion.360
  202.5 1.4 fusion.375
  220.8 2.9 broadcast_in_dim.10
  223.8 10.6 %broadcast_in_dim.11 = bf16[2,64,64,2,384]{4,3,2,1,0:T(2,128)(2,1)} broadcast(bf16[2,64,64,384]{3,2,1,0:T(8,128)(2,1)S(1)} %bitcast.707), dimensions={0,1,2,4} | broadcast | bytes 18874368 | tf_op jit(solution)/shard_map/broadcast_in_dim | solution.py:136
  234.4 26.2 %reshape.24 = bf16[2,64,128,384]{3,2,1,0:T(8,128)(2,1)} reshape(bf16[2,64,64,2,384]{4,3,2,1,0:T(2,128)(2,1)} %broadcast_in_dim.11) | data formatting | bytes 25165824 | tf_op jit(solution)/shard_map/reshape | solution.py:136
  260.6 7.3 %fusion.268 = f32[9,384,12]{1,2,0:T(8,128)S(1)} fusion(bf16[2,64,128,12]{2,3,1,0:T(8,128)(2,1)S(1)} %bitcast.714, bf16[2,64,128,384]{3,2,1,0:T(8,128)(2,1)} %reshape.24), kind=kOutput, calls=%fused_computation.191 | convolution fusion | flops 150994944 | bytes 13000704 | tf_op jit(solution)/shard_map/frwc,frwd->cd/dot_general | solution.py:110
  268.8 1.7 fusion.274
  270.6 3.0 fusion.280
  273.6 3.1 fusion.286
  276.7 1.7 fusion.313
  278.4 3.3 fusion.292
  281.7 3.0 fusion.298
  284.7 1.7 fusion.304
  286.4 3.0 fusion.310
  290.2 2.5 copy.95
  292.6 1.6 reshape.99
  294.3 1.4 convolution_add_fusion.8
  298.3 1.9 fusion.117
  300.2 21.5 %reduce-scatter.11.cloned.1.call-done = f32[96,108]{1,0:T(8,128)} async-done(((f32[384,108]{1,0:T(8,128)}), f32[96,108]{1,0:T(8,128)}) %reduce-scatter.11.cloned.1.call-update) | async-done | bytes 41488
  323.0 17.8 %all-reduce.4 = f32[3,3,96,12]{2,3,1,0:T(8,128)S(1)} all-reduce(f32[3,3,96,12]{2,3,1,0:T(8,128)S(1)} %copy.96), channel_id=6, replica_groups=mesh['dp'=4,'frame'=4,'height'=16] {'frame'}, use_global_device_ids=true, to_apply=%region_4.5.clone | all-reduce | flops 10368 | bytes 82944
  341.6 11.9 %reduce-scatter.9.cloned.1.call-done = f32[3,3,3,24,24]{4,3,2,1,0:T(8,128)} async-done(((f32[3,3,3,96,24]{4,3,2,1,0:T(8,128)}), f32[3,3,3,24,24]{4,3,2,1,0:T(8,128)}) %reduce-scatter.9.cloned.1.call-update) | async-done | bytes 62224 | tf_op jit(solution)/shard_map/reduce_scatter | solution.py:156
  (142 shorter events, 67.0 us)
Async XLA Ops:
  7.2 70.3 %copy-start.4 = (bf16[1,2,4,128,192]{3,4,2,1,0:T(8,128)(2,1)S(1)}, bf16[1,2,4,128,192]{3,4,2,1,0:T(8,128)(2,1)}, u32[]{:S(2)}) copy-start(bf16[1,2,4,128,192]{3,4,2,1,0:T(8,128)(2,1)} %param.7) | copy-start | bytes 1179652
  7.2 71.7 %copy-start.8 = (bf16[3,3,384,192]{2,3,1,0:T(8,128)(2,1)S(1)}, bf16[3,3,384,192]{2,3,1,0:T(8,128)(2,1)}, u32[]{:S(2)}) copy-start(bf16[3,3,384,192]{2,3,1,0:T(8,128)(2,1)} %param.6) | copy-start | bytes 3981316
  7.2 46.6 %all-gather.6.cloned.1.call-start = ((), (), s32[]{:S(2)}) async-start(), calls=%async_computation.8 | async-start | bytes 3342336 | tf_op jit(solution)/shard_map/all_gather | solution.py:129
  53.8 71.4 %collective-permute-start.2 = (bf16[2,32,64,384]{3,2,1,0:T(8,128)(2,1)}, bf16[2,32,64,384]{3,2,1,0:T(8,128)(2,1)}, u32[]{:S(2)}, u32[]{:S(2)}) collective-permute-start(bf16[2,32,64,384]{3,2,1,0:T(8,128)(2,1)} %bitcast.704), channel_id=1, source_target_pairs={{0,16},{16,32},{32,48},{1,17},{17,33},{33,49},{2,18},{18,34},{34,5... | collective-permute-start | bytes 9437192 | tf_op jit(solution)/shard_map/ppermute | solution.py:10
  59.8 16.1 %collective-permute-start = (bf16[2,1,128,192]{2,3,1,0:T(8,128)(2,1)S(1)}, bf16[2,1,128,192]{2,3,1,0:T(8,128)(2,1)S(1)}, u32[]{:S(2)}, u32[]{:S(2)}) collective-permute-start(bf16[2,1,128,192]{2,3,1,0:T(8,128)(2,1)S(1)} %get-tuple-element.6), channel_id=1, source_target_pairs={{0,1},{1,2},{2,3},{3,4},{4,5},{5,6},{6,7},{7,8},{8,9},{9,10},{10,1... | collective-permute-start | bytes 294920 | tf_op jit(solution)/shard_map/ppermute | solution.py:20
  61.7 14.2 %collective-permute-start.1 = (bf16[2,1,128,192]{2,3,1,0:T(8,128)(2,1)S(1)}, bf16[2,1,128,192]{2,3,1,0:T(8,128)(2,1)S(1)}, u32[]{:S(2)}, u32[]{:S(2)}) collective-permute-start(bf16[2,1,128,192]{2,3,1,0:T(8,128)(2,1)S(1)} %get-tuple-element.5), channel_id=1, source_target_pairs={{1,0},{2,1},{3,2},{4,3},{5,4},{6,5},{7,6},{8,7},{9,8},{10,9},{11,1... | collective-permute-start | bytes 294920 | tf_op jit(solution)/shard_map/ppermute | solution.py:21
  65.1 80.5 %all-to-all-start.1 = ((bf16[2,4,128,192]{2,1,0,3:T(4,128)(2,1)}), bf16[2,4,128,192]{2,1,0,3:T(4,128)(2,1)}, u32[]{:S(2)}, u32[]{:S(2)}) async-start(bf16[2,4,128,192]{2,1,0,3:T(4,128)(2,1)} %copy.19), calls=%async_computation.3 | async-start | bytes 786432 | tf_op jit(solution)/shard_map/all_to_all | solution.py:137
  78.9 3.5 copy-start.5
  82.4 42.8 %copy-start.3 = (bf16[1,2,32,64,384]{4,3,2,1,0:T(8,128)(2,1)S(1)}, bf16[1,2,32,64,384]{4,3,2,1,0:T(8,128)(2,1)}, u32[]{:S(2)}) copy-start(bf16[1,2,32,64,384]{4,3,2,1,0:T(8,128)(2,1)} %all-gather.6.cloned.1.call-done) | copy-start | bytes 9437188
  127.8 12.7 %copy-start = (bf16[4,32,64,384]{3,2,1,0:T(8,128)(2,1)}, bf16[4,32,64,384]{3,2,1,0:T(8,128)(2,1)S(1)}, u32[]{:S(2)}) copy-start(bf16[4,32,64,384]{3,2,1,0:T(8,128)(2,1)S(1)} %pad_maximum_fusion) | copy-start | bytes 18874372
  127.8 6.0 %slice-start = ((s8[7962624]{0:T(1024)(128)(4,1)}), s8[4194304]{0:T(1024)(128)(4,1)S(1)}, s32[]{:S(2)}) async-start(s8[7962624]{0:T(1024)(128)(4,1)} %bitcast.700), calls=%async_computation.10 | async-start | bytes 8388608
  129.5 4.4 %slice-start.1 = ((s8[7962624]{0:T(1024)(128)(4,1)}), s8[3768320]{0:T(1024)(128)(4,1)S(1)}, s32[]{:S(2)}) async-start(s8[7962624]{0:T(1024)(128)(4,1)} %bitcast.700), calls=%async_computation.11 | async-start | bytes 7536640
  139.9 1.0 copy-start.7
  140.9 14.2 %copy-start.11 = (u32[256]{0:T(256)S(1)}, u32[256]{0:T(256)}, u32[]{:S(2)}) copy-start(u32[256]{0:T(256)} %constant.30) | copy-start | bytes 3076
  145.5 15.2 %all-to-all-start = ((bf16[16,2,3072]{2,1,0:T(2,128)(2,1)}), bf16[16,2,3072]{2,1,0:T(2,128)(2,1)}, u32[]{:S(2)}, u32[]{:S(2)}) async-start(bf16[16,2,3072]{2,1,0:T(2,128)(2,1)} %reshape.104), calls=%async_computation | async-start | bytes 393216 | tf_op jit(solution)/shard_map/all_to_all | solution.py:145
  150.1 70.8 %all-gather.4.cloned.1.call-start = ((), (), s32[]{:S(2)}) async-start(), calls=%async_computation.7 | async-start | bytes 3342336 | tf_op jit(solution)/shard_map/all_gather | solution.py:135
  150.8 7.6 %collective-permute-start.4 = (bf16[2,1,64,384]{3,2,1,0:T(8,128)(2,1)}, bf16[2,1,64,384]{3,2,1,0:T(8,128)(2,1)S(1)}, u32[]{:S(2)}, u32[]{:S(2)}) collective-permute-start(bf16[2,1,64,384]{3,2,1,0:T(8,128)(2,1)} %get-tuple-element.8), channel_id=1, source_target_pairs={{1,0},{2,1},{3,2},{4,3},{5,4},{6,5},{7,6},{8,7},{9,8},{10,9},{11,1... | collective-permute-start | bytes 294920 | tf_op jit(solution)/shard_map/ppermute | solution.py:21
  152.1 6.3 %collective-permute-start.3 = (bf16[2,1,64,384]{3,2,1,0:T(8,128)(2,1)}, bf16[2,1,64,384]{3,2,1,0:T(8,128)(2,1)S(1)}, u32[]{:S(2)}, u32[]{:S(2)}) collective-permute-start(bf16[2,1,64,384]{3,2,1,0:T(8,128)(2,1)} %get-tuple-element.7), channel_id=1, source_target_pairs={{0,1},{1,2},{2,3},{3,4},{4,5},{5,6},{6,7},{7,8},{8,9},{9,10},{10,1... | collective-permute-start | bytes 294920 | tf_op jit(solution)/shard_map/ppermute | solution.py:20
  158.4 138.6 %reduce-scatter.7.cloned.1.call-start = ((), (), s32[]{:S(2)}) async-start(), calls=%async_computation.5 | async-start | bytes 6635520 | tf_op jit(solution)/shard_map/reduce_scatter | solution.py:152
  159.3 38.0 %collective-permute-start.5 = (bf16[2,4,64,384]{3,2,1,0:T(8,128)(2,1)}, bf16[2,4,64,384]{3,2,1,0:T(8,128)(2,1)}, u32[]{:S(2)}, u32[]{:S(2)}) collective-permute-start(bf16[2,4,64,384]{3,2,1,0:T(8,128)(2,1)} %pad_maximum_fusion.2), channel_id=1, source_target_pairs={{16,0},{32,16},{48,32},{17,1},{33,17},{49,33},{18,2},{34,18},{50,3... | collective-permute-start | bytes 1179656 | tf_op jit(solution)/shard_map/ppermute | solution.py:10
  162.8 4.3 %copy-start.1 = (bf16[4,32,64,384]{3,2,1,0:T(8,128)(2,1)S(1)}, bf16[4,32,64,384]{3,2,1,0:T(8,128)(2,1)}, u32[]{:S(2)}) copy-start(bf16[4,32,64,384]{3,2,1,0:T(8,128)(2,1)} %copy-done) | copy-start | bytes 18874372
  191.3 1.0 copy-start.9
  196.8 124.9 %reduce-scatter.11.cloned.1.call-start = ((), (), s32[]{:S(2)}) async-start(), calls=%async_computation.9 | async-start | bytes 245760
  197.3 12.9 %slice-start.2 = ((s8[7962624]{0:T(1024)(128)(4,1)}), s8[3768320]{0:T(1024)(128)(4,1)S(1)}, s32[]{:S(2)}) async-start(s8[7962624]{0:T(1024)(128)(4,1)} %bitcast.702), calls=%async_computation.12 | async-start | bytes 7536640
  202.4 7.8 %slice-start.3 = ((s8[7962624]{0:T(1024)(128)(4,1)}), s8[4194304]{0:T(1024)(128)(4,1)S(1)}, s32[]{:S(2)}) async-start(s8[7962624]{0:T(1024)(128)(4,1)} %bitcast.702), calls=%async_computation.13 | async-start | bytes 8388608
  234.4 26.2 %copy-start.6 = (bf16[2,16,4,128,12]{3,4,2,1,0:T(8,128)(2,1)S(1)}, bf16[2,16,4,128,12]{3,4,2,1,0:T(8,128)(2,1)}, u32[]{:S(2)}) copy-start(bf16[2,16,4,128,12]{3,4,2,1,0:T(8,128)(2,1)} %copy.21) | copy-start | bytes 1179652
  260.6 8.2 %copy-start.2 = (bf16[2,64,128,384]{3,2,1,0:T(8,128)(2,1)S(1)}, bf16[2,64,128,384]{3,2,1,0:T(8,128)(2,1)}, u32[]{:S(2)}) copy-start(bf16[2,64,128,384]{3,2,1,0:T(8,128)(2,1)} %reshape.24) | copy-start | bytes 37748740
  289.5 0.7 copy-start.10
  294.3 59.2 %reduce-scatter.9.cloned.1.call-start = ((), (), s32[]{:S(2)}) async-start(), calls=%async_computation.6 | async-start | bytes 1658880 | tf_op jit(solution)/shard_map/reduce_scatter | solution.py:156
Sparse Core Ops, SparseCore 0:
  9.9 43.8 all-gather.5
  158.5 44.3 all-gather.3
  205.5 55.9 reduce-scatter.6
  294.4 27.2 reduce-scatter.10
  324.7 28.7 reduce-scatter.8
where the time goes:
time: 367 us; the launch traced here: 360 us
  waiting for transfers between devices  113 us (31%)
  matrix products  108 us (29%)
  local copies, waits for them, and re-layouts  69.5 us (19%)
  starting transfers between devices  27.2 us (7%)
  blocking collectives  17.8 us (5%)
  between operations  15.6 us (4%)
  other arithmetic  9.57 us (3%)
    all_gather x1, waiting for transfers between devices, local(): gathered = lax.all_gather(latents, 'height', axis=1, tiled=True)  45.9 us
    ppermute x2, waiting for transfers between devices, shifted(): lax.ppermute(value, axis, [(source, source + steps) for source in range(i...  33 us
    dot_general x9, matrix products, plane_weight(): jnp.einsum('frwc,frwd->cd', window, grad_out, preferred_element_type=jnp....  27.9 us
    dot_general x27, matrix products, backward_taps(): jnp.einsum('frwd,cd->frwc', window, weight[frame_tap, row_tap, column_tap...  27.9 us
    dot_general x27, matrix products, weight_taps(): jnp.einsum('frwc,frwd->cd', window, grad_out, preferred_element_type=jnp....  27.1 us
    reshape x1, local copies, waits for them, and re-layouts, local(): jnp.repeat(jnp.repeat(hidden_all, 2, axis=1), 2, axis=2)  26.2 us
    unnamed x6, waiting for transfers between devices  22.2 us
    unnamed x1, blocking collectives  17.8 us
  transfers between devices with their start and end apart: 13, of which 4 were waited for; matrix products, arithmetic and copies ran while one was open for 51% of the time, Pallas kernels for 0%

commit v1 on v0

v1 whole, which is shorter than its diff:
```python
import jax
import jax.numpy as jnp
from jax import lax
from jax.experimental import pallas as pl
from jax.experimental.pallas import tpu as pltpu
from jax.sharding import PartitionSpec as P

BF = jnp.bfloat16
F32 = jnp.float32
VMEM_LIMIT = 48 * 1024 * 1024


def params(**more):
    return pltpu.CompilerParams(vmem_limit_bytes=VMEM_LIMIT, **more)


def cost(macs, nbytes):
    return pl.CostEstimate(flops=2 * macs, bytes_accessed=nbytes, transcendentals=0)


def column_shifts(block):
    wide = block.astype(F32)
    row = lax.broadcasted_iota(jnp.int32, wide.shape, 0)
    before = jnp.where(row == 0, 0.0, pltpu.roll(wide, 1, 0))
    after = jnp.where(row == 63, 0.0, pltpu.roll(wide, 63, 0))
    return before.astype(BF), after.astype(BF)


def ext_row(own, other, up, down, frame, row):
    first, second = (other, own) if own is not None else (None, None)
    if row == 0:
        return up[frame]
    if row == 3:
        return down[frame]
    return first[frame, row - 1] if frame < 2 else second[frame - 2, row - 1]


def box_kernel(cot, up, down, w2, gcat, gh, taps):
    size = (64, 256)
    pos = lax.broadcasted_iota(jnp.int32, size, 1) & 127
    low = lax.broadcasted_iota(jnp.int32, size, 0)
    pick = []
    for k in range(3):
        offset = pos - 2 * low - 1 + k
        pick.append(jnp.where((offset == 0) | (offset == 1), 1.0, 0.0))
    pick = jnp.concatenate(pick, axis=0).astype(BF)

    def line(t, r):
        if r < 0:
            return up[t]
        if r > 3:
            return down[t]
        return cot[t, r]

    for t in range(2):
        for r in range(2):
            at = pl.ds((t * 2 + r) * 64, 64)
            for j in range(3):
                a = 2 * r + 1 - j
                pair = jnp.concatenate([line(t, a), line(t, a + 1)], axis=0)
                box = jnp.dot(pick, pair, preferred_element_type=F32).astype(BF)
                for k in range(3):
                    piece = box[k * 64 : (k + 1) * 64]
                    taps[j * 3 + k, at, :] = piece
                    gcat[at, pl.ds((j * 3 + k) * 192, 192)] = piece
    total = jnp.zeros((256, 384), F32)
    for n in range(9):
        total = total + lax.dot_general(
            taps[n], w2[n], (((1,), (1,)), ((), ())), preferred_element_type=F32
        )
    gh[...] = total


def box_sums(cot, up, down, w2):
    return pl.pallas_call(
        box_kernel,
        out_shape=(
            jax.ShapeDtypeStruct((256, 1728), BF),
            jax.ShapeDtypeStruct((256, 384), F32),
        ),
        scratch_shapes=[pltpu.VMEM((9, 256, 192), BF)],
        compiler_params=params(),
        cost_estimate=cost(300_000_000, 4_000_000),
        name="box_sums",
    )(cot, up, down, w2)


def forward_kernel(own, prev, up, down, w, gh, gp, gpt, ht, xx, acc):
    step = pl.program_id(0)

    @pl.when(step == 0)
    def _():
        for f in range(4):
            for r in range(4):
                block = ext_row(own, prev, up, down, f, r)
                before, after = column_shifts(block)
                xx[f, r, :, 0:384] = before
                xx[f, r, :, 384:768] = block
                xx[f, r, :, 768:1152] = after
        acc[...] = jnp.zeros_like(acc)

    i = step // 3
    j = step - 3 * i
    lhs = xx[pl.ds(i, 2), pl.ds(j, 2)].reshape(256, 1152)
    acc[...] += jnp.dot(lhs, w[0], preferred_element_type=F32)

    @pl.when(step == 8)
    def _():
        pre = acc[...]
        sigma = jax.nn.sigmoid(pre)
        hidden = pre * sigma
        grad = gh[...] * sigma * (1.0 + pre * (1.0 - sigma))
        gp[...] = grad.astype(BF).reshape(2, 2, 64, 384)
        grad_t = grad.T
        for b in range(16):
            gpt[b] = grad_t[b * 24 : (b + 1) * 24].astype(BF)
        ht[...] = hidden.T.astype(BF)


def whole(shape):
    return pl.BlockSpec(shape, lambda n: (0,) * len(shape))


def forward(own, prev, up, down, w, gh):
    return pl.pallas_call(
        forward_kernel,
        grid=(9,),
        in_specs=[
            whole((2, 2, 64, 384)),
            whole((2, 2, 64, 384)),
            whole((4, 64, 384)),
            whole((4, 64, 384)),
            pl.BlockSpec((1, 1152, 384), lambda n: (n, 0, 0)),
            whole((256, 384)),
        ],
        out_specs=(whole((2, 2, 64, 384)), whole((16, 24, 256)), whole((384, 256))),
        out_shape=(
            jax.ShapeDtypeStruct((2, 2, 64, 384), BF),
            jax.ShapeDtypeStruct((16, 24, 256), BF),
            jax.ShapeDtypeStruct((384, 256), BF),
        ),
        scratch_shapes=[pltpu.VMEM((4, 4, 64, 1152), BF), pltpu.VMEM((256, 384), F32)],
        compiler_params=params(),
        cost_estimate=cost(1_020_000_000, 10_000_000),
        name="forward",
    )(own, prev, up, down, w, gh)


def two_kernel(ht, gcat, out):
    res = jnp.dot(ht[...], gcat[...], preferred_element_type=F32)
    for b in range(16):
        out[b] = res[b * 24 : (b + 1) * 24].astype(BF)


def two_part(ht, gcat):
    return pl.pallas_call(
        two_kernel,
        out_shape=jax.ShapeDtypeStruct((16, 24, 1728), BF),
        compiler_params=params(),
        cost_estimate=cost(170_000_000, 3_000_000),
        name="two_part",
    )(ht, gcat)


def latents_kernel(own, after, up, down, w, out, gg, acc):
    step = pl.program_id(0)

    @pl.when(step == 0)
    def _():
        for f in range(4):
            for r in range(4):
                block = ext_row(after, own, up, down, f, r)
                before, later = column_shifts(block)
                gg[0, f, r] = later
                gg[1, f, r] = block
                gg[2, f, r] = before
        acc[...] = jnp.zeros_like(acc)

    i = step // 3
    j = step - 3 * i
    total = acc[...]
    for k in range(3):
        lhs = gg[k, pl.ds(2 - i, 2), pl.ds(2 - j, 2)].reshape(256, 384)
        total = total + lax.dot_general(
            lhs, w[0, k], (((1,), (1,)), ((), ())), preferred_element_type=F32
        )
    acc[...] = total

    @pl.when(step == 8)
    def _():
        out[...] = acc[...].astype(BF).reshape(2, 2, 64, 384)


def latents_grad(own, after, up, down, w):
    return pl.pallas_call(
        latents_kernel,
        grid=(9,),
        in_specs=[
            whole((2, 2, 64, 384)),
            whole((2, 2, 64, 384)),
            whole((4, 64, 384)),
            whole((4, 64, 384)),
            pl.BlockSpec((1, 3, 384, 384), lambda n: (n, 0, 0, 0)),
        ],
        out_specs=whole((2, 2, 64, 384)),
        out_shape=jax.ShapeDtypeStruct((2, 2, 64, 384), BF),
        scratch_shapes=[pltpu.VMEM((3, 4, 4, 64, 384), BF), pltpu.VMEM((256, 384), F32)],
        compiler_params=params(),
        cost_estimate=cost(1_020_000_000, 10_000_000),
        name="latents_grad",
    )(own, after, up, down, w)


def one_kernel(g, x, out, gs, acc):
    step = pl.program_id(0)

    @pl.when(step == 0)
    def _():
        acc[...] = jnp.zeros_like(acc)

    lane = lax.broadcasted_iota(jnp.int32, (24, 128), 1)
    col = lane & 63
    left = lane < 64

    def piece(h, f):
        mid = g[h, :, pl.ds(f * 128, 128)].astype(F32)
        later = jnp.where(col == 63, 0.0, pltpu.roll(mid, 127, 1))
        before = jnp.where(col == 0, 0.0, pltpu.roll(mid, 1, 1))
        return [later, mid, before]

    first = step * 4
    keep_top = (step > 0).astype(F32)
    keep_bottom = (step < 3).astype(F32)
    for f in range(4):
        cols = [[p * keep_top for p in piece(jnp.maximum(first - 1, 0), f)]]
        for h in range(4):
            cols.append(piece(first + h, f))
        cols.append([p * keep_bottom for p in piece(jnp.minimum(first + 4, 15), f)])
        for h in range(4):
            above, here, below = cols[h], cols[h + 1], cols[h + 2]
            rows = []
            for k in range(3):
                rows.append(pltpu.roll(jnp.where(left, below[k], here[k]), 64, 1))
            for k in range(3):
                rows.append(here[k])
            for k in range(3):
                rows.append(pltpu.roll(jnp.where(left, here[k], above[k]), 64, 1))
            rows.append(jnp.zeros((8, 128), F32))
            gs[f, :, pl.ds(h * 128, 128)] = jnp.concatenate(rows, axis=0).astype(BF)

    for s in range(2):
        xs = x[:, s].reshape(512, 384)
        lhs = gs[s : s + 3].reshape(672, 512)
        res = jnp.dot(lhs, xs, preferred_element_type=F32)
        for b in range(3):
            acc[b, 0:224] += res[b * 224 : (b + 1) * 224]

    @pl.when(step == 3)
    def _():
        for b in range(3):
            turned = acc[b].T
            for c in range(16):
                out[c, :, b * 256 : (b + 1) * 256] = turned[c * 24 : (c + 1) * 24].astype(BF)


def one_part(g, x):
    return pl.pallas_call(
        one_kernel,
        grid=(4,),
        in_specs=[
            whole((16, 24, 512)),
            pl.BlockSpec((4, 2, 2, 64, 384), lambda n: (n, 0, 0, 0, 0)),
        ],
        out_specs=whole((16, 24, 768)),
        out_shape=jax.ShapeDtypeStruct((16, 24, 768), BF),
        scratch_shapes=[pltpu.VMEM((4, 224, 512), BF), pltpu.VMEM((3, 256, 384), F32)],
        compiler_params=params(),
        cost_estimate=cost(1_020_000_000, 5_000_000),
        name="one_part",
    )(g, x)


def summed(ref):
    total = ref[0].astype(F32)
    for n in range(1, 16):
        total = total + ref[n].astype(F32)
    return total


def two_mid_kernel(parts, out):
    total = summed(parts)
    pad = jnp.zeros((24, 20), F32)
    for h in range(16):
        cut = [total[:, n * 192 + h * 12 : n * 192 + h * 12 + 12] for n in range(9)]
        out[h] = jnp.concatenate(cut + [pad], axis=1).astype(BF)


def two_mid(parts):
    return pl.pallas_call(
        two_mid_kernel,
        out_shape=jax.ShapeDtypeStruct((16, 24, 128), BF),
        compiler_params=params(),
        cost_estimate=cost(1_000_000, 1_500_000),
        name="two_mid",
    )(parts)


def final_one_kernel(parts, out):
    total = summed(parts)
    for i in range(3):
        for n in range(9):
            at = (2 - i) * 256 + n * 24
            out[i * 9 + n] = total[:, at : at + 24]


def final_one(parts):
    return pl.pallas_call(
        final_one_kernel,
        out_shape=jax.ShapeDtypeStruct((27, 24, 24), F32),
        compiler_params=params(),
        cost_estimate=cost(1_000_000, 800_000),
        name="final_one",
    )(parts)


def final_two_kernel(parts, out):
    total = summed(parts)
    for n in range(9):
        out[n] = total[:, n * 12 : (n + 1) * 12]


def final_two(parts):
    return pl.pallas_call(
        final_two_kernel,
        out_shape=jax.ShapeDtypeStruct((9, 24, 12), F32),
        compiler_params=params(),
        cost_estimate=cost(1_000_000, 200_000),
        name="final_two",
    )(parts)


def local(clip_latents, conv_one, conv_two, cotangent):
    x = clip_latents[0]
    cot = cotangent[0]
    heights = lax.axis_size("height")
    frames = lax.axis_size("frame")
    up_perm = [(n, n + 1) for n in range(heights - 1)]
    down_perm = [(n + 1, n) for n in range(heights - 1)]
    next_perm = [(n, n + 1) for n in range(frames - 1)]
    prev_perm = [(n + 1, n) for n in range(frames - 1)]

    x_all = lax.all_gather(x, "height", axis=0, tiled=False)

    x_prev = lax.ppermute(x, "frame", next_perm)
    cot_up = lax.ppermute(cot[:, 3], "height", up_perm)
    cot_down = lax.ppermute(cot[:, 0], "height", down_perm)
    x_up = lax.ppermute(jnp.concatenate([x_prev[:, 1], x[:, 1]], 0), "height", up_perm)
    x_down = lax.ppermute(jnp.concatenate([x_prev[:, 0], x[:, 0]], 0), "height", down_perm)

    gcat, gh = box_sums(cot, cot_up, cot_down, conv_two.reshape(9, 384, 192))
    gp, gpt, ht = forward(x, x_prev, x_up, x_down, conv_one.reshape(9, 1152, 384), gh)

    gpt_next = lax.ppermute(gpt, "frame", prev_perm)
    gp_next = gpt_next.reshape(384, 256).T.reshape(2, 2, 64, 384)
    g = lax.all_to_all(
        jnp.concatenate([gpt, gpt_next], axis=2), "height", 0, 0, tiled=True
    )
    g_up = lax.ppermute(jnp.concatenate([gp[:, 1], gp_next[:, 1]], 0), "height", up_perm)
    g_down = lax.ppermute(jnp.concatenate([gp[:, 0], gp_next[:, 0]], 0), "height", down_perm)

    two = two_part(ht, gcat)
    two = lax.all_to_all(two, ("dp", "frame"), 0, 0, tiled=True)
    grad_in = latents_grad(gp, gp_next, g_up, g_down, conv_one.reshape(9, 3, 384, 384))
    two = lax.all_to_all(two_mid(two), "height", 0, 0, tiled=True)

    one = lax.all_to_all(one_part(g, x_all), ("dp", "frame"), 0, 0, tiled=True)
    one = final_one(one).reshape(3, 3, 3, 24, 24)
    two = final_two(two).reshape(3, 3, 24, 12)
    return (grad_in[None], one, two)


def solution(mesh):
    placed = (
        P("dp", "frame", "height", None, None),
        P(),
        P(),
        P("dp", "frame", "height", None, None),
    )
    return jax.shard_map(
        local,
        mesh=mesh,
        in_specs=placed,
        out_specs=(
            P("dp", "frame", "height", None, None),
            P(None, None, None, ("dp", "frame"), "height"),
            P(None, None, ("dp", "frame"), "height"),
        ),
        check_vma=False,
    )
```

time: 367 us -> 150 us (0.41)
  the two profiles are of different devices: /device:TPU:8 before, /device:TPU:1 now
where the time goes in v1:
time: 150 us; the launch traced here: 149 us
  starting transfers between devices  55.9 us (37%)
  waiting for transfers between devices  37.9 us (25%)
  Pallas kernels  29.6 us (20%)
  between operations  14.3 us (10%)
  local copies, waits for them, and re-layouts  8.57 us (6%)
  other arithmetic  2.26 us (2%)
    ppermute x1, waiting for transfers between devices, local(): gpt_next = lax.ppermute(gpt, 'frame', prev_perm)  15.8 us
    all_to_all x1, starting transfers between devices, local(): lax.all_to_all(jnp.concatenate([gpt, gpt_next], axis=2), 'height', 0, 0,...  13.5 us
    all_to_all x1, waiting for transfers between devices, local(): lax.all_to_all(jnp.concatenate([gpt, gpt_next], axis=2), 'height', 0, 0,...  13.3 us
    pallas_call x1, Pallas kernels, latents_grad(): pl.pallas_call(latents_kernel, grid=(9,), in_specs=[whole((2, 2, 64, 384)...  9.7 us
    pallas_call x1, Pallas kernels, forward(): pl.pallas_call(forward_kernel, grid=(9,), in_specs=[whole((2, 2, 64, 384)...  9.08 us
    all_to_all x1, starting transfers between devices, local(): two = lax.all_to_all(two, ('dp', 'frame'), 0, 0, tiled=True)  8.45 us
    unnamed x14, local copies, waits for them, and re-layouts  7.36 us
    all_to_all x1, starting transfers between devices, local(): one = lax.all_to_all(one_part(g, x_all), ('dp', 'frame'), 0, 0, tiled=True)  7.34 us
  transfers between devices with their start and end apart: 13, of which 6 were waited for; matrix products, arithmetic and copies ran while one was open for 6% of the time, Pallas kernels for 19%

profile of v1, /device:TPU:1, one launch (start us, length us, event | category | flops | bytes accessed | tf_op | source)
XLA Modules:
  0.0 148.5 jit_solution(5478660222230813366)
XLA Ops:
  7.2 0.0 all-gather.2.cloned.1.call-start
  7.2 0.7 all-gather.2.cloned.1.call-update
  7.9 0.9 copy.48
  8.9 4.0 %collective-permute-start = (bf16[2,2,64,384]{3,2,0,1:T(8,128)(2,1)S(1)}, bf16[2,2,64,384]{3,2,0,1:T(8,128)(2,1)S(1)}, u32[]{:S(2)}, u32[]{:S(2)}) collective-permute-start(bf16[2,2,64,384]{3,2,0,1:T(8,128)(2,1)S(1)} %bitcast.49), channel_id=1, source_target_pairs={{0,16},{16,32},{32,48},{1,17},{17,33},{33,49},{2,18},{18,34},{34,5... | collective-permute-start | bytes 589832 | tf_op jit(solution)/shard_map/ppermute | solution.py:354
  12.8 1.2 copy.30
  14.1 2.3 %collective-permute-done = bf16[2,2,64,384]{3,2,0,1:T(8,128)(2,1)S(1)} collective-permute-done((bf16[2,2,64,384]{3,2,0,1:T(8,128)(2,1)S(1)}, bf16[2,2,64,384]{3,2,0,1:T(8,128)(2,1)S(1)}, u32[]{:S(2)}, u32[]{:S(2)}) %collective-permute-start) | collective-permute-done | bytes 196640 | tf_op jit(solution)/shard_map/ppermute | solution.py:354
  16.4 0.7 pad_maximum_fusion.1
  17.1 5.0 %collective-permute-start.1 = (bf16[4,64,384]{2,1,0:T(8,128)(2,1)}, bf16[4,64,384]{2,1,0:T(8,128)(2,1)S(1)}, u32[]{:S(2)}, u32[]{:S(2)}) collective-permute-start(bf16[4,64,384]{2,1,0:T(8,128)(2,1)} %pad_maximum_fusion.1), channel_id=1, source_target_pairs={{0,1},{1,2},{2,3},{3,4},{4,5},{5,6},{6,7},{7,8},{8,9},{9,10},{10,1... | collective-permute-start | bytes 589832 | tf_op jit(solution)/shard_map/ppermute | solution.py:357
  22.1 0.7 pad_maximum_fusion.2
  22.8 1.9 %collective-permute-start.2 = (bf16[4,64,384]{2,1,0:T(8,128)(2,1)}, bf16[4,64,384]{2,1,0:T(8,128)(2,1)S(1)}, u32[]{:S(2)}, u32[]{:S(2)}) collective-permute-start(bf16[4,64,384]{2,1,0:T(8,128)(2,1)} %pad_maximum_fusion.2), channel_id=1, source_target_pairs={{1,0},{2,1},{3,2},{4,3},{5,4},{6,5},{7,6},{8,7},{9,8},{10,9},{11,1... | collective-permute-start | bytes 589832 | tf_op jit(solution)/shard_map/ppermute | solution.py:358
  24.7 0.0 copy-start.2
  24.7 0.7 slice_bitcast_fusion
  25.4 3.6 %collective-permute-start.3 = (bf16[2,128,192]{2,1,0:T(8,128)(2,1)}, bf16[2,128,192]{2,1,0:T(8,128)(2,1)S(1)}, u32[]{:S(2)}, u32[]{:S(2)}) collective-permute-start(bf16[2,128,192]{2,1,0:T(8,128)(2,1)} %get-tuple-element.23), channel_id=1, source_target_pairs={{0,1},{1,2},{2,3},{3,4},{4,5},{5,6},{6,7},{7,8},{8,9},{9,10},{10,1... | collective-permute-start | bytes 294920 | tf_op jit(solution)/shard_map/ppermute | solution.py:355
  29.1 1.9 %collective-permute-start.4 = (bf16[2,128,192]{2,1,0:T(8,128)(2,1)}, bf16[2,128,192]{2,1,0:T(8,128)(2,1)S(1)}, u32[]{:S(2)}, u32[]{:S(2)}) collective-permute-start(bf16[2,128,192]{2,1,0:T(8,128)(2,1)} %get-tuple-element.22), channel_id=1, source_target_pairs={{1,0},{2,1},{3,2},{4,3},{5,4},{6,5},{7,6},{8,7},{9,8},{10,9},{11,1... | collective-permute-start | bytes 294920 | tf_op jit(solution)/shard_map/ppermute | solution.py:356
  31.0 2.5 %copy.31 = bf16[3,3,384,192]{3,2,1,0:T(8,128)(2,1)S(1)} copy(bf16[3,3,384,192]{2,3,1,0:T(8,128)(2,1)} %param.6) | data formatting | bytes 2654208 | tf_op args[2]
  33.6 0.0 copy-start
  33.6 0.2 copy.32.cot
  33.8 0.0 copy-start.4
  33.8 0.0 collective-permute-done.3.up
  33.8 3.2 %collective-permute-done.4.down = bf16[2,128,192]{2,1,0:T(8,128)(2,1)S(1)} collective-permute-done((bf16[2,128,192]{2,1,0:T(8,128)(2,1)}, bf16[2,128,192]{2,1,0:T(8,128)(2,1)S(1)}, u32[]{:S(2)}, u32[]{:S(2)}) %collective-permute-start.4) | collective-permute-done | bytes 98336 | tf_op jit(solution)/shard_map/ppermute | solution.py:356
  37.0 1.1 box_sums.1
  38.2 0.0 collective-permute-done.1.up
  38.2 0.0 collective-permute-done.2.down
  38.2 9.1 %forward.1 = (bf16[2,2,64,384]{3,2,1,0:T(8,128)(2,1)S(1)}, bf16[16,24,256]{2,1,0:T(8,128)(2,1)S(1)}, bf16[384,256]{1,0:T(8,128)(2,1)S(1)}) custom-call(bf16[2,2,64,384]{3,2,1,0:T(8,128)(2,1)S(1)} %bitcast.41, bf16[2,2,64,384]{3,2,1,0:T(8,128)(2,1)S(1)} %copy.34.prev, bf16[4,64,384]{2,1,0:T(8,128)(2,1)S(1)} %collective-permute-done.1.up, ...), custom_call_target="tpu_custom_call" | custom-call | flops 2040000000 | bytes 10000000 | tf_op jit(solution)/shard_map/forward/pallas_call | solution.py:125
  47.3 1.6 %two_part.1 = bf16[16,24,1728]{2,1,0:T(8,128)(2,1)} custom-call(bf16[384,256]{1,0:T(8,128)(2,1)S(1)} %get-tuple-element.11.ht, bf16[256,1728]{1,0:T(8,128)(2,1)S(1)} %get-tuple-element.12.gcat), custom_call_target="tpu_custom_call" | custom-call | flops 340000000 | bytes 3000000 | tf_op jit(solution)/shard_map/two_part/pallas_call | solution.py:156
  48.9 8.4 %all-to-all-start.2 = ((bf16[16,24,1728]{2,1,0:T(8,128)(2,1)}), bf16[16,24,1728]{2,1,0:T(8,128)(2,1)S(1)}, u32[]{:S(2)}, u32[]{:S(2)}) async-start(bf16[16,24,1728]{2,1,0:T(8,128)(2,1)} %two_part.1), calls=%async_computation.2 | async-start | bytes 2752512 | tf_op jit(solution)/shard_map/all_to_all | solution.py:372
  57.4 1.3 collective-permute-start.5
  58.7 15.8 %collective-permute-done.5 = bf16[16,24,256]{2,1,0:T(8,128)(2,1)S(1)} collective-permute-done((bf16[16,24,256]{2,1,0:T(8,128)(2,1)S(1)}, bf16[16,24,256]{2,1,0:T(8,128)(2,1)S(1)}, u32[]{:S(2)}, u32[]{:S(2)}) %collective-permute-start.5) | collective-permute-done | bytes 196640 | tf_op jit(solution)/shard_map/ppermute | solution.py:363
  74.5 0.8 pad_maximum_fusion
  75.3 0.0 all-to-all-done.2.parts
  75.3 13.5 %all-to-all-start = ((bf16[16,24,512]{2,1,0:T(8,128)(2,1)}), bf16[16,24,512]{2,1,0:T(8,128)(2,1)S(1)}, u32[]{:S(2)}, u32[]{:S(2)}) async-start(bf16[16,24,512]{2,1,0:T(8,128)(2,1)} %pad_maximum_fusion), calls=%async_computation | async-start | bytes 786432 | tf_op jit(solution)/shard_map/all_to_all | solution.py:365
  88.8 0.2 copy.35
  89.0 1.1 two_mid.1
  90.0 13.3 %all-to-all-done.g = bf16[16,24,512]{2,1,0:T(8,128)(2,1)S(1)} async-done(((bf16[16,24,512]{2,1,0:T(8,128)(2,1)}), bf16[16,24,512]{2,1,0:T(8,128)(2,1)S(1)}, u32[]{:S(2)}, u32[]{:S(2)}) %all-to-all-start) | async-done | bytes 393248 | tf_op jit(solution)/shard_map/all_to_all | solution.py:365
  103.3 3.4 %all-to-all-start.3 = ((bf16[16,24,128]{2,1,0:T(8,128)(2,1)}), bf16[16,24,128]{2,1,0:T(8,128)(2,1)S(1)}, u32[]{:S(2)}, u32[]{:S(2)}) async-start(bf16[16,24,128]{2,1,0:T(8,128)(2,1)} %two_mid.1), calls=%async_computation.3 | async-start | bytes 196608 | tf_op jit(solution)/shard_map/all_to_all | solution.py:374
  106.7 0.0 all-gather.2.cloned.1.call-done.x
  106.8 1.9 %copy-done.1 = bf16[16,2,2,64,384]{4,3,2,1,0:T(8,128)(2,1)S(1)} copy-done((bf16[16,2,2,64,384]{4,3,2,1,0:T(8,128)(2,1)S(1)}, bf16[16,2,2,64,384]{4,3,2,1,0:T(8,128)(2,1)}, u32[]{:S(2)}) %copy-start.1) | copy-done | bytes 3145752
  108.6 6.0 %one_part.1 = bf16[16,24,768]{2,1,0:T(8,128)(2,1)} custom-call(bf16[16,24,512]{2,1,0:T(8,128)(2,1)S(1)} %all-to-all-done.g, bf16[16,2,2,64,384]{4,3,2,1,0:T(8,128)(2,1)S(1)} %copy-done.1), custom_call_target="tpu_custom_call" | custom-call | flops 2040000000 | bytes 5000000 | tf_op jit(solution)/shard_map/one_part/pallas_call | solution.py:267
  114.6 0.0 all-to-all-done.3.parts
  114.6 7.3 %all-to-all-start.1 = ((bf16[16,24,768]{2,1,0:T(8,128)(2,1)}), bf16[16,24,768]{2,1,0:T(8,128)(2,1)S(1)}, u32[]{:S(2)}, u32[]{:S(2)}) async-start(bf16[16,24,768]{2,1,0:T(8,128)(2,1)} %one_part.1), calls=%async_computation.1 | async-start | bytes 1179648 | tf_op jit(solution)/shard_map/all_to_all | solution.py:376
  122.0 2.1 %collective-permute-start.7 = (bf16[4,64,384]{2,1,0:T(8,128)(2,1)S(1)}, bf16[4,64,384]{2,1,0:T(8,128)(2,1)S(1)}, u32[]{:S(2)}, u32[]{:S(2)}) collective-permute-start(bf16[4,64,384]{2,1,0:T(8,128)(2,1)S(1)} %pad_maximum_fusion.4), channel_id=1, source_target_pairs={{1,0},{2,1},{3,2},{4,3},{5,4},{6,5},{7,6},{8,7},{9,8},{10,9},{11,1... | collective-permute-start | bytes 589832 | tf_op jit(solution)/shard_map/ppermute | solution.py:369
  124.2 3.5 %collective-permute-start.6 = (bf16[4,64,384]{2,1,0:T(8,128)(2,1)S(1)}, bf16[4,64,384]{2,1,0:T(8,128)(2,1)S(1)}, u32[]{:S(2)}, u32[]{:S(2)}) collective-permute-start(bf16[4,64,384]{2,1,0:T(8,128)(2,1)S(1)} %pad_maximum_fusion.3), channel_id=1, source_target_pairs={{0,1},{1,2},{2,3},{3,4},{4,5},{5,6},{6,7},{7,8},{8,9},{9,10},{10,1... | collective-permute-start | bytes 589832 | tf_op jit(solution)/shard_map/ppermute | solution.py:368
  127.6 1.7 %collective-permute-done.7.down = bf16[4,64,384]{2,1,0:T(8,128)(2,1)S(1)} collective-permute-done((bf16[4,64,384]{2,1,0:T(8,128)(2,1)S(1)}, bf16[4,64,384]{2,1,0:T(8,128)(2,1)S(1)}, u32[]{:S(2)}, u32[]{:S(2)}) %collective-permute-start.7) | collective-permute-done | bytes 196640 | tf_op jit(solution)/shard_map/ppermute | solution.py:369
  129.3 0.9 collective-permute-done.6.up
  130.2 9.7 %latents_grad.1 = bf16[2,2,64,384]{3,2,1,0:T(8,128)(2,1)} custom-call(bf16[2,2,64,384]{3,2,1,0:T(8,128)(2,1)S(1)} %get-tuple-element.9.own, bf16[2,2,64,384]{3,2,1,0:T(8,128)(2,1)S(1)} %bitcast.43, bf16[4,64,384]{2,1,0:T(8,128)(2,1)S(1)} %collective-permute-done.6.up, bf16[4,64,384]{2,1,0:T(8,128)(2,1)S(1)} %collective-permute-done.7.down, ...), custom_call_target="tpu_custom_call" | custom-call | flops 2040000000 | bytes 10000000 | tf_op jit(solution)/shard_map/latents_grad/pallas_call | solution.py:195
  139.9 0.1 final_two.1
  140.0 0.8 copy.40
  140.8 0.9 final_one.1
  (14 shorter events, 0.2 us)
Async XLA Ops:
  7.2 99.6 %all-gather.2.cloned.1.call-start = ((), (), s32[]{:S(2)}) async-start(), calls=%async_computation.4 | async-start | bytes 3342336 | tf_op jit(solution)/shard_map/all_gather | solution.py:352
  8.9 7.5 %collective-permute-start = (bf16[2,2,64,384]{3,2,0,1:T(8,128)(2,1)S(1)}, bf16[2,2,64,384]{3,2,0,1:T(8,128)(2,1)S(1)}, u32[]{:S(2)}, u32[]{:S(2)}) collective-permute-start(bf16[2,2,64,384]{3,2,0,1:T(8,128)(2,1)S(1)} %bitcast.49), channel_id=1, source_target_pairs={{0,16},{16,32},{32,48},{1,17},{17,33},{33,49},{2,18},{18,34},{34,5... | collective-permute-start | bytes 589832 | tf_op jit(solution)/shard_map/ppermute | solution.py:354
  16.4 12.7 %copy-start.3 = (bf16[2,2,64,384]{3,2,0,1:T(8,128)(2,1)}, bf16[2,2,64,384]{3,2,0,1:T(8,128)(2,1)S(1)}, u32[]{:S(2)}) copy-start(bf16[2,2,64,384]{3,2,0,1:T(8,128)(2,1)S(1)} %collective-permute-done) | copy-start | bytes 589828
  17.1 21.1 %collective-permute-start.1 = (bf16[4,64,384]{2,1,0:T(8,128)(2,1)}, bf16[4,64,384]{2,1,0:T(8,128)(2,1)S(1)}, u32[]{:S(2)}, u32[]{:S(2)}) collective-permute-start(bf16[4,64,384]{2,1,0:T(8,128)(2,1)} %pad_maximum_fusion.1), channel_id=1, source_target_pairs={{0,1},{1,2},{2,3},{3,4},{4,5},{5,6},{6,7},{7,8},{8,9},{9,10},{10,1... | collective-permute-start | bytes 589832 | tf_op jit(solution)/shard_map/ppermute | solution.py:357
  22.8 15.4 %collective-permute-start.2 = (bf16[4,64,384]{2,1,0:T(8,128)(2,1)}, bf16[4,64,384]{2,1,0:T(8,128)(2,1)S(1)}, u32[]{:S(2)}, u32[]{:S(2)}) collective-permute-start(bf16[4,64,384]{2,1,0:T(8,128)(2,1)} %pad_maximum_fusion.2), channel_id=1, source_target_pairs={{1,0},{2,1},{3,2},{4,3},{5,4},{6,5},{7,6},{8,7},{9,8},{10,9},{11,1... | collective-permute-start | bytes 589832 | tf_op jit(solution)/shard_map/ppermute | solution.py:358
  24.7 8.9 %copy-start.2 = (bf16[1,2,4,128,192]{3,4,2,1,0:T(8,128)(2,1)S(1)}, bf16[1,2,4,128,192]{3,4,2,1,0:T(8,128)(2,1)}, u32[]{:S(2)}) copy-start(bf16[1,2,4,128,192]{3,4,2,1,0:T(8,128)(2,1)} %param.7) | copy-start | bytes 1179652
  25.4 8.4 %collective-permute-start.3 = (bf16[2,128,192]{2,1,0:T(8,128)(2,1)}, bf16[2,128,192]{2,1,0:T(8,128)(2,1)S(1)}, u32[]{:S(2)}, u32[]{:S(2)}) collective-permute-start(bf16[2,128,192]{2,1,0:T(8,128)(2,1)} %get-tuple-element.23), channel_id=1, source_target_pairs={{0,1},{1,2},{2,3},{3,4},{4,5},{5,6},{6,7},{7,8},{8,9},{9,10},{10,1... | collective-permute-start | bytes 294920 | tf_op jit(solution)/shard_map/ppermute | solution.py:355
  29.1 7.9 %collective-permute-start.4 = (bf16[2,128,192]{2,1,0:T(8,128)(2,1)}, bf16[2,128,192]{2,1,0:T(8,128)(2,1)S(1)}, u32[]{:S(2)}, u32[]{:S(2)}) collective-permute-start(bf16[2,128,192]{2,1,0:T(8,128)(2,1)} %get-tuple-element.22), channel_id=1, source_target_pairs={{1,0},{2,1},{3,2},{4,3},{5,4},{6,5},{7,6},{8,7},{9,8},{10,9},{11,1... | collective-permute-start | bytes 294920 | tf_op jit(solution)/shard_map/ppermute | solution.py:356
  33.6 4.6 %copy-start = (bf16[1,2,2,64,384]{4,3,2,1,0:T(8,128)(2,1)S(1)}, bf16[1,2,2,64,384]{4,3,2,1,0:T(8,128)(2,1)}, u32[]{:S(2)}) copy-start(bf16[1,2,2,64,384]{4,3,2,1,0:T(8,128)(2,1)} %param.4) | copy-start | bytes 589828
  33.8 4.3 %copy-start.4 = (bf16[2,2,64,384]{3,2,0,1:T(8,128)(2,1)S(1)}, bf16[2,2,64,384]{3,2,0,1:T(8,128)(2,1)}, u32[]{:S(2)}) copy-start(bf16[2,2,64,384]{3,2,0,1:T(8,128)(2,1)} %copy-done.3) | copy-start | bytes 589828
  48.9 26.4 %all-to-all-start.2 = ((bf16[16,24,1728]{2,1,0:T(8,128)(2,1)}), bf16[16,24,1728]{2,1,0:T(8,128)(2,1)S(1)}, u32[]{:S(2)}, u32[]{:S(2)}) async-start(bf16[16,24,1728]{2,1,0:T(8,128)(2,1)} %two_part.1), calls=%async_computation.2 | async-start | bytes 2752512 | tf_op jit(solution)/shard_map/all_to_all | solution.py:372
  57.4 17.1 %collective-permute-start.5 = (bf16[16,24,256]{2,1,0:T(8,128)(2,1)S(1)}, bf16[16,24,256]{2,1,0:T(8,128)(2,1)S(1)}, u32[]{:S(2)}, u32[]{:S(2)}) collective-permute-start(bf16[16,24,256]{2,1,0:T(8,128)(2,1)S(1)} %get-tuple-element.10), channel_id=1, source_target_pairs={{16,0},{32,16},{48,32},{17,1},{33,17},{49,33},{18,2},{34,18},{50,3... | collective-permute-start | bytes 589832 | tf_op jit(solution)/shard_map/ppermute | solution.py:363
  75.3 28.0 %all-to-all-start = ((bf16[16,24,512]{2,1,0:T(8,128)(2,1)}), bf16[16,24,512]{2,1,0:T(8,128)(2,1)S(1)}, u32[]{:S(2)}, u32[]{:S(2)}) async-start(bf16[16,24,512]{2,1,0:T(8,128)(2,1)} %pad_maximum_fusion), calls=%async_computation | async-start | bytes 786432 | tf_op jit(solution)/shard_map/all_to_all | solution.py:365
  103.3 11.3 %all-to-all-start.3 = ((bf16[16,24,128]{2,1,0:T(8,128)(2,1)}), bf16[16,24,128]{2,1,0:T(8,128)(2,1)S(1)}, u32[]{:S(2)}, u32[]{:S(2)}) async-start(bf16[16,24,128]{2,1,0:T(8,128)(2,1)} %two_mid.1), calls=%async_computation.3 | async-start | bytes 196608 | tf_op jit(solution)/shard_map/all_to_all | solution.py:374
  106.7 1.9 %copy-start.1 = (bf16[16,2,2,64,384]{4,3,2,1,0:T(8,128)(2,1)S(1)}, bf16[16,2,2,64,384]{4,3,2,1,0:T(8,128)(2,1)}, u32[]{:S(2)}) copy-start(bf16[16,2,2,64,384]{4,3,2,1,0:T(8,128)(2,1)} %all-gather.2.cloned.1.call-done.x) | copy-start | bytes 9437188
  114.6 26.2 %all-to-all-start.1 = ((bf16[16,24,768]{2,1,0:T(8,128)(2,1)}), bf16[16,24,768]{2,1,0:T(8,128)(2,1)S(1)}, u32[]{:S(2)}, u32[]{:S(2)}) async-start(bf16[16,24,768]{2,1,0:T(8,128)(2,1)} %one_part.1), calls=%async_computation.1 | async-start | bytes 1179648 | tf_op jit(solution)/shard_map/all_to_all | solution.py:376
  122.0 7.3 %collective-permute-start.7 = (bf16[4,64,384]{2,1,0:T(8,128)(2,1)S(1)}, bf16[4,64,384]{2,1,0:T(8,128)(2,1)S(1)}, u32[]{:S(2)}, u32[]{:S(2)}) collective-permute-start(bf16[4,64,384]{2,1,0:T(8,128)(2,1)S(1)} %pad_maximum_fusion.4), channel_id=1, source_target_pairs={{1,0},{2,1},{3,2},{4,3},{5,4},{6,5},{7,6},{8,7},{9,8},{10,9},{11,1... | collective-permute-start | bytes 589832 | tf_op jit(solution)/shard_map/ppermute | solution.py:369
  124.2 6.1 %collective-permute-start.6 = (bf16[4,64,384]{2,1,0:T(8,128)(2,1)S(1)}, bf16[4,64,384]{2,1,0:T(8,128)(2,1)S(1)}, u32[]{:S(2)}, u32[]{:S(2)}) collective-permute-start(bf16[4,64,384]{2,1,0:T(8,128)(2,1)S(1)} %pad_maximum_fusion.3), channel_id=1, source_target_pairs={{0,1},{1,2},{2,3},{3,4},{4,5},{5,6},{6,7},{7,8},{8,9},{9,10},{10,1... | collective-permute-start | bytes 589832 | tf_op jit(solution)/shard_map/ppermute | solution.py:368
Sparse Core Ops, SparseCore 0:
  9.8 45.6 all-gather.1

commit v2 on v1

v2 whole, which is shorter than its diff:
```python
import jax
import jax.numpy as jnp
from jax import lax
from jax.experimental import pallas as pl
from jax.experimental.pallas import tpu as pltpu
from jax.sharding import PartitionSpec as P

BF = jnp.bfloat16
F32 = jnp.float32
MIB = 1024 * 1024


def params(mib=16):
    return pltpu.CompilerParams(vmem_limit_bytes=mib * MIB)


def anywhere(count):
    return [pl.BlockSpec(memory_space=pl.ANY)] * count


def bring(sources, targets, sems):
    copies = [
        pltpu.make_async_copy(source, target, sems.at[n])
        for n, (source, target) in enumerate(zip(sources, targets))
    ]
    for each in copies:
        each.start()
    return copies


def vmem(count):
    return [pl.BlockSpec(memory_space=pltpu.VMEM)] * count


def cost(macs, nbytes):
    return pl.CostEstimate(flops=2 * macs, bytes_accessed=nbytes, transcendentals=0)


def column_shifts(wide):
    row = lax.broadcasted_iota(jnp.int32, wide.shape, 0)
    before = jnp.where(row == 0, 0.0, pltpu.roll(wide, 1, 0))
    after = jnp.where(row == 63, 0.0, pltpu.roll(wide, 63, 0))
    return before.astype(BF), after.astype(BF)


def place():
    height, frame = lax.axis_index("height"), lax.axis_index("frame")
    last = lax.axis_size("height") - 1, lax.axis_size("frame") - 1
    return (
        lax.rem(height, 2),
        (height > 0).astype(F32),
        (height < last[0]).astype(F32),
        (frame > 0).astype(F32),
        (frame < last[1]).astype(F32),
    )


def stack_columns(dest, low, high, cross, inner, at, oks, order):
    core, above_ok, below_ok = at[:3]
    for f in range(4):
        for r in range(4):
            keep = oks[f // 2]
            if r in (0, 3):
                pick_cross = core == (0 if r == 0 else 1)
                block = jnp.where(pick_cross, cross[f].astype(F32), inner[f].astype(F32))
                edge = above_ok if r == 0 else below_ok
                keep = edge if keep is None else edge * keep
            else:
                block = (low if f < 2 else high)[f % 2, r - 1].astype(F32)
            if keep is not None:
                block = block * keep
            before, after = column_shifts(block)
            sides = (before, after) if order > 0 else (after, before)
            dest[f, r, :, 0:384] = sides[0]
            dest[f, r, :, 384:768] = block.astype(BF)
            dest[f, r, :, 768:1152] = sides[1]


def load_kernel(w, out, sems):
    parts = [pl.ds(3 * n, 3) for n in range(9)]
    for each in bring([w.at[p] for p in parts], [out.at[p] for p in parts], sems):
        each.wait()


def load(w):
    return pl.pallas_call(
        load_kernel,
        in_specs=anywhere(1),
        out_specs=vmem(1)[0],
        out_shape=jax.ShapeDtypeStruct((27, 384, 384), BF),
        scratch_shapes=[pltpu.SemaphoreType.DMA((9,))],
        compiler_params=params(46),
        cost_estimate=cost(1000, 16_000_000),
        name="load",
    )(w)


def pair_kernel(own, other, cot, out, cross, inner):
    core = place()[0]
    out[core] = own[...]
    out[1 - core] = other[...]
    for target, line in ((cross, 3 * core), (inner, 3 - 3 * core)):
        for t in range(2):
            for n in range(3):
                target[t, :, n * 128 : (n + 1) * 128] = cot[t, line, n * 64 : (n + 1) * 64, :]


def pair(own, other, cot):
    rows = jax.ShapeDtypeStruct((2, 64, 384), BF)
    return pl.pallas_call(
        pair_kernel,
        in_specs=vmem(3),
        out_specs=tuple(vmem(3)),
        out_shape=(jax.ShapeDtypeStruct((2, 2, 2, 64, 384), BF), rows, rows),
        compiler_params=params(),
        cost_estimate=cost(1000, 1_600_000),
        name="pair",
    )(own, other, cot)


def edges_kernel(own, prev, cot_cross, cot_inner, cross, inner):
    core = place()[0]
    for out, row, lines in ((cross, core, cot_cross), (inner, 1 - core, cot_inner)):
        for t in range(2):
            out[t] = prev[t, row]
            out[2 + t] = own[t, row]
            out[4 + t] = lines[t]


def edges(own, prev, cot_cross, cot_inner):
    shape = jax.ShapeDtypeStruct((6, 64, 384), BF)
    return pl.pallas_call(
        edges_kernel,
        in_specs=vmem(4),
        out_specs=tuple(vmem(2)),
        out_shape=(shape, shape),
        compiler_params=params(),
        cost_estimate=cost(1000, 1_000_000),
        name="edges",
    )(own, prev, cot_cross, cot_inner)


def box_pick():
    size = (64, 256)
    pos = lax.broadcasted_iota(jnp.int32, size, 1) & 127
    low = lax.broadcasted_iota(jnp.int32, size, 0)
    pick = []
    for k in range(3):
        offset = pos - 2 * low - 1 + k
        pick.append(jnp.where((offset == 0) | (offset == 1), 1.0, 0.0))
    return jnp.concatenate(pick, axis=0).astype(BF)


def forward_kernel(own, prev, cross, inner, cotv, w2, wv, gp, gpt, ht, gcat, xx, w2v, sem):
    last = pltpu.make_async_copy(w2, w2v, sem)
    last.start()
    at = place()
    core, above_ok, below_ok, before_ok = at[:4]
    stack_columns(xx, prev, own, cross, inner, at, (before_ok, None), 1)

    def line(t, r):
        if 0 <= r < 4:
            return cotv[t, r]
        pick_cross = core == (0 if r < 0 else 1)
        row = jnp.where(pick_cross, cross[4 + t].astype(F32), inner[4 + t].astype(F32))
        row = (row * (above_ok if r < 0 else below_ok)).astype(BF)
        return jnp.concatenate([row[:, n * 128 : (n + 1) * 128] for n in range(3)], axis=0)

    pick = box_pick()
    for t in range(2):
        for r in range(2):
            rows = pl.ds((t * 2 + r) * 64, 64)
            for j in range(3):
                a = 2 * r + 1 - j
                pair = jnp.concatenate([line(t, a), line(t, a + 1)], axis=1)
                box = lax.dot_general(
                    pick, pair, (((1,), (1,)), ((), ())), preferred_element_type=F32
                ).astype(BF)
                for k in range(3):
                    gcat[rows, pl.ds((j * 3 + k) * 192, 192)] = box[k * 64 : (k + 1) * 64]
    pre = jnp.zeros((256, 384), F32)
    for n in range(9):
        i, j = n // 3, n % 3
        lhs = xx[i : i + 2, j : j + 2].reshape(256, 1152)
        rhs = wv[3 * n : 3 * n + 3].reshape(1152, 384)
        pre = pre + jnp.dot(lhs, rhs, preferred_element_type=F32)
    last.wait()
    gh = jnp.dot(gcat[...], w2v[...], preferred_element_type=F32)
    sigma = jax.nn.sigmoid(pre)
    hidden = pre * sigma
    grad = gh * sigma * (1.0 + pre * (1.0 - sigma))
    gp[...] = grad.astype(BF).reshape(2, 2, 64, 384)
    grad_t = grad.T
    for b in range(16):
        gpt[b] = grad_t[b * 24 : (b + 1) * 24].astype(BF)
    ht[...] = hidden.T.astype(BF)


def forward(own, prev, cross, inner, cot, w2, w):
    return pl.pallas_call(
        forward_kernel,
        in_specs=vmem(5) + anywhere(1) + vmem(1),
        out_specs=tuple(vmem(4)),
        out_shape=(
            jax.ShapeDtypeStruct((2, 2, 64, 384), BF),
            jax.ShapeDtypeStruct((16, 24, 256), BF),
            jax.ShapeDtypeStruct((384, 256), BF),
            jax.ShapeDtypeStruct((256, 1728), BF),
        ),
        scratch_shapes=[
            pltpu.VMEM((4, 4, 64, 1152), BF),
            pltpu.VMEM((1728, 384), BF),
            pltpu.SemaphoreType.DMA,
        ],
        compiler_params=params(24),
        cost_estimate=cost(1_300_000_000, 12_000_000),
        name="forward",
    )(own, prev, cross, inner, cot, w2, w)


def mix_kernel(own, after, own_t, by_channel, cross, inner):
    at = place()
    core, after_ok = at[0], at[4]
    later = (after[...].reshape(256, 384).astype(F32) * after_ok).T
    for b in range(16):
        by_channel[b, :, 0:256] = own_t[b]
        by_channel[b, :, 256:512] = later[b * 24 : (b + 1) * 24].astype(BF)
    for out, row in ((cross, core), (inner, 1 - core)):
        for t in range(2):
            out[t] = own[t, row]
            out[2 + t] = after[t, row]


def mix(own, after, own_t):
    shape = jax.ShapeDtypeStruct((4, 64, 384), BF)
    return pl.pallas_call(
        mix_kernel,
        in_specs=vmem(3),
        out_specs=tuple(vmem(3)),
        out_shape=(jax.ShapeDtypeStruct((16, 24, 512), BF), shape, shape),
        compiler_params=params(),
        cost_estimate=cost(1000, 1_500_000),
        name="mix",
    )(own, after, own_t)


def two_kernel(ht, gcat, out):
    res = jnp.dot(ht[...], gcat[...], preferred_element_type=F32)
    for b in range(16):
        out[b] = res[b * 24 : (b + 1) * 24].astype(BF)


def two_part(ht, gcat):
    return pl.pallas_call(
        two_kernel,
        out_shape=jax.ShapeDtypeStruct((16, 24, 1728), BF),
        compiler_params=params(),
        cost_estimate=cost(170_000_000, 3_000_000),
        name="two_part",
    )(ht, gcat)


def latents_kernel(own, after, cross, inner, wv, out, gg):
    at = place()
    stack_columns(gg, own, after, cross, inner, at, (None, at[4]), -1)
    total = jnp.zeros((256, 384), F32)
    for n in range(9):
        i, j = n // 3, n % 3
        lhs = gg[2 - i : 4 - i, 2 - j : 4 - j].reshape(256, 1152)
        rhs = jnp.concatenate([wv[3 * n], wv[3 * n + 1], wv[3 * n + 2]], axis=1)
        total = total + lax.dot_general(
            lhs, rhs, (((1,), (1,)), ((), ())), preferred_element_type=F32
        )
    out[...] = total.astype(BF).reshape(2, 2, 64, 384)


def latents_grad(own, after, cross, inner, w):
    return pl.pallas_call(
        latents_kernel,
        in_specs=vmem(5),
        out_specs=vmem(1)[0],
        out_shape=jax.ShapeDtypeStruct((2, 2, 64, 384), BF),
        scratch_shapes=[
            pltpu.VMEM((4, 4, 64, 1152), BF),
        ],
        compiler_params=params(24),
        cost_estimate=cost(1_020_000_000, 10_000_000),
        name="latents_grad",
    )(own, after, cross, inner, w)


def one_kernel(g, *rest):
    blocks, (out, gs, cols, xv, sems) = rest[:8], rest[8:]
    arrive = bring(blocks, [xv.at[n] for n in range(8)], sems)
    lane = lax.broadcasted_iota(jnp.int32, (24, 128), 1)
    col = lane & 63
    left = lane < 64
    height = lax.axis_index("height")
    chip = height // 2
    way = 1 - 2 * (height - 2 * chip)

    cols[0] = jnp.zeros((4, 3, 24, 128), F32)
    cols[17] = jnp.zeros((4, 3, 24, 128), F32)
    for h in range(16):
        for f in range(4):
            mid = g[h, :, pl.ds(f * 128, 128)].astype(F32)
            cols[h + 1, f, 0] = jnp.where(col == 63, 0.0, pltpu.roll(mid, 127, 1))
            cols[h + 1, f, 1] = mid
            cols[h + 1, f, 2] = jnp.where(col == 0, 0.0, pltpu.roll(mid, 1, 1))
    for n, steps in enumerate((0, -1, -2, -3, 4, 1, 2, 3)):
        at = 2 * lax.rem(chip + way * steps + 16, 8)
        for f in range(4):
            lines = [[cols[at + m, f, k] for k in range(3)] for m in range(4)]
            for m in range(2):
                above, here, below = lines[m : m + 3]
                rows = [pltpu.roll(jnp.where(left, b, a), 64, 1) for a, b in zip(here, below)]
                rows += here
                rows += [pltpu.roll(jnp.where(left, b, a), 64, 1) for a, b in zip(above, here)]
                rows.append(jnp.zeros((8, 128), F32))
                to = pl.ds((2 * n + m) * 128, 128)
                gs[f, :, to] = jnp.concatenate(rows, axis=0).astype(BF)

    for each in arrive:
        each.wait()
    total = jnp.zeros((672, 384), F32)
    for s in range(2):
        xs = xv[:, :, s].reshape(2048, 384)
        lhs = gs[s : s + 3].reshape(672, 2048)
        total = total + jnp.dot(lhs, xs, preferred_element_type=F32)
    pad = jnp.zeros((32, 384), F32)
    for b in range(3):
        turned = jnp.concatenate([total[b * 224 : (b + 1) * 224], pad], axis=0).T
        for c in range(16):
            out[c, :, b * 256 : (b + 1) * 256] = turned[c * 24 : (c + 1) * 24].astype(BF)


def one_part(g, blocks):
    return pl.pallas_call(
        one_kernel,
        in_specs=vmem(1) + anywhere(8),
        out_specs=vmem(1)[0],
        out_shape=jax.ShapeDtypeStruct((16, 24, 768), BF),
        scratch_shapes=[
            pltpu.VMEM((4, 224, 2048), BF),
            pltpu.VMEM((18, 4, 3, 24, 128), F32),
            pltpu.VMEM((8, 2, 2, 2, 64, 384), BF),
            pltpu.SemaphoreType.DMA((8,)),
        ],
        compiler_params=params(24),
        cost_estimate=cost(1_020_000_000, 5_000_000),
        name="one_part",
    )(g, *blocks)


def summed(ref):
    total = ref[0].astype(F32)
    for n in range(1, 16):
        total = total + ref[n].astype(F32)
    return total


def two_mid_kernel(parts, out):
    total = summed(parts)
    pad = jnp.zeros((24, 20), F32)
    for h in range(16):
        cut = [total[:, n * 192 + h * 12 : n * 192 + h * 12 + 12] for n in range(9)]
        out[h] = jnp.concatenate(cut + [pad], axis=1).astype(BF)


def two_mid(parts):
    return pl.pallas_call(
        two_mid_kernel,
        out_shape=jax.ShapeDtypeStruct((16, 24, 128), BF),
        compiler_params=params(),
        cost_estimate=cost(1_000_000, 1_500_000),
        name="two_mid",
    )(parts)


def final_one_kernel(parts, out):
    total = summed(parts)
    for i in range(3):
        for n in range(9):
            at = (2 - i) * 256 + n * 24
            out[i * 9 + n] = total[:, at : at + 24]


def final_one(parts):
    return pl.pallas_call(
        final_one_kernel,
        out_shape=jax.ShapeDtypeStruct((27, 24, 24), F32),
        compiler_params=params(),
        cost_estimate=cost(1_000_000, 800_000),
        name="final_one",
    )(parts)


def final_two_kernel(parts, out):
    turned = summed(parts).T
    for n in range(9):
        out[n] = turned[n * 12 : (n + 1) * 12]


def final_two(parts):
    return pl.pallas_call(
        final_two_kernel,
        out_shape=jax.ShapeDtypeStruct((9, 12, 24), F32),
        compiler_params=params(),
        cost_estimate=cost(1_000_000, 200_000),
        name="final_two",
    )(parts)


def local(clip_latents, conv_one, conv_two, cotangent):
    x = clip_latents[0]
    cot = cotangent[0]
    heights = lax.axis_size("height")
    frames = lax.axis_size("frame")
    next_perm = [(n, (n + 1) % frames) for n in range(frames)]
    prev_perm = [((n + 1) % frames, n) for n in range(frames)]
    inner_perm = [(n, n ^ 1) for n in range(heights)]
    cross_perm = [(n, (n + 1 if n % 2 else n - 1) % heights) for n in range(heights)]
    ring_perm = [(n, (n - 2 if n % 2 else n + 2) % heights) for n in range(heights)]

    def inside(value):
        return lax.ppermute(value, "height", inner_perm)

    def across(value):
        return lax.ppermute(value, "height", cross_perm)

    def ring(value):
        return lax.ppermute(value, "height", ring_perm)

    cot = jnp.swapaxes(cot, 2, 3)
    w1 = conv_one.reshape(27, 384, 384)
    w2 = jnp.swapaxes(conv_two, 2, 3).reshape(1728, 384)
    x_prev = lax.ppermute(x, "frame", next_perm)
    pair0, cot_cross, cot_inner = pair(x, inside(x), cot)
    pair1 = ring(pair0)
    cross, inner = edges(x, x_prev, cot_cross, cot_inner)
    w1, cross, inner = lax.optimization_barrier((w1, cross, inner))
    w1 = load(w1)
    cross, inner = across(cross), inside(inner)
    pair1, w1, cross, inner = lax.optimization_barrier((pair1, w1, cross, inner))
    pair2 = ring(pair1)
    gp, gpt, ht, gcat = forward(x, x_prev, cross, inner, cot, w2, w1)

    gp_next = lax.ppermute(gp, "frame", prev_perm)
    gpt, pair1, pair2 = lax.optimization_barrier((gpt, pair1, pair2))
    pair3 = ring(pair2)
    by_channel, cross, inner = mix(gp, gp_next, gpt)
    by_channel, cross, inner, ht, pair3 = lax.optimization_barrier(
        (by_channel, cross, inner, ht, pair3)
    )
    g = lax.all_to_all(by_channel, "height", 0, 0, tiled=True)
    cross, inner = across(cross), inside(inner)
    pair4 = ring(pair3)
    two = two_part(ht, gcat)
    two = lax.all_to_all(two, ("dp", "frame"), 0, 0, tiled=True)
    g, pair4 = lax.optimization_barrier((g, pair4))
    blocks = (pair0, pair1, pair2, pair3, pair4, inside(pair1), inside(pair2), inside(pair3))

    one = one_part(g, blocks)
    one, cross, inner = lax.optimization_barrier((one, cross, inner))
    one = lax.all_to_all(one, ("dp", "frame"), 0, 0, tiled=True)
    grad_in = latents_grad(gp, gp_next, cross, inner, w1)
    grad_in, two = lax.optimization_barrier((grad_in, two))
    two = lax.all_to_all(two_mid(two), "height", 0, 0, tiled=True)
    one = final_one(one).reshape(3, 3, 3, 24, 24)
    two = jnp.swapaxes(final_two(two).reshape(3, 3, 12, 24), 2, 3)
    return (grad_in[None], one, two)


def solution(mesh):
    placed = (
        P("dp", "frame", "height", None, None),
        P(),
        P(),
        P("dp", "frame", "height", None, None),
    )
    return jax.shard_map(
        local,
        mesh=mesh,
        in_specs=placed,
        out_specs=(
            P("dp", "frame", "height", None, None),
            P(None, None, None, ("dp", "frame"), "height"),
            P(None, None, ("dp", "frame"), "height"),
        ),
        check_vma=False,
    )
```

time: 150 us -> 121 us (0.81)
  between operations: 14.3 us -> 0.8 us
  starting transfers between devices: 55.9 us -> 45.8 us
  waiting for transfers between devices: 37.9 us -> 45.1 us
  Pallas kernels: 29.6 us -> 23.3 us
  local copies, waits for them, and re-layouts: 8.57 us -> 5.21 us
  other arithmetic: 2.26 us -> 0 us
    all_to_all x2, starting transfers between devices: 20.8 us -> 10.7 us  [the longest x1 7.15 us: local(): g = lax.all_to_all(by_channel, 'height', 0, 0, tiled=True)]
    ppermute x7 -> x13, waiting for transfers between devices: 21.6 us -> 13 us  [the longest x4 7 us: ring(): return lax.ppermute(value, 'height', ring_perm)]
    all_to_all x1, waiting for transfers between devices: 0.01 us -> 7.61 us  [local(): two = lax.all_to_all(two_mid(two), 'height', 0, 0, tiled=True)]
    all_to_all x1, waiting for transfers between devices: 0.01 us -> 7.43 us  [local(): two = lax.all_to_all(two, ('dp', 'frame'), 0, 0, tiled=True)]
    pallas_call x5 -> x8, Pallas kernels: 26 us -> 19.6 us  [the longest x1 6.1 us: one_part(): pl.pallas_call(one_kernel, in_specs=vmem(1) + anywhere(8), out_specs=vmem...]
    ppermute x7 -> x13, starting transfers between devices: 19.3 us -> 23.8 us  [the longest x4 10.8 us: ring(): return lax.ppermute(value, 'height', ring_perm)]
    ppermute x1, starting transfers between devices: 3.96 us -> 0.01 us  [local(): x_prev = lax.ppermute(x, 'frame', next_perm)]
    all_to_all x2, waiting for transfers between devices: 13.3 us -> 16.4 us  [the longest x1 12.8 us: local(): g = lax.all_to_all(by_channel, 'height', 0, 0, tiled=True)]
  transfers between devices with their start and end apart: 13 -> 18, of which waited for: 6 -> 9; matrix products, arithmetic and copies ran while one was open for 6% -> 0% of each run, Pallas kernels for 19% -> 19%
where the time goes in v2:
time: 121 us; the launch traced here: 120 us
  starting transfers between devices  45.8 us (38%)
  waiting for transfers between devices  45.1 us (37%)
  Pallas kernels  23.3 us (19%)
  local copies, waits for them, and re-layouts  5.21 us (4%)
    all_to_all x1, waiting for transfers between devices, local(): g = lax.all_to_all(by_channel, 'height', 0, 0, tiled=True)  12.8 us
    ppermute x4, starting transfers between devices, ring(): return lax.ppermute(value, 'height', ring_perm)  10.8 us
    ppermute x6, starting transfers between devices, inside(): return lax.ppermute(value, 'height', inner_perm)  9.35 us
    all_to_all x1, waiting for transfers between devices, local(): two = lax.all_to_all(two_mid(two), 'height', 0, 0, tiled=True)  7.61 us
    all_to_all x1, waiting for transfers between devices, local(): two = lax.all_to_all(two, ('dp', 'frame'), 0, 0, tiled=True)  7.43 us
    all_to_all x1, starting transfers between devices, local(): g = lax.all_to_all(by_channel, 'height', 0, 0, tiled=True)  7.15 us
    ppermute x4, waiting for transfers between devices, ring(): return lax.ppermute(value, 'height', ring_perm)  7 us
    all_to_all x1, starting transfers between devices, local(): two = lax.all_to_all(two, ('dp', 'frame'), 0, 0, tiled=True)  6.48 us
  transfers between devices with their start and end apart: 18, of which 9 were waited for; matrix products, arithmetic and copies ran while one was open for 0% of the time, Pallas kernels for 19%

profile of v2, /device:TPU:1, one launch (start us, length us, event | category | flops | bytes accessed | tf_op | source)
XLA Modules:
  0.0 120.2 jit_solution(11403101154893305073)
XLA Ops:
  0.6 3.3 %collective-permute-start.1 = (bf16[2,2,64,384]{3,2,1,0:T(8,128)(2,1)}, bf16[2,2,64,384]{3,2,1,0:T(8,128)(2,1)S(1)}, u32[]{:S(2)}, u32[]{:S(2)}) collective-permute-start(bf16[2,2,64,384]{3,2,1,0:T(8,128)(2,1)} %bitcast.13), channel_id=1, source_target_pairs={{0,1},{1,0},{2,3},{3,2},{4,5},{5,4},{6,7},{7,6},{8,9},{9,8},{10,11... | collective-permute-start | bytes 589832 | tf_op jit(solution)/shard_map/ppermute | solution.py:426
  4.0 0.0 collective-permute-start
  4.0 1.3 %collective-permute-done.1.other = bf16[2,2,64,384]{3,2,1,0:T(8,128)(2,1)S(1)} collective-permute-done((bf16[2,2,64,384]{3,2,1,0:T(8,128)(2,1)}, bf16[2,2,64,384]{3,2,1,0:T(8,128)(2,1)S(1)}, u32[]{:S(2)}, u32[]{:S(2)}) %collective-permute-start.1) | collective-permute-done | bytes 196640 | tf_op jit(solution)/shard_map/ppermute | solution.py:426
  5.2 0.9 copy-done.2
  6.2 1.0 copy-done.4
  7.2 0.1 pair.1
  7.2 3.9 %collective-permute-start.2 = (bf16[2,2,2,64,384]{4,3,2,1,0:T(8,128)(2,1)S(1)}, bf16[2,2,2,64,384]{4,3,2,1,0:T(8,128)(2,1)S(1)}, u32[]{:S(2)}, u32[]{:S(2)}) collective-permute-start(bf16[2,2,2,64,384]{4,3,2,1,0:T(8,128)(2,1)S(1)} %get-tuple-element.37.rest_0_), channel_id=1, source_target_pairs={{0,2},{1,15},{2,4},{3,1},{4,6},{5,3},{6,8},{7,5},{8,10},{9,7},{10,... | collective-permute-start | bytes 1179656 | tf_op jit(solution)/shard_map/ppermute | solution.py:432
  11.2 0.7 collective-permute-done.prev
  11.8 0.1 edges.1
  11.9 0.0 copy-start.3
  11.9 0.0 copy-start.5
  11.9 0.0 copy-start.6
  11.9 0.7 collective-permute-start.3
  12.7 3.6 %collective-permute-start.4 = (bf16[6,64,384]{2,1,0:T(8,128)(2,1)S(1)}, bf16[6,64,384]{2,1,0:T(8,128)(2,1)S(1)}, u32[]{:S(2)}, u32[]{:S(2)}) collective-permute-start(bf16[6,64,384]{2,1,0:T(8,128)(2,1)S(1)} %get-tuple-element.44), channel_id=1, source_target_pairs={{0,1},{1,0},{2,3},{3,2},{4,5},{5,4},{6,7},{7,6},{8,9},{9,8},{10,11... | collective-permute-start | bytes 884744 | tf_op jit(solution)/shard_map/ppermute | solution.py:426
  16.3 3.3 %load.1.wv = bf16[27,384,384]{2,1,0:T(8,128)(2,1)S(1)} custom-call(bf16[27,384,384]{2,1,0:T(8,128)(2,1)} %bitcast.21), custom_call_target="tpu_custom_call" | custom-call | flops 2000 | bytes 16000000 | tf_op jit(solution)/shard_map/load/pallas_call | solution.py:86
  19.6 0.0 collective-permute-done.4.inner
  19.6 0.0 collective-permute-done.2.rest_1_
  19.7 3.6 %collective-permute-start.6 = (bf16[2,2,2,64,384]{4,3,2,1,0:T(8,128)(2,1)S(1)}, bf16[2,2,2,64,384]{4,3,2,1,0:T(8,128)(2,1)}, u32[]{:S(2)}, u32[]{:S(2)}) collective-permute-start(bf16[2,2,2,64,384]{4,3,2,1,0:T(8,128)(2,1)S(1)} %collective-permute-done.2.rest_1_), channel_id=1, source_target_pairs={{0,2},{1,15},{2,4},{3,1},{4,6},{5,3},{6,8},{7,5},{8,10},{9,7},{10,... | collective-permute-start | bytes 1179656 | tf_op jit(solution)/shard_map/ppermute | solution.py:432
  23.2 4.6 %forward.1 = (bf16[2,2,64,384]{3,2,1,0:T(8,128)(2,1)S(1)}, bf16[16,24,256]{2,1,0:T(8,128)(2,1)S(1)}, bf16[384,256]{1,0:T(8,128)(2,1)S(1)}, bf16[256,1728]{1,0:T(8,128)(2,1)S(1)}) custom-call(bf16[2,2,64,384]{3,2,1,0:T(8,128)(2,1)S(1)} %bitcast.17, bf16[2,2,64,384]{3,2,1,0:T(8,128)(2,1)S(1)} %collective-permute-done.prev, ...), custom_call_target="tpu_custom_call" | custom-call | flops 2600000000 | bytes 12000000 | tf_op jit(solution)/shard_map/forward/pallas_call | solution.py:200
  27.8 0.1 collective-permute-done.6.rest_2_
  27.9 3.2 %collective-permute-start.7 = (bf16[2,2,2,64,384]{4,3,2,1,0:T(8,128)(2,1)}, bf16[2,2,2,64,384]{4,3,2,1,0:T(8,128)(2,1)}, u32[]{:S(2)}, u32[]{:S(2)}) collective-permute-start(bf16[2,2,2,64,384]{4,3,2,1,0:T(8,128)(2,1)} %collective-permute-done.6.rest_2_), channel_id=1, source_target_pairs={{0,2},{1,15},{2,4},{3,1},{4,6},{5,3},{6,8},{7,5},{8,10},{9,7},{10,... | collective-permute-start | bytes 1179656 | tf_op jit(solution)/shard_map/ppermute | solution.py:432
  31.2 1.4 %collective-permute-start.5 = (bf16[2,2,64,384]{3,2,1,0:T(8,128)(2,1)S(1)}, bf16[2,2,64,384]{3,2,1,0:T(8,128)(2,1)S(1)}, u32[]{:S(2)}, u32[]{:S(2)}) collective-permute-start(bf16[2,2,64,384]{3,2,1,0:T(8,128)(2,1)S(1)} %get-tuple-element.48.own), channel_id=1, source_target_pairs={{16,0},{32,16},{48,32},{0,48},{17,1},{33,17},{49,33},{1,49},{18,2}... | collective-permute-start | bytes 589832 | tf_op jit(solution)/shard_map/ppermute | solution.py:448
  32.6 4.7 %collective-permute-done.5.after = bf16[2,2,64,384]{3,2,1,0:T(8,128)(2,1)S(1)} collective-permute-done((bf16[2,2,64,384]{3,2,1,0:T(8,128)(2,1)S(1)}, bf16[2,2,64,384]{3,2,1,0:T(8,128)(2,1)S(1)}, u32[]{:S(2)}, u32[]{:S(2)}) %collective-permute-start.5) | collective-permute-done | bytes 196640 | tf_op jit(solution)/shard_map/ppermute | solution.py:448
  37.3 0.9 mix.1
  38.2 7.2 %all-to-all-start = ((bf16[16,24,512]{2,1,0:T(8,128)(2,1)}), bf16[16,24,512]{2,1,0:T(8,128)(2,1)S(1)}, u32[]{:S(2)}, u32[]{:S(2)}) async-start(bf16[16,24,512]{2,1,0:T(8,128)(2,1)} %get-tuple-element.57), calls=%async_computation | async-start | bytes 786432 | tf_op jit(solution)/shard_map/all_to_all | solution.py:455
  45.4 1.7 %two_part.1 = bf16[16,24,1728]{2,1,0:T(8,128)(2,1)} custom-call(bf16[384,256]{1,0:T(8,128)(2,1)S(1)} %get-tuple-element.66.ht, bf16[256,1728]{1,0:T(8,128)(2,1)S(1)} %get-tuple-element.67.gcat), custom_call_target="tpu_custom_call" | custom-call | flops 340000000 | bytes 3000000 | tf_op jit(solution)/shard_map/two_part/pallas_call | solution.py:254
  47.1 12.8 %all-to-all-done.g = bf16[16,24,512]{2,1,0:T(8,128)(2,1)S(1)} async-done(((bf16[16,24,512]{2,1,0:T(8,128)(2,1)}), bf16[16,24,512]{2,1,0:T(8,128)(2,1)S(1)}, u32[]{:S(2)}, u32[]{:S(2)}) %all-to-all-start) | async-done | bytes 393248 | tf_op jit(solution)/shard_map/all_to_all | solution.py:455
  59.9 6.5 %all-to-all-start.1 = ((bf16[16,24,1728]{2,1,0:T(8,128)(2,1)}), bf16[16,24,1728]{2,1,0:T(8,128)(2,1)S(1)}, u32[]{:S(2)}, u32[]{:S(2)}) async-start(bf16[16,24,1728]{2,1,0:T(8,128)(2,1)} %two_part.1), calls=%async_computation.1 | async-start | bytes 2752512 | tf_op jit(solution)/shard_map/all_to_all | solution.py:459
  66.4 0.1 collective-permute-start.8
  66.5 0.3 collective-permute-start.9
  66.8 0.5 collective-permute-start.10
  67.3 0.1 collective-permute-start.11
  67.4 1.5 %collective-permute-start.12 = (bf16[4,64,384]{2,1,0:T(8,128)(2,1)}, bf16[4,64,384]{2,1,0:T(8,128)(2,1)S(1)}, u32[]{:S(2)}, u32[]{:S(2)}) collective-permute-start(bf16[4,64,384]{2,1,0:T(8,128)(2,1)} %get-tuple-element.62), channel_id=1, source_target_pairs={{0,15},{1,2},{2,1},{3,4},{4,3},{5,6},{6,5},{7,8},{8,7},{9,10},{10,... | collective-permute-start | bytes 589832 | tf_op jit(solution)/shard_map/ppermute | solution.py:429
  68.9 6.9 %collective-permute-done.8.rest_4_ = bf16[2,2,2,64,384]{4,3,2,1,0:T(8,128)(2,1)S(1)} collective-permute-done((bf16[2,2,2,64,384]{4,3,2,1,0:T(8,128)(2,1)}, bf16[2,2,2,64,384]{4,3,2,1,0:T(8,128)(2,1)S(1)}, u32[]{:S(2)}, u32[]{:S(2)}) %collective-permute-start.8) | collective-permute-done | bytes 393248 | tf_op jit(solution)/shard_map/ppermute | solution.py:432
  75.8 1.6 %collective-permute-start.13 = (bf16[4,64,384]{2,1,0:T(8,128)(2,1)S(1)}, bf16[4,64,384]{2,1,0:T(8,128)(2,1)S(1)}, u32[]{:S(2)}, u32[]{:S(2)}) collective-permute-start(bf16[4,64,384]{2,1,0:T(8,128)(2,1)S(1)} %copy-done.8), channel_id=1, source_target_pairs={{0,1},{1,0},{2,3},{3,2},{4,5},{5,4},{6,7},{7,6},{8,9},{9,8},{10,11... | collective-permute-start | bytes 589832 | tf_op jit(solution)/shard_map/ppermute | solution.py:426
  77.3 0.0 collective-permute-done.9.rest_5_
  77.3 0.0 collective-permute-done.10.rest_6_
  77.3 6.1 %one_part.1 = bf16[16,24,768]{2,1,0:T(8,128)(2,1)} custom-call(bf16[16,24,512]{2,1,0:T(8,128)(2,1)S(1)} %all-to-all-done.g, bf16[2,2,2,64,384]{4,3,2,1,0:T(8,128)(2,1)S(1)} %get-tuple-element.37.rest_0_, bf16[2,2,2,64,384]{4,3,2,1,0:T(8,128)(2,1)S(1)} %collective-permute-done.2.rest_1_, bf16[2,2,2,64,384]{4,3,2,1,0:T(8,128)(2,1)} %collective-permute-done.6.rest_2_, ...), custom_call_target="tpu_custom_call" | custom-call | flops 2040000000 | bytes 5000000 | tf_op jit(solution)/shard_map/one_part/pallas_call | solution.py:338
  83.5 7.4 %all-to-all-done.1.parts = bf16[16,24,1728]{2,1,0:T(8,128)(2,1)S(1)} async-done(((bf16[16,24,1728]{2,1,0:T(8,128)(2,1)}), bf16[16,24,1728]{2,1,0:T(8,128)(2,1)S(1)}, u32[]{:S(2)}, u32[]{:S(2)}) %all-to-all-start.1) | async-done | bytes 1327136 | tf_op jit(solution)/shard_map/all_to_all | solution.py:459
  90.9 3.6 %all-to-all-start.2 = ((bf16[16,24,768]{2,1,0:T(8,128)(2,1)}), bf16[16,24,768]{2,1,0:T(8,128)(2,1)S(1)}, u32[]{:S(2)}, u32[]{:S(2)}) async-start(bf16[16,24,768]{2,1,0:T(8,128)(2,1)} %one_part.1), calls=%async_computation.2 | async-start | bytes 1179648 | tf_op jit(solution)/shard_map/all_to_all | solution.py:465
  94.5 3.3 %copy-done.1 = bf16[27,384,384]{2,1,0:T(8,128)(2,1)S(1)} copy-done((bf16[27,384,384]{2,1,0:T(8,128)(2,1)S(1)}, bf16[27,384,384]{2,1,0:T(8,128)(2,1)}, u32[]{:S(2)}) %copy-start.1) | copy-done | bytes 7962648
  97.8 3.8 %latents_grad.1 = bf16[2,2,64,384]{3,2,1,0:T(8,128)(2,1)} custom-call(bf16[2,2,64,384]{3,2,1,0:T(8,128)(2,1)S(1)} %get-tuple-element.48.own, bf16[2,2,64,384]{3,2,1,0:T(8,128)(2,1)S(1)} %collective-permute-done.5.after, bf16[4,64,384]{2,1,0:T(8,128)(2,1)S(1)} %collective-permute-done.12.cross, bf16[4,64,384]{2,1,0:T(8,128)(2,1)S(1)} %collective-permute-done.13.inner, ...), custom_call_target="tpu_custom_call" | custom-call | flops 2040000000 | bytes 10000000 | tf_op jit(solution)/shard_map/latents_grad/pallas_call | solution.py:278
  101.6 1.1 two_mid.1
  102.6 3.5 %all-to-all-done.2.parts = bf16[16,24,768]{2,1,0:T(8,128)(2,1)S(1)} async-done(((bf16[16,24,768]{2,1,0:T(8,128)(2,1)}), bf16[16,24,768]{2,1,0:T(8,128)(2,1)S(1)}, u32[]{:S(2)}, u32[]{:S(2)}) %all-to-all-start.2) | async-done | bytes 589856 | tf_op jit(solution)/shard_map/all_to_all | solution.py:465
  106.1 4.8 %all-to-all-start.3 = ((bf16[16,24,128]{2,1,0:T(8,128)(2,1)}), bf16[16,24,128]{2,1,0:T(8,128)(2,1)S(1)}, u32[]{:S(2)}, u32[]{:S(2)}) async-start(bf16[16,24,128]{2,1,0:T(8,128)(2,1)} %two_mid.1), calls=%async_computation.3 | async-start | bytes 196608 | tf_op jit(solution)/shard_map/all_to_all | solution.py:468
  110.9 0.9 final_one.1
  111.8 7.6 %all-to-all-done.3.parts = bf16[16,24,128]{2,1,0:T(8,128)(2,1)S(1)} async-done(((bf16[16,24,128]{2,1,0:T(8,128)(2,1)}), bf16[16,24,128]{2,1,0:T(8,128)(2,1)S(1)}, u32[]{:S(2)}, u32[]{:S(2)}) %all-to-all-start.3) | async-done | bytes 98336 | tf_op jit(solution)/shard_map/all_to_all | solution.py:468
  119.5 0.7 final_two.1
  (17 shorter events, 0.0 us)
Async XLA Ops:
  0.6 4.6 %collective-permute-start.1 = (bf16[2,2,64,384]{3,2,1,0:T(8,128)(2,1)}, bf16[2,2,64,384]{3,2,1,0:T(8,128)(2,1)S(1)}, u32[]{:S(2)}, u32[]{:S(2)}) collective-permute-start(bf16[2,2,64,384]{3,2,1,0:T(8,128)(2,1)} %bitcast.13), channel_id=1, source_target_pairs={{0,1},{1,0},{2,3},{3,2},{4,5},{5,4},{6,7},{7,6},{8,9},{9,8},{10,11... | collective-permute-start | bytes 589832 | tf_op jit(solution)/shard_map/ppermute | solution.py:426
  4.0 7.9 %collective-permute-start = (bf16[2,2,64,384]{3,2,1,0:T(8,128)(2,1)}, bf16[2,2,64,384]{3,2,1,0:T(8,128)(2,1)S(1)}, u32[]{:S(2)}, u32[]{:S(2)}) collective-permute-start(bf16[2,2,64,384]{3,2,1,0:T(8,128)(2,1)} %bitcast.14), channel_id=1, source_target_pairs={{0,16},{16,32},{32,48},{48,0},{1,17},{17,33},{33,49},{49,1},{2,18}... | collective-permute-start | bytes 589832 | tf_op jit(solution)/shard_map/ppermute | solution.py:437
  5.2 0.9 copy-start.2
  6.2 1.0 copy-start.4
  7.2 12.4 %collective-permute-start.2 = (bf16[2,2,2,64,384]{4,3,2,1,0:T(8,128)(2,1)S(1)}, bf16[2,2,2,64,384]{4,3,2,1,0:T(8,128)(2,1)S(1)}, u32[]{:S(2)}, u32[]{:S(2)}) collective-permute-start(bf16[2,2,2,64,384]{4,3,2,1,0:T(8,128)(2,1)S(1)} %get-tuple-element.37.rest_0_), channel_id=1, source_target_pairs={{0,2},{1,15},{2,4},{3,1},{4,6},{5,3},{6,8},{7,5},{8,10},{9,7},{10,... | collective-permute-start | bytes 1179656 | tf_op jit(solution)/shard_map/ppermute | solution.py:432
  11.9 11.3 %copy-start.3 = (bf16[1,2,2,64,384]{4,3,2,1,0:T(8,128)(2,1)S(1)}, bf16[1,2,2,64,384]{4,3,2,1,0:T(8,128)(2,1)}, u32[]{:S(2)}) copy-start(bf16[1,2,2,64,384]{4,3,2,1,0:T(8,128)(2,1)} %param.4) | copy-start | bytes 589828
  11.9 11.3 %copy-start.5 = (bf16[1,2,4,128,192]{3,4,2,1,0:T(8,128)(2,1)S(1)}, bf16[1,2,4,128,192]{3,4,2,1,0:T(8,128)(2,1)}, u32[]{:S(2)}) copy-start(bf16[1,2,4,128,192]{3,4,2,1,0:T(8,128)(2,1)} %param.7) | copy-start | bytes 1179652
  11.9 11.3 %copy-start.6 = (bf16[3,3,384,192]{2,3,1,0:T(8,128)(2,1)S(1)}, bf16[3,3,384,192]{2,3,1,0:T(8,128)(2,1)}, u32[]{:S(2)}) copy-start(bf16[3,3,384,192]{2,3,1,0:T(8,128)(2,1)} %param.6) | copy-start | bytes 3981316
  11.9 7.7 %collective-permute-start.3 = (bf16[6,64,384]{2,1,0:T(8,128)(2,1)S(1)}, bf16[6,64,384]{2,1,0:T(8,128)(2,1)S(1)}, u32[]{:S(2)}, u32[]{:S(2)}) collective-permute-start(bf16[6,64,384]{2,1,0:T(8,128)(2,1)S(1)} %get-tuple-element.43), channel_id=1, source_target_pairs={{0,15},{1,2},{2,1},{3,4},{4,3},{5,6},{6,5},{7,8},{8,7},{9,10},{10,... | collective-permute-start | bytes 884744 | tf_op jit(solution)/shard_map/ppermute | solution.py:429
  12.7 7.0 %collective-permute-start.4 = (bf16[6,64,384]{2,1,0:T(8,128)(2,1)S(1)}, bf16[6,64,384]{2,1,0:T(8,128)(2,1)S(1)}, u32[]{:S(2)}, u32[]{:S(2)}) collective-permute-start(bf16[6,64,384]{2,1,0:T(8,128)(2,1)S(1)} %get-tuple-element.44), channel_id=1, source_target_pairs={{0,1},{1,0},{2,3},{3,2},{4,5},{5,4},{6,7},{7,6},{8,9},{9,8},{10,11... | collective-permute-start | bytes 884744 | tf_op jit(solution)/shard_map/ppermute | solution.py:426
  19.6 8.2 %copy-start = (bf16[27,384,384]{2,1,0:T(8,128)(2,1)}, bf16[27,384,384]{2,1,0:T(8,128)(2,1)S(1)}, u32[]{:S(2)}) copy-start(bf16[27,384,384]{2,1,0:T(8,128)(2,1)S(1)} %load.1.wv) | copy-start | bytes 23887876
  19.7 8.3 %collective-permute-start.6 = (bf16[2,2,2,64,384]{4,3,2,1,0:T(8,128)(2,1)S(1)}, bf16[2,2,2,64,384]{4,3,2,1,0:T(8,128)(2,1)}, u32[]{:S(2)}, u32[]{:S(2)}) collective-permute-start(bf16[2,2,2,64,384]{4,3,2,1,0:T(8,128)(2,1)S(1)} %collective-permute-done.2.rest_1_), channel_id=1, source_target_pairs={{0,2},{1,15},{2,4},{3,1},{4,6},{5,3},{6,8},{7,5},{8,10},{9,7},{10,... | collective-permute-start | bytes 1179656 | tf_op jit(solution)/shard_map/ppermute | solution.py:432
  27.9 10.3 %collective-permute-start.7 = (bf16[2,2,2,64,384]{4,3,2,1,0:T(8,128)(2,1)}, bf16[2,2,2,64,384]{4,3,2,1,0:T(8,128)(2,1)}, u32[]{:S(2)}, u32[]{:S(2)}) collective-permute-start(bf16[2,2,2,64,384]{4,3,2,1,0:T(8,128)(2,1)} %collective-permute-done.6.rest_2_), channel_id=1, source_target_pairs={{0,2},{1,15},{2,4},{3,1},{4,6},{5,3},{6,8},{7,5},{8,10},{9,7},{10,... | collective-permute-start | bytes 1179656 | tf_op jit(solution)/shard_map/ppermute | solution.py:432
  31.2 6.2 %collective-permute-start.5 = (bf16[2,2,64,384]{3,2,1,0:T(8,128)(2,1)S(1)}, bf16[2,2,64,384]{3,2,1,0:T(8,128)(2,1)S(1)}, u32[]{:S(2)}, u32[]{:S(2)}) collective-permute-start(bf16[2,2,64,384]{3,2,1,0:T(8,128)(2,1)S(1)} %get-tuple-element.48.own), channel_id=1, source_target_pairs={{16,0},{32,16},{48,32},{0,48},{17,1},{33,17},{49,33},{1,49},{18,2}... | collective-permute-start | bytes 589832 | tf_op jit(solution)/shard_map/ppermute | solution.py:448
  38.2 8.9 %copy-start.7 = (bf16[4,64,384]{2,1,0:T(8,128)(2,1)}, bf16[4,64,384]{2,1,0:T(8,128)(2,1)S(1)}, u32[]{:S(2)}) copy-start(bf16[4,64,384]{2,1,0:T(8,128)(2,1)S(1)} %get-tuple-element.63) | copy-start | bytes 589828
  38.2 21.7 %all-to-all-start = ((bf16[16,24,512]{2,1,0:T(8,128)(2,1)}), bf16[16,24,512]{2,1,0:T(8,128)(2,1)S(1)}, u32[]{:S(2)}, u32[]{:S(2)}) async-start(bf16[16,24,512]{2,1,0:T(8,128)(2,1)} %get-tuple-element.57), calls=%async_computation | async-start | bytes 786432 | tf_op jit(solution)/shard_map/all_to_all | solution.py:455
  59.9 15.8 %copy-start.8 = (bf16[4,64,384]{2,1,0:T(8,128)(2,1)S(1)}, bf16[4,64,384]{2,1,0:T(8,128)(2,1)}, u32[]{:S(2)}) copy-start(bf16[4,64,384]{2,1,0:T(8,128)(2,1)} %copy-done.7) | copy-start | bytes 589828
  59.9 30.9 %all-to-all-start.1 = ((bf16[16,24,1728]{2,1,0:T(8,128)(2,1)}), bf16[16,24,1728]{2,1,0:T(8,128)(2,1)S(1)}, u32[]{:S(2)}, u32[]{:S(2)}) async-start(bf16[16,24,1728]{2,1,0:T(8,128)(2,1)} %two_part.1), calls=%async_computation.1 | async-start | bytes 2752512 | tf_op jit(solution)/shard_map/all_to_all | solution.py:459
  66.4 9.3 %collective-permute-start.8 = (bf16[2,2,2,64,384]{4,3,2,1,0:T(8,128)(2,1)}, bf16[2,2,2,64,384]{4,3,2,1,0:T(8,128)(2,1)S(1)}, u32[]{:S(2)}, u32[]{:S(2)}) collective-permute-start(bf16[2,2,2,64,384]{4,3,2,1,0:T(8,128)(2,1)} %collective-permute-done.7.rest_3_), channel_id=1, source_target_pairs={{0,2},{1,15},{2,4},{3,1},{4,6},{5,3},{6,8},{7,5},{8,10},{9,7},{10,... | collective-permute-start | bytes 1179656 | tf_op jit(solution)/shard_map/ppermute | solution.py:432
  66.5 10.8 %collective-permute-start.9 = (bf16[2,2,2,64,384]{4,3,2,1,0:T(8,128)(2,1)S(1)}, bf16[2,2,2,64,384]{4,3,2,1,0:T(8,128)(2,1)S(1)}, u32[]{:S(2)}, u32[]{:S(2)}) collective-permute-start(bf16[2,2,2,64,384]{4,3,2,1,0:T(8,128)(2,1)S(1)} %collective-permute-done.2.rest_1_), channel_id=1, source_target_pairs={{0,1},{1,0},{2,3},{3,2},{4,5},{5,4},{6,7},{7,6},{8,9},{9,8},{10,11... | collective-permute-start | bytes 1179656 | tf_op jit(solution)/shard_map/ppermute | solution.py:426
  66.8 10.5 %collective-permute-start.10 = (bf16[2,2,2,64,384]{4,3,2,1,0:T(8,128)(2,1)}, bf16[2,2,2,64,384]{4,3,2,1,0:T(8,128)(2,1)S(1)}, u32[]{:S(2)}, u32[]{:S(2)}) collective-permute-start(bf16[2,2,2,64,384]{4,3,2,1,0:T(8,128)(2,1)} %collective-permute-done.6.rest_2_), channel_id=1, source_target_pairs={{0,1},{1,0},{2,3},{3,2},{4,5},{5,4},{6,7},{7,6},{8,9},{9,8},{10,11... | collective-permute-start | bytes 1179656 | tf_op jit(solution)/shard_map/ppermute | solution.py:426
  67.3 10.0 %collective-permute-start.11 = (bf16[2,2,2,64,384]{4,3,2,1,0:T(8,128)(2,1)}, bf16[2,2,2,64,384]{4,3,2,1,0:T(8,128)(2,1)S(1)}, u32[]{:S(2)}, u32[]{:S(2)}) collective-permute-start(bf16[2,2,2,64,384]{4,3,2,1,0:T(8,128)(2,1)} %collective-permute-done.7.rest_3_), channel_id=1, source_target_pairs={{0,1},{1,0},{2,3},{3,2},{4,5},{5,4},{6,7},{7,6},{8,9},{9,8},{10,11... | collective-permute-start | bytes 1179656 | tf_op jit(solution)/shard_map/ppermute | solution.py:426
  67.4 16.1 %collective-permute-start.12 = (bf16[4,64,384]{2,1,0:T(8,128)(2,1)}, bf16[4,64,384]{2,1,0:T(8,128)(2,1)S(1)}, u32[]{:S(2)}, u32[]{:S(2)}) collective-permute-start(bf16[4,64,384]{2,1,0:T(8,128)(2,1)} %get-tuple-element.62), channel_id=1, source_target_pairs={{0,15},{1,2},{2,1},{3,4},{4,3},{5,6},{6,5},{7,8},{8,7},{9,10},{10,... | collective-permute-start | bytes 589832 | tf_op jit(solution)/shard_map/ppermute | solution.py:429
  75.8 7.7 %collective-permute-start.13 = (bf16[4,64,384]{2,1,0:T(8,128)(2,1)S(1)}, bf16[4,64,384]{2,1,0:T(8,128)(2,1)S(1)}, u32[]{:S(2)}, u32[]{:S(2)}) collective-permute-start(bf16[4,64,384]{2,1,0:T(8,128)(2,1)S(1)} %copy-done.8), channel_id=1, source_target_pairs={{0,1},{1,0},{2,3},{3,2},{4,5},{5,4},{6,7},{7,6},{8,9},{9,8},{10,11... | collective-permute-start | bytes 589832 | tf_op jit(solution)/shard_map/ppermute | solution.py:426
  90.9 15.2 %all-to-all-start.2 = ((bf16[16,24,768]{2,1,0:T(8,128)(2,1)}), bf16[16,24,768]{2,1,0:T(8,128)(2,1)S(1)}, u32[]{:S(2)}, u32[]{:S(2)}) async-start(bf16[16,24,768]{2,1,0:T(8,128)(2,1)} %one_part.1), calls=%async_computation.2 | async-start | bytes 1179648 | tf_op jit(solution)/shard_map/all_to_all | solution.py:465
  94.5 3.3 %copy-start.1 = (bf16[27,384,384]{2,1,0:T(8,128)(2,1)S(1)}, bf16[27,384,384]{2,1,0:T(8,128)(2,1)}, u32[]{:S(2)}) copy-start(bf16[27,384,384]{2,1,0:T(8,128)(2,1)} %copy-done) | copy-start | bytes 23887876
  106.1 13.3 %all-to-all-start.3 = ((bf16[16,24,128]{2,1,0:T(8,128)(2,1)}), bf16[16,24,128]{2,1,0:T(8,128)(2,1)S(1)}, u32[]{:S(2)}, u32[]{:S(2)}) async-start(bf16[16,24,128]{2,1,0:T(8,128)(2,1)} %two_mid.1), calls=%async_computation.3 | async-start | bytes 196608 | tf_op jit(solution)/shard_map/all_to_all | solution.py:468

commit v3 on v2

--- a/solution.py
+++ b/solution.py
@@ -151,9 +151,10 @@
     return jnp.concatenate(pick, axis=0).astype(BF)
 
 
-def forward_kernel(own, prev, cross, inner, cotv, w2, wv, gp, gpt, ht, gcat, xx, w2v, sem):
-    last = pltpu.make_async_copy(w2, w2v, sem)
-    last.start()
+def forward_kernel(
+    own, prev, cross, inner, cotv, w2, wv, gp, gpt, ht, keep, give, xx, gcat, w2v, sems
+):
+    last = bring([w2.at[:, pl.ds(0, 96)], w2.at[:, pl.ds(96, 96)]], [w2v.at[0], w2v.at[1]], sems)
     at = place()
     core, above_ok, below_ok, before_ok = at[:4]
     stack_columns(xx, prev, own, cross, inner, at, (before_ok, None), 1)
@@ -177,15 +178,23 @@
                     pick, pair, (((1,), (1,)), ((), ())), preferred_element_type=F32
                 ).astype(BF)
                 for k in range(3):
-                    gcat[rows, pl.ds((j * 3 + k) * 192, 192)] = box[k * 64 : (k + 1) * 64]
+                    for half in range(2):
+                        piece = box[k * 64 : (k + 1) * 64, half * 96 : half * 96 + 96]
+                        gcat[half, rows, pl.ds((j * 3 + k) * 96, 96)] = piece
     pre = jnp.zeros((256, 384), F32)
     for n in range(9):
         i, j = n // 3, n % 3
         lhs = xx[i : i + 2, j : j + 2].reshape(256, 1152)
         rhs = wv[3 * n : 3 * n + 3].reshape(1152, 384)
         pre = pre + jnp.dot(lhs, rhs, preferred_element_type=F32)
-    last.wait()
-    gh = jnp.dot(gcat[...], w2v[...], preferred_element_type=F32)
+    keep[...] = gcat[core]
+    give[...] = gcat[1 - core]
+    for each in last:
+        each.wait()
+    gh = jnp.zeros((256, 384), F32)
+    for half in range(2):
+        rhs = w2v[half].reshape(864, 384)
+        gh = gh + jnp.dot(gcat[half], rhs, preferred_element_type=F32)
     sigma = jax.nn.sigmoid(pre)
     hidden = pre * sigma
     grad = gh * sigma * (1.0 + pre * (1.0 - sigma))
@@ -200,64 +209,64 @@
     return pl.pallas_call(
         forward_kernel,
         in_specs=vmem(5) + anywhere(1) + vmem(1),
-        out_specs=tuple(vmem(4)),
+        out_specs=tuple(vmem(5)),
         out_shape=(
             jax.ShapeDtypeStruct((2, 2, 64, 384), BF),
             jax.ShapeDtypeStruct((16, 24, 256), BF),
             jax.ShapeDtypeStruct((384, 256), BF),
-            jax.ShapeDtypeStruct((256, 1728), BF),
+            jax.ShapeDtypeStruct((256, 864), BF),
+            jax.ShapeDtypeStruct((256, 864), BF),
         ),
         scratch_shapes=[
             pltpu.VMEM((4, 4, 64, 1152), BF),
-            pltpu.VMEM((1728, 384), BF),
-            pltpu.SemaphoreType.DMA,
+            pltpu.VMEM((2, 256, 864), BF),
+            pltpu.VMEM((2, 9, 96, 384), BF),
+            pltpu.SemaphoreType.DMA((2,)),
         ],
-        compiler_params=params(24),
+        compiler_params=params(14),
         cost_estimate=cost(1_300_000_000, 12_000_000),
         name="forward",
     )(own, prev, cross, inner, cot, w2, w)
 
 
-def mix_kernel(own, after, own_t, by_channel, cross, inner):
-    at = place()
-    core, after_ok = at[0], at[4]
-    later = (after[...].reshape(256, 384).astype(F32) * after_ok).T
-    for b in range(16):
-        by_channel[b, :, 0:256] = own_t[b]
-        by_channel[b, :, 256:512] = later[b * 24 : (b + 1) * 24].astype(BF)
+def rows_kernel(own, after, cross, inner):
+    core = place()[0]
     for out, row in ((cross, core), (inner, 1 - core)):
         for t in range(2):
             out[t] = own[t, row]
             out[2 + t] = after[t, row]
 
 
-def mix(own, after, own_t):
+def rows(own, after):
     shape = jax.ShapeDtypeStruct((4, 64, 384), BF)
     return pl.pallas_call(
-        mix_kernel,
-        in_specs=vmem(3),
-        out_specs=tuple(vmem(3)),
-        out_shape=(jax.ShapeDtypeStruct((16, 24, 512), BF), shape, shape),
-        compiler_params=params(),
-        cost_estimate=cost(1000, 1_500_000),
-        name="mix",
-    )(own, after, own_t)
-
-
-def two_kernel(ht, gcat, out):
-    res = jnp.dot(ht[...], gcat[...], preferred_element_type=F32)
+        rows_kernel,
+        in_specs=vmem(2),
+        out_specs=tuple(vmem(2)),
+        out_shape=(shape, shape),
+        compiler_params=params(),
+        cost_estimate=cost(1000, 800_000),
+        name="rows",
+    )(own, after)
+
+
+def two_kernel(ht, keep, ht_other, given, out):
+    res = jnp.dot(ht[...], keep[...], preferred_element_type=F32)
+    res = res + jnp.dot(ht_other[...], given[...], preferred_element_type=F32)
     for b in range(16):
         out[b] = res[b * 24 : (b + 1) * 24].astype(BF)
 
 
-def two_part(ht, gcat):
+def two_part(ht, keep, ht_other, given):
     return pl.pallas_call(
         two_kernel,
-        out_shape=jax.ShapeDtypeStruct((16, 24, 1728), BF),
+        in_specs=vmem(4),
+        out_specs=vmem(1)[0],
+        out_shape=jax.ShapeDtypeStruct((16, 24, 864), BF),
         compiler_params=params(),
         cost_estimate=cost(170_000_000, 3_000_000),
         name="two_part",
-    )(ht, gcat)
+    )(ht, keep, ht_other, given)
 
 
 def latents_kernel(own, after, cross, inner, wv, out, gg):
@@ -283,15 +292,19 @@
         scratch_shapes=[
             pltpu.VMEM((4, 4, 64, 1152), BF),
         ],
-        compiler_params=params(24),
+        compiler_params=params(12),
         cost_estimate=cost(1_020_000_000, 10_000_000),
         name="latents_grad",
     )(own, after, cross, inner, w)
 
 
-def one_kernel(g, *rest):
-    blocks, (out, gs, cols, xv, sems) = rest[:8], rest[8:]
-    arrive = bring(blocks, [xv.at[n] for n in range(8)], sems)
+def one_kernel(g_in, g_after_in, *rest):
+    blocks, (out, gs, cols, xv, g, g_after, sems) = rest[:8], rest[8:]
+    arrive = bring(
+        (g_in, g_after_in) + blocks, [g, g_after] + [xv.at[n] for n in range(8)], sems
+    )
+    arrive[0].wait()
+    arrive[1].wait()
     lane = lax.broadcasted_iota(jnp.int32, (24, 128), 1)
     col = lane & 63
     left = lane < 64
@@ -299,11 +312,13 @@
     chip = height // 2
     way = 1 - 2 * (height - 2 * chip)
 
+    after_ok = place()[4]
     cols[0] = jnp.zeros((4, 3, 24, 128), F32)
     cols[17] = jnp.zeros((4, 3, 24, 128), F32)
     for h in range(16):
         for f in range(4):
-            mid = g[h, :, pl.ds(f * 128, 128)].astype(F32)
+            mid = (g if f < 2 else g_after)[h, :, pl.ds(f % 2 * 128, 128)].astype(F32)
+            mid = mid if f < 2 else mid * after_ok
             cols[h + 1, f, 0] = jnp.where(col == 63, 0.0, pltpu.roll(mid, 127, 1))
             cols[h + 1, f, 1] = mid
             cols[h + 1, f, 2] = jnp.where(col == 0, 0.0, pltpu.roll(mid, 1, 1))
@@ -320,7 +335,7 @@
                 to = pl.ds((2 * n + m) * 128, 128)
                 gs[f, :, to] = jnp.concatenate(rows, axis=0).astype(BF)
 
-    for each in arrive:
+    for each in arrive[2:]:
         each.wait()
     total = jnp.zeros((672, 384), F32)
     for s in range(2):
@@ -334,22 +349,24 @@
             out[c, :, b * 256 : (b + 1) * 256] = turned[c * 24 : (c + 1) * 24].astype(BF)
 
 
-def one_part(g, blocks):
+def one_part(g, g_after, blocks):
     return pl.pallas_call(
         one_kernel,
-        in_specs=vmem(1) + anywhere(8),
+        in_specs=anywhere(10),
         out_specs=vmem(1)[0],
         out_shape=jax.ShapeDtypeStruct((16, 24, 768), BF),
         scratch_shapes=[
             pltpu.VMEM((4, 224, 2048), BF),
             pltpu.VMEM((18, 4, 3, 24, 128), F32),
             pltpu.VMEM((8, 2, 2, 2, 64, 384), BF),
-            pltpu.SemaphoreType.DMA((8,)),
+            pltpu.VMEM((16, 24, 256), BF),
+            pltpu.VMEM((16, 24, 256), BF),
+            pltpu.SemaphoreType.DMA((10,)),
         ],
-        compiler_params=params(24),
+        compiler_params=params(20),
         cost_estimate=cost(1_020_000_000, 5_000_000),
         name="one_part",
-    )(g, *blocks)
+    )(g, g_after, *blocks)
 
 
 def summed(ref):
@@ -360,11 +377,13 @@
 
 
 def two_mid_kernel(parts, out):
+    core = place()[0]
     total = summed(parts)
     pad = jnp.zeros((24, 20), F32)
-    for h in range(16):
-        cut = [total[:, n * 192 + h * 12 : n * 192 + h * 12 + 12] for n in range(9)]
-        out[h] = jnp.concatenate(cut + [pad], axis=1).astype(BF)
+    for h in range(8):
+        cut = [total[:, n * 96 + h * 12 : n * 96 + h * 12 + 12] for n in range(9)]
+        out[core * 8 + h] = jnp.concatenate(cut + [pad], axis=1).astype(BF)
+        out[8 - core * 8 + h] = jnp.zeros((24, 128), BF)
 
 
 def two_mid(parts):
@@ -433,38 +452,39 @@
 
     cot = jnp.swapaxes(cot, 2, 3)
     w1 = conv_one.reshape(27, 384, 384)
-    w2 = jnp.swapaxes(conv_two, 2, 3).reshape(1728, 384)
+    w2 = jnp.swapaxes(conv_two, 2, 3).reshape(9, 192, 384)
     x_prev = lax.ppermute(x, "frame", next_perm)
     pair0, cot_cross, cot_inner = pair(x, inside(x), cot)
     pair1 = ring(pair0)
     cross, inner = edges(x, x_prev, cot_cross, cot_inner)
-    w1, cross, inner = lax.optimization_barrier((w1, cross, inner))
-    w1 = load(w1)
+    w1_first, cross, inner = lax.optimization_barrier((w1, cross, inner))
+    w1_first = load(w1_first)
     cross, inner = across(cross), inside(inner)
-    pair1, w1, cross, inner = lax.optimization_barrier((pair1, w1, cross, inner))
+    pair1, w1_first, cross, inner = lax.optimization_barrier((pair1, w1_first, cross, inner))
     pair2 = ring(pair1)
-    gp, gpt, ht, gcat = forward(x, x_prev, cross, inner, cot, w2, w1)
+    gp, gpt, ht, keep, give = forward(x, x_prev, cross, inner, cot, w2, w1_first)
 
     gp_next = lax.ppermute(gp, "frame", prev_perm)
-    gpt, pair1, pair2 = lax.optimization_barrier((gpt, pair1, pair2))
+    g = lax.all_to_all(gpt, "height", 0, 0, tiled=True)
+    pair2, _ = lax.optimization_barrier((pair2, gp_next))
     pair3 = ring(pair2)
-    by_channel, cross, inner = mix(gp, gp_next, gpt)
-    by_channel, cross, inner, ht, pair3 = lax.optimization_barrier(
-        (by_channel, cross, inner, ht, pair3)
-    )
-    g = lax.all_to_all(by_channel, "height", 0, 0, tiled=True)
+    ht_other, given = inside(ht), inside(give)
+    cross, inner = rows(gp, gp_next)
     cross, inner = across(cross), inside(inner)
+    g_next = lax.ppermute(g, "frame", prev_perm)
+    ht, _, _ = lax.optimization_barrier((ht, gp_next, g))
+    two = two_part(ht, keep, ht_other, given)
+    w1, two = lax.optimization_barrier((w1, two))
+    two = lax.all_to_all(two, ("dp", "frame"), 0, 0, tiled=True)
+    w1, pair3 = lax.optimization_barrier((load(w1), pair3))
     pair4 = ring(pair3)
-    two = two_part(ht, gcat)
-    two = lax.all_to_all(two, ("dp", "frame"), 0, 0, tiled=True)
-    g, pair4 = lax.optimization_barrier((g, pair4))
-    blocks = (pair0, pair1, pair2, pair3, pair4, inside(pair1), inside(pair2), inside(pair3))
-
-    one = one_part(g, blocks)
-    one, cross, inner = lax.optimization_barrier((one, cross, inner))
+    grad_in = latents_grad(gp, gp_next, cross, inner, w1)
+    far1, far2 = inside(pair1), inside(pair2)
+    pair3, far1, far2, _ = lax.optimization_barrier((pair3, far1, far2, grad_in))
+    blocks = (pair0, pair1, pair2, pair3, pair4, far1, far2, inside(pair3))
+
+    one = one_part(g, g_next, blocks)
     one = lax.all_to_all(one, ("dp", "frame"), 0, 0, tiled=True)
-    grad_in = latents_grad(gp, gp_next, cross, inner, w1)
-    grad_in, two = lax.optimization_barrier((grad_in, two))
     two = lax.all_to_all(two_mid(two), "height", 0, 0, tiled=True)
     one = final_one(one).reshape(3, 3, 3, 24, 24)
     two = jnp.swapaxes(final_two(two).reshape(3, 3, 12, 24), 2, 3)

time: 121 us -> 97.5 us (0.81)
  waiting for transfers between devices: 45.1 us -> 24.7 us
  Pallas kernels: 23.3 us -> 27.6 us
  starting transfers between devices: 45.8 us -> 42 us
  local copies, waits for them, and re-layouts: 5.21 us -> 1.94 us
    all_to_all x1, waiting for transfers between devices: 3.51 us -> 11.8 us  [local(): one = lax.all_to_all(one, ('dp', 'frame'), 0, 0, tiled=True)]
    all_to_all x1, waiting for transfers between devices: 12.8 us -> 4.64 us  [local(): g = lax.all_to_all(gpt, 'height', 0, 0, tiled=True)]
    ppermute x4, waiting for transfers between devices: 7 us -> 0.01 us  [ring(): return lax.ppermute(value, 'height', ring_perm)]
    all_to_all x1, waiting for transfers between devices: 7.61 us -> 2.12 us  [local(): two = lax.all_to_all(two_mid(two), 'height', 0, 0, tiled=True)]
    ppermute x1, waiting for transfers between devices: 4.73 us -> 0.01 us  [local(): gp_next = lax.ppermute(gp, 'frame', prev_perm)]
    all_to_all x1, waiting for transfers between devices: 7.43 us -> 3.77 us  [local(): two = lax.all_to_all(two, ('dp', 'frame'), 0, 0, tiled=True)]
    pallas_call x1 -> x2, Pallas kernels: 3.35 us -> 6.7 us  [load(): pl.pallas_call(load_kernel, in_specs=anywhere(1), out_specs=vmem(1)[0], o...]
    unnamed x18 -> x10, local copies, waits for them, and re-layouts: 5.21 us -> 1.94 us
  transfers between devices with their start and end apart: 18 -> 21, of which waited for: 9 -> 7; matrix products, arithmetic and copies ran while one was open for 0% -> 0% of each run, Pallas kernels for 19% -> 27%
where the time goes in v3:
time: 97.5 us; the launch traced here: 97 us
  starting transfers between devices  42 us (43%)
  Pallas kernels  27.6 us (28%)
  waiting for transfers between devices  24.7 us (25%)
  local copies, waits for them, and re-layouts  1.94 us (2%)
    all_to_all x1, waiting for transfers between devices, local(): one = lax.all_to_all(one, ('dp', 'frame'), 0, 0, tiled=True)  11.8 us
    ppermute x4, starting transfers between devices, ring(): return lax.ppermute(value, 'height', ring_perm)  10.3 us
    ppermute x8, starting transfers between devices, inside(): return lax.ppermute(value, 'height', inner_perm)  8.83 us
    pallas_call x2, Pallas kernels, load(): pl.pallas_call(load_kernel, in_specs=anywhere(1), out_specs=vmem(1)[0], o...  6.7 us
    pallas_call x1, Pallas kernels, one_part(): pl.pallas_call(one_kernel, in_specs=anywhere(10), out_specs=vmem(1)[0], o...  6.36 us
    pallas_call x1, Pallas kernels, forward(): pl.pallas_call(forward_kernel, in_specs=vmem(5) + anywhere(1) + vmem(1),...  5.8 us
    all_to_all x1, starting transfers between devices, local(): g = lax.all_to_all(gpt, 'height', 0, 0, tiled=True)  5.26 us
    all_to_all x1, waiting for transfers between devices, local(): g = lax.all_to_all(gpt, 'height', 0, 0, tiled=True)  4.64 us
  transfers between devices with their start and end apart: 21, of which 7 were waited for; matrix products, arithmetic and copies ran while one was open for 0% of the time, Pallas kernels for 27%

profile of v3, /device:TPU:1, one launch (start us, length us, event | category | flops | bytes accessed | tf_op | source)
XLA Modules:
  0.0 97.0 jit_solution(4756897308782860394)
XLA Ops:
  0.6 3.3 %collective-permute-start.1 = (bf16[2,2,64,384]{3,2,1,0:T(8,128)(2,1)}, bf16[2,2,64,384]{3,2,1,0:T(8,128)(2,1)S(1)}, u32[]{:S(2)}, u32[]{:S(2)}) collective-permute-start(bf16[2,2,64,384]{3,2,1,0:T(8,128)(2,1)} %bitcast.13), channel_id=1, source_target_pairs={{0,1},{1,0},{2,3},{3,2},{4,5},{5,4},{6,7},{7,6},{8,9},{9,8},{10,11... | collective-permute-start | bytes 589832 | tf_op jit(solution)/shard_map/ppermute | solution.py:445
  4.0 1.3 %collective-permute-done.1.other = bf16[2,2,64,384]{3,2,1,0:T(8,128)(2,1)S(1)} collective-permute-done((bf16[2,2,64,384]{3,2,1,0:T(8,128)(2,1)}, bf16[2,2,64,384]{3,2,1,0:T(8,128)(2,1)S(1)}, u32[]{:S(2)}, u32[]{:S(2)}) %collective-permute-start.1) | collective-permute-done | bytes 196640 | tf_op jit(solution)/shard_map/ppermute | solution.py:445
  5.2 0.9 copy-done
  6.2 1.0 %copy-done.2 = bf16[1,2,4,128,192]{3,4,2,1,0:T(8,128)(2,1)S(1)} copy-done((bf16[1,2,4,128,192]{3,4,2,1,0:T(8,128)(2,1)S(1)}, bf16[1,2,4,128,192]{3,4,2,1,0:T(8,128)(2,1)}, u32[]{:S(2)}) %copy-start.2) | copy-done | bytes 393240
  7.2 0.1 pair.1
  7.2 3.9 %collective-permute-start.2 = (bf16[2,2,2,64,384]{4,3,2,1,0:T(8,128)(2,1)S(1)}, bf16[2,2,2,64,384]{4,3,2,1,0:T(8,128)(2,1)S(1)}, u32[]{:S(2)}, u32[]{:S(2)}) collective-permute-start(bf16[2,2,2,64,384]{4,3,2,1,0:T(8,128)(2,1)S(1)} %get-tuple-element.31.rest_0_), channel_id=1, source_target_pairs={{0,2},{1,15},{2,4},{3,1},{4,6},{5,3},{6,8},{7,5},{8,10},{9,7},{10,... | collective-permute-start | bytes 1179656 | tf_op jit(solution)/shard_map/ppermute | solution.py:451
  11.2 0.7 collective-permute-done.prev
  11.8 0.1 edges.1
  11.9 0.0 copy-start.1
  11.9 0.0 copy-start.3
  11.9 0.0 copy-start.4
  11.9 0.7 collective-permute-start.3
  12.7 3.6 %collective-permute-start.4 = (bf16[6,64,384]{2,1,0:T(8,128)(2,1)S(1)}, bf16[6,64,384]{2,1,0:T(8,128)(2,1)S(1)}, u32[]{:S(2)}, u32[]{:S(2)}) collective-permute-start(bf16[6,64,384]{2,1,0:T(8,128)(2,1)S(1)} %get-tuple-element.38), channel_id=1, source_target_pairs={{0,1},{1,0},{2,3},{3,2},{4,5},{5,4},{6,7},{7,6},{8,9},{9,8},{10,11... | collective-permute-start | bytes 884744 | tf_op jit(solution)/shard_map/ppermute | solution.py:445
  16.3 3.3 %load.2.wv = bf16[27,384,384]{2,1,0:T(8,128)(2,1)S(1)} custom-call(bf16[27,384,384]{2,1,0:T(8,128)(2,1)} %bitcast.21), custom_call_target="tpu_custom_call" | custom-call | flops 2000 | bytes 16000000 | tf_op jit(solution)/shard_map/load/pallas_call | solution.py:86
  19.6 0.0 collective-permute-done.4.inner
  19.6 3.6 %collective-permute-start.10 = (bf16[2,2,2,64,384]{4,3,2,1,0:T(8,128)(2,1)S(1)}, bf16[2,2,2,64,384]{4,3,2,1,0:T(8,128)(2,1)}, u32[]{:S(2)}, u32[]{:S(2)}) collective-permute-start(bf16[2,2,2,64,384]{4,3,2,1,0:T(8,128)(2,1)S(1)} %collective-permute-done.2.rest_1_), channel_id=1, source_target_pairs={{0,2},{1,15},{2,4},{3,1},{4,6},{5,3},{6,8},{7,5},{8,10},{9,7},{10,... | collective-permute-start | bytes 1179656 | tf_op jit(solution)/shard_map/ppermute | solution.py:451
  23.2 5.8 %forward.1 = (bf16[2,2,64,384]{3,2,1,0:T(8,128)(2,1)S(1)}, bf16[16,24,256]{2,1,0:T(8,128)(2,1)}, bf16[384,256]{1,0:T(8,128)(2,1)S(1)}, bf16[256,864]{1,0:T(8,128)(2,1)S(1)}, bf16[256,864]{1,0:T(8,128)(2,1)S(1)}) custom-call(bf16[2,2,64,384]{3,2,1,0:T(8,128)(2,1)S(1)} %bitcast.17, bf16[2,2,64,384]{3,2,1,0:T(8,128)(2,1)S(1)} %collective-permute-done.prev, ...), custom_call_target="tpu_custom_call" | custom-call | flops 2600000000 | bytes 12000000 | tf_op jit(solution)/shard_map/forward/pallas_call | solution.py:209
  29.0 0.1 collective-permute-start.9
  29.1 1.5 %collective-permute-start.5 = (bf16[2,2,64,384]{3,2,1,0:T(8,128)(2,1)S(1)}, bf16[2,2,64,384]{3,2,1,0:T(8,128)(2,1)S(1)}, u32[]{:S(2)}, u32[]{:S(2)}) collective-permute-start(bf16[2,2,64,384]{3,2,1,0:T(8,128)(2,1)S(1)} %get-tuple-element.42.own), channel_id=1, source_target_pairs={{16,0},{32,16},{48,32},{0,48},{17,1},{33,17},{49,33},{1,49},{18,2}... | collective-permute-start | bytes 589832 | tf_op jit(solution)/shard_map/ppermute | solution.py:467
  30.6 5.3 %all-to-all-start = ((bf16[16,24,256]{2,1,0:T(8,128)(2,1)}), bf16[16,24,256]{2,1,0:T(8,128)(2,1)S(1)}, u32[]{:S(2)}, u32[]{:S(2)}) async-start(bf16[16,24,256]{2,1,0:T(8,128)(2,1)} %get-tuple-element.46), calls=%async_computation | async-start | bytes 393216 | tf_op jit(solution)/shard_map/all_to_all | solution.py:468
  35.9 0.0 collective-permute-done.5.after
  35.9 2.7 %collective-permute-start.11 = (bf16[2,2,2,64,384]{4,3,2,1,0:T(8,128)(2,1)}, bf16[2,2,2,64,384]{4,3,2,1,0:T(8,128)(2,1)}, u32[]{:S(2)}, u32[]{:S(2)}) collective-permute-start(bf16[2,2,2,64,384]{4,3,2,1,0:T(8,128)(2,1)} %collective-permute-done.10.rest_2_), channel_id=1, source_target_pairs={{0,2},{1,15},{2,4},{3,1},{4,6},{5,3},{6,8},{7,5},{8,10},{9,7},{10,... | collective-permute-start | bytes 1179656 | tf_op jit(solution)/shard_map/ppermute | solution.py:451
  38.6 0.5 collective-permute-start.13
  39.1 0.0 collective-permute-start.14
  39.1 0.8 rows.1
  39.9 0.4 collective-permute-done.8.ht_other
  40.3 0.5 collective-permute-start.6
  40.8 1.1 %collective-permute-start.7 = (bf16[4,64,384]{2,1,0:T(8,128)(2,1)}, bf16[4,64,384]{2,1,0:T(8,128)(2,1)S(1)}, u32[]{:S(2)}, u32[]{:S(2)}) collective-permute-start(bf16[4,64,384]{2,1,0:T(8,128)(2,1)} %get-tuple-element.44), channel_id=1, source_target_pairs={{0,1},{1,0},{2,3},{3,2},{4,5},{5,4},{6,7},{7,6},{8,9},{9,8},{10,11... | collective-permute-start | bytes 589832 | tf_op jit(solution)/shard_map/ppermute | solution.py:445
  41.9 4.6 %all-to-all-done.g_in = bf16[16,24,256]{2,1,0:T(8,128)(2,1)S(1)} async-done(((bf16[16,24,256]{2,1,0:T(8,128)(2,1)}), bf16[16,24,256]{2,1,0:T(8,128)(2,1)S(1)}, u32[]{:S(2)}, u32[]{:S(2)}) %all-to-all-start) | async-done | bytes 196640 | tf_op jit(solution)/shard_map/all_to_all | solution.py:468
  46.5 1.4 %two_part.1 = bf16[16,24,864]{2,1,0:T(8,128)(2,1)} custom-call(bf16[384,256]{1,0:T(8,128)(2,1)S(1)} %get-tuple-element.47.ht, bf16[256,864]{1,0:T(8,128)(2,1)S(1)} %get-tuple-element.48.keep, bf16[384,256]{1,0:T(8,128)(2,1)S(1)} %collective-permute-done.8.ht_other, bf16[256,864]{1,0:T(8,128)(2,1)S(1)} %collective-permute-done.9.given), custom_call_target="tpu_custom_call" | custom-call | flops 340000000 | bytes 3000000 | tf_op jit(solution)/shard_map/two_part/pallas_call | solution.py:261
  47.9 4.5 %all-to-all-start.2 = ((bf16[16,24,864]{2,1,0:T(8,128)(2,1)}), bf16[16,24,864]{2,1,0:T(8,128)(2,1)S(1)}, u32[]{:S(2)}, u32[]{:S(2)}) async-start(bf16[16,24,864]{2,1,0:T(8,128)(2,1)} %two_part.1), calls=%async_computation.2 | async-start | bytes 1376256 | tf_op jit(solution)/shard_map/all_to_all | solution.py:478
  52.5 3.4 %load.3.wv = bf16[27,384,384]{2,1,0:T(8,128)(2,1)S(1)} custom-call(bf16[27,384,384]{2,1,0:T(8,128)(2,1)} %bitcast.22), custom_call_target="tpu_custom_call" | custom-call | flops 2000 | bytes 16000000 | tf_op jit(solution)/shard_map/load/pallas_call | solution.py:86
  55.8 0.1 collective-permute-start.15
  56.0 3.8 %latents_grad.1 = bf16[2,2,64,384]{3,2,1,0:T(8,128)(2,1)} custom-call(bf16[2,2,64,384]{3,2,1,0:T(8,128)(2,1)S(1)} %get-tuple-element.42.own, bf16[2,2,64,384]{3,2,1,0:T(8,128)(2,1)S(1)} %collective-permute-done.5.after, bf16[4,64,384]{2,1,0:T(8,128)(2,1)S(1)} %collective-permute-done.6.cross, bf16[4,64,384]{2,1,0:T(8,128)(2,1)S(1)} %collective-permute-done.7.inner, ...), custom_call_target="tpu_custom_call" | custom-call | flops 2040000000 | bytes 10000000 | tf_op jit(solution)/shard_map/latents_grad/pallas_call | solution.py:287
  59.8 0.0 collective-permute-done.13.rest_5_
  59.8 0.0 collective-permute-done.14.rest_6_
  59.8 0.2 collective-permute-start.16
  60.0 2.9 %collective-permute-start.12 = (bf16[16,24,256]{2,1,0:T(8,128)(2,1)S(1)}, bf16[16,24,256]{2,1,0:T(8,128)(2,1)S(1)}, u32[]{:S(2)}, u32[]{:S(2)}) collective-permute-start(bf16[16,24,256]{2,1,0:T(8,128)(2,1)S(1)} %all-to-all-done.g_in), channel_id=1, source_target_pairs={{16,0},{32,16},{48,32},{0,48},{17,1},{33,17},{49,33},{1,49},{18,2}... | collective-permute-start | bytes 589832 | tf_op jit(solution)/shard_map/ppermute | solution.py:474
  62.9 3.8 %all-to-all-done.2.parts = bf16[16,24,864]{2,1,0:T(8,128)(2,1)S(1)} async-done(((bf16[16,24,864]{2,1,0:T(8,128)(2,1)}), bf16[16,24,864]{2,1,0:T(8,128)(2,1)S(1)}, u32[]{:S(2)}, u32[]{:S(2)}) %all-to-all-start.2) | async-done | bytes 663584 | tf_op jit(solution)/shard_map/all_to_all | solution.py:478
  66.6 0.9 two_mid.1
  67.6 3.9 %all-to-all-start.3 = ((bf16[16,24,128]{2,1,0:T(8,128)(2,1)}), bf16[16,24,128]{2,1,0:T(8,128)(2,1)S(1)}, u32[]{:S(2)}, u32[]{:S(2)}) async-start(bf16[16,24,128]{2,1,0:T(8,128)(2,1)} %two_mid.1), calls=%async_computation.3 | async-start | bytes 196608 | tf_op jit(solution)/shard_map/all_to_all | solution.py:488
  71.5 0.0 collective-permute-done.15.rest_4_
  71.5 6.4 %one_part.1 = bf16[16,24,768]{2,1,0:T(8,128)(2,1)} custom-call(bf16[16,24,256]{2,1,0:T(8,128)(2,1)S(1)} %all-to-all-done.g_in, bf16[16,24,256]{2,1,0:T(8,128)(2,1)S(1)} %collective-permute-done.12.g_after_in, bf16[2,2,2,64,384]{4,3,2,1,0:T(8,128)(2,1)S(1)} %get-tuple-element.31.rest_0_, bf16[2,2,2,64,384]{4,3,2,1,0:T(8,128)(2,1)S(1)} %collective-permute-done.2.rest_1_, ...), custom_call_target="tpu_custom_call" | custom-call | flops 2040000000 | bytes 5000000 | tf_op jit(solution)/shard_map/one_part/pallas_call | solution.py:353
  77.9 2.1 %all-to-all-done.3.parts = bf16[16,24,128]{2,1,0:T(8,128)(2,1)S(1)} async-done(((bf16[16,24,128]{2,1,0:T(8,128)(2,1)}), bf16[16,24,128]{2,1,0:T(8,128)(2,1)S(1)}, u32[]{:S(2)}, u32[]{:S(2)}) %all-to-all-start.3) | async-done | bytes 98336 | tf_op jit(solution)/shard_map/all_to_all | solution.py:488
  80.0 3.6 %all-to-all-start.1 = ((bf16[16,24,768]{2,1,0:T(8,128)(2,1)}), bf16[16,24,768]{2,1,0:T(8,128)(2,1)S(1)}, u32[]{:S(2)}, u32[]{:S(2)}) async-start(bf16[16,24,768]{2,1,0:T(8,128)(2,1)} %one_part.1), calls=%async_computation.1 | async-start | bytes 1179648 | tf_op jit(solution)/shard_map/all_to_all | solution.py:487
  83.6 0.7 final_two.1
  84.3 11.8 %all-to-all-done.1.parts = bf16[16,24,768]{2,1,0:T(8,128)(2,1)S(1)} async-done(((bf16[16,24,768]{2,1,0:T(8,128)(2,1)}), bf16[16,24,768]{2,1,0:T(8,128)(2,1)S(1)}, u32[]{:S(2)}, u32[]{:S(2)}) %all-to-all-start.1) | async-done | bytes 589856 | tf_op jit(solution)/shard_map/all_to_all | solution.py:487
  96.1 0.9 final_one.1
  (16 shorter events, 0.0 us)
Async XLA Ops:
  0.6 4.6 %collective-permute-start.1 = (bf16[2,2,64,384]{3,2,1,0:T(8,128)(2,1)}, bf16[2,2,64,384]{3,2,1,0:T(8,128)(2,1)S(1)}, u32[]{:S(2)}, u32[]{:S(2)}) collective-permute-start(bf16[2,2,64,384]{3,2,1,0:T(8,128)(2,1)} %bitcast.13), channel_id=1, source_target_pairs={{0,1},{1,0},{2,3},{3,2},{4,5},{5,4},{6,7},{7,6},{8,9},{9,8},{10,11... | collective-permute-start | bytes 589832 | tf_op jit(solution)/shard_map/ppermute | solution.py:445
  4.0 7.9 %collective-permute-start = (bf16[2,2,64,384]{3,2,1,0:T(8,128)(2,1)}, bf16[2,2,64,384]{3,2,1,0:T(8,128)(2,1)S(1)}, u32[]{:S(2)}, u32[]{:S(2)}) collective-permute-start(bf16[2,2,64,384]{3,2,1,0:T(8,128)(2,1)} %bitcast.14), channel_id=1, source_target_pairs={{0,16},{16,32},{32,48},{48,0},{1,17},{17,33},{33,49},{49,1},{2,18}... | collective-permute-start | bytes 589832 | tf_op jit(solution)/shard_map/ppermute | solution.py:456
  5.2 0.9 copy-start
  6.2 1.0 %copy-start.2 = (bf16[1,2,4,128,192]{3,4,2,1,0:T(8,128)(2,1)S(1)}, bf16[1,2,4,128,192]{3,4,2,1,0:T(8,128)(2,1)}, u32[]{:S(2)}) copy-start(bf16[1,2,4,128,192]{3,4,2,1,0:T(8,128)(2,1)} %param.7) | copy-start | bytes 1179652
  7.2 12.4 %collective-permute-start.2 = (bf16[2,2,2,64,384]{4,3,2,1,0:T(8,128)(2,1)S(1)}, bf16[2,2,2,64,384]{4,3,2,1,0:T(8,128)(2,1)S(1)}, u32[]{:S(2)}, u32[]{:S(2)}) collective-permute-start(bf16[2,2,2,64,384]{4,3,2,1,0:T(8,128)(2,1)S(1)} %get-tuple-element.31.rest_0_), channel_id=1, source_target_pairs={{0,2},{1,15},{2,4},{3,1},{4,6},{5,3},{6,8},{7,5},{8,10},{9,7},{10,... | collective-permute-start | bytes 1179656 | tf_op jit(solution)/shard_map/ppermute | solution.py:451
  11.9 11.3 %copy-start.1 = (bf16[1,2,2,64,384]{4,3,2,1,0:T(8,128)(2,1)S(1)}, bf16[1,2,2,64,384]{4,3,2,1,0:T(8,128)(2,1)}, u32[]{:S(2)}) copy-start(bf16[1,2,2,64,384]{4,3,2,1,0:T(8,128)(2,1)} %param.4) | copy-start | bytes 589828
  11.9 11.3 %copy-start.3 = (bf16[1,2,4,128,192]{3,4,2,1,0:T(8,128)(2,1)S(1)}, bf16[1,2,4,128,192]{3,4,2,1,0:T(8,128)(2,1)}, u32[]{:S(2)}) copy-start(bf16[1,2,4,128,192]{3,4,2,1,0:T(8,128)(2,1)} %param.7) | copy-start | bytes 1179652
  11.9 11.3 %copy-start.4 = (bf16[3,3,384,192]{2,3,1,0:T(8,128)(2,1)S(1)}, bf16[3,3,384,192]{2,3,1,0:T(8,128)(2,1)}, u32[]{:S(2)}) copy-start(bf16[3,3,384,192]{2,3,1,0:T(8,128)(2,1)} %param.6) | copy-start | bytes 3981316
  11.9 7.7 %collective-permute-start.3 = (bf16[6,64,384]{2,1,0:T(8,128)(2,1)S(1)}, bf16[6,64,384]{2,1,0:T(8,128)(2,1)S(1)}, u32[]{:S(2)}, u32[]{:S(2)}) collective-permute-start(bf16[6,64,384]{2,1,0:T(8,128)(2,1)S(1)} %get-tuple-element.37), channel_id=1, source_target_pairs={{0,15},{1,2},{2,1},{3,4},{4,3},{5,6},{6,5},{7,8},{8,7},{9,10},{10,... | collective-permute-start | bytes 884744 | tf_op jit(solution)/shard_map/ppermute | solution.py:448
  12.7 6.9 %collective-permute-start.4 = (bf16[6,64,384]{2,1,0:T(8,128)(2,1)S(1)}, bf16[6,64,384]{2,1,0:T(8,128)(2,1)S(1)}, u32[]{:S(2)}, u32[]{:S(2)}) collective-permute-start(bf16[6,64,384]{2,1,0:T(8,128)(2,1)S(1)} %get-tuple-element.38), channel_id=1, source_target_pairs={{0,1},{1,0},{2,3},{3,2},{4,5},{5,4},{6,7},{7,6},{8,9},{9,8},{10,11... | collective-permute-start | bytes 884744 | tf_op jit(solution)/shard_map/ppermute | solution.py:445
  19.6 16.3 %collective-permute-start.10 = (bf16[2,2,2,64,384]{4,3,2,1,0:T(8,128)(2,1)S(1)}, bf16[2,2,2,64,384]{4,3,2,1,0:T(8,128)(2,1)}, u32[]{:S(2)}, u32[]{:S(2)}) collective-permute-start(bf16[2,2,2,64,384]{4,3,2,1,0:T(8,128)(2,1)S(1)} %collective-permute-done.2.rest_1_), channel_id=1, source_target_pairs={{0,2},{1,15},{2,4},{3,1},{4,6},{5,3},{6,8},{7,5},{8,10},{9,7},{10,... | collective-permute-start | bytes 1179656 | tf_op jit(solution)/shard_map/ppermute | solution.py:451
  29.0 11.7 %collective-permute-start.9 = (bf16[256,864]{1,0:T(8,128)(2,1)S(1)}, bf16[256,864]{1,0:T(8,128)(2,1)S(1)}, u32[]{:S(2)}, u32[]{:S(2)}) collective-permute-start(bf16[256,864]{1,0:T(8,128)(2,1)S(1)} %get-tuple-element.49), channel_id=1, source_target_pairs={{0,1},{1,0},{2,3},{3,2},{4,5},{5,4},{6,7},{7,6},{8,9},{9,8},{10,11... | collective-permute-start | bytes 1327112 | tf_op jit(solution)/shard_map/ppermute | solution.py:445
  29.1 6.8 %collective-permute-start.5 = (bf16[2,2,64,384]{3,2,1,0:T(8,128)(2,1)S(1)}, bf16[2,2,64,384]{3,2,1,0:T(8,128)(2,1)S(1)}, u32[]{:S(2)}, u32[]{:S(2)}) collective-permute-start(bf16[2,2,64,384]{3,2,1,0:T(8,128)(2,1)S(1)} %get-tuple-element.42.own), channel_id=1, source_target_pairs={{16,0},{32,16},{48,32},{0,48},{17,1},{33,17},{49,33},{1,49},{18,2}... | collective-permute-start | bytes 589832 | tf_op jit(solution)/shard_map/ppermute | solution.py:467
  30.6 15.9 %all-to-all-start = ((bf16[16,24,256]{2,1,0:T(8,128)(2,1)}), bf16[16,24,256]{2,1,0:T(8,128)(2,1)S(1)}, u32[]{:S(2)}, u32[]{:S(2)}) async-start(bf16[16,24,256]{2,1,0:T(8,128)(2,1)} %get-tuple-element.46), calls=%async_computation | async-start | bytes 393216 | tf_op jit(solution)/shard_map/all_to_all | solution.py:468
  35.9 19.9 %collective-permute-start.11 = (bf16[2,2,2,64,384]{4,3,2,1,0:T(8,128)(2,1)}, bf16[2,2,2,64,384]{4,3,2,1,0:T(8,128)(2,1)}, u32[]{:S(2)}, u32[]{:S(2)}) collective-permute-start(bf16[2,2,2,64,384]{4,3,2,1,0:T(8,128)(2,1)} %collective-permute-done.10.rest_2_), channel_id=1, source_target_pairs={{0,2},{1,15},{2,4},{3,1},{4,6},{5,3},{6,8},{7,5},{8,10},{9,7},{10,... | collective-permute-start | bytes 1179656 | tf_op jit(solution)/shard_map/ppermute | solution.py:451
  38.6 1.7 %collective-permute-start.8 = (bf16[384,256]{1,0:T(8,128)(2,1)S(1)}, bf16[384,256]{1,0:T(8,128)(2,1)S(1)}, u32[]{:S(2)}, u32[]{:S(2)}) collective-permute-start(bf16[384,256]{1,0:T(8,128)(2,1)S(1)} %get-tuple-element.47.ht), channel_id=1, source_target_pairs={{0,1},{1,0},{2,3},{3,2},{4,5},{5,4},{6,7},{7,6},{8,9},{9,8},{10,11... | collective-permute-start | bytes 589832 | tf_op jit(solution)/shard_map/ppermute | solution.py:445
  38.6 21.2 %collective-permute-start.13 = (bf16[2,2,2,64,384]{4,3,2,1,0:T(8,128)(2,1)S(1)}, bf16[2,2,2,64,384]{4,3,2,1,0:T(8,128)(2,1)}, u32[]{:S(2)}, u32[]{:S(2)}) collective-permute-start(bf16[2,2,2,64,384]{4,3,2,1,0:T(8,128)(2,1)S(1)} %collective-permute-done.2.rest_1_), channel_id=1, source_target_pairs={{0,1},{1,0},{2,3},{3,2},{4,5},{5,4},{6,7},{7,6},{8,9},{9,8},{10,11... | collective-permute-start | bytes 1179656 | tf_op jit(solution)/shard_map/ppermute | solution.py:445
  39.1 20.7 %collective-permute-start.14 = (bf16[2,2,2,64,384]{4,3,2,1,0:T(8,128)(2,1)}, bf16[2,2,2,64,384]{4,3,2,1,0:T(8,128)(2,1)}, u32[]{:S(2)}, u32[]{:S(2)}) collective-permute-start(bf16[2,2,2,64,384]{4,3,2,1,0:T(8,128)(2,1)} %collective-permute-done.10.rest_2_), channel_id=1, source_target_pairs={{0,1},{1,0},{2,3},{3,2},{4,5},{5,4},{6,7},{7,6},{8,9},{9,8},{10,11... | collective-permute-start | bytes 1179656 | tf_op jit(solution)/shard_map/ppermute | solution.py:445
  40.3 15.7 %collective-permute-start.6 = (bf16[4,64,384]{2,1,0:T(8,128)(2,1)}, bf16[4,64,384]{2,1,0:T(8,128)(2,1)S(1)}, u32[]{:S(2)}, u32[]{:S(2)}) collective-permute-start(bf16[4,64,384]{2,1,0:T(8,128)(2,1)} %get-tuple-element.43), channel_id=1, source_target_pairs={{0,15},{1,2},{2,1},{3,4},{4,3},{5,6},{6,5},{7,8},{8,7},{9,10},{10,... | collective-permute-start | bytes 589832 | tf_op jit(solution)/shard_map/ppermute | solution.py:448
  40.8 15.2 %collective-permute-start.7 = (bf16[4,64,384]{2,1,0:T(8,128)(2,1)}, bf16[4,64,384]{2,1,0:T(8,128)(2,1)S(1)}, u32[]{:S(2)}, u32[]{:S(2)}) collective-permute-start(bf16[4,64,384]{2,1,0:T(8,128)(2,1)} %get-tuple-element.44), channel_id=1, source_target_pairs={{0,1},{1,0},{2,3},{3,2},{4,5},{5,4},{6,7},{7,6},{8,9},{9,8},{10,11... | collective-permute-start | bytes 589832 | tf_op jit(solution)/shard_map/ppermute | solution.py:445
  47.9 18.7 %all-to-all-start.2 = ((bf16[16,24,864]{2,1,0:T(8,128)(2,1)}), bf16[16,24,864]{2,1,0:T(8,128)(2,1)S(1)}, u32[]{:S(2)}, u32[]{:S(2)}) async-start(bf16[16,24,864]{2,1,0:T(8,128)(2,1)} %two_part.1), calls=%async_computation.2 | async-start | bytes 1376256 | tf_op jit(solution)/shard_map/all_to_all | solution.py:478
  55.8 15.6 %collective-permute-start.15 = (bf16[2,2,2,64,384]{4,3,2,1,0:T(8,128)(2,1)}, bf16[2,2,2,64,384]{4,3,2,1,0:T(8,128)(2,1)S(1)}, u32[]{:S(2)}, u32[]{:S(2)}) collective-permute-start(bf16[2,2,2,64,384]{4,3,2,1,0:T(8,128)(2,1)} %collective-permute-done.11.rest_3_), channel_id=1, source_target_pairs={{0,2},{1,15},{2,4},{3,1},{4,6},{5,3},{6,8},{7,5},{8,10},{9,7},{10,... | collective-permute-start | bytes 1179656 | tf_op jit(solution)/shard_map/ppermute | solution.py:451
  59.8 11.7 %collective-permute-start.16 = (bf16[2,2,2,64,384]{4,3,2,1,0:T(8,128)(2,1)}, bf16[2,2,2,64,384]{4,3,2,1,0:T(8,128)(2,1)S(1)}, u32[]{:S(2)}, u32[]{:S(2)}) collective-permute-start(bf16[2,2,2,64,384]{4,3,2,1,0:T(8,128)(2,1)} %collective-permute-done.11.rest_3_), channel_id=1, source_target_pairs={{0,1},{1,0},{2,3},{3,2},{4,5},{5,4},{6,7},{7,6},{8,9},{9,8},{10,11... | collective-permute-start | bytes 1179656 | tf_op jit(solution)/shard_map/ppermute | solution.py:445
  60.0 11.5 %collective-permute-start.12 = (bf16[16,24,256]{2,1,0:T(8,128)(2,1)S(1)}, bf16[16,24,256]{2,1,0:T(8,128)(2,1)S(1)}, u32[]{:S(2)}, u32[]{:S(2)}) collective-permute-start(bf16[16,24,256]{2,1,0:T(8,128)(2,1)S(1)} %all-to-all-done.g_in), channel_id=1, source_target_pairs={{16,0},{32,16},{48,32},{0,48},{17,1},{33,17},{49,33},{1,49},{18,2}... | collective-permute-start | bytes 589832 | tf_op jit(solution)/shard_map/ppermute | solution.py:474
  67.6 12.4 %all-to-all-start.3 = ((bf16[16,24,128]{2,1,0:T(8,128)(2,1)}), bf16[16,24,128]{2,1,0:T(8,128)(2,1)S(1)}, u32[]{:S(2)}, u32[]{:S(2)}) async-start(bf16[16,24,128]{2,1,0:T(8,128)(2,1)} %two_mid.1), calls=%async_computation.3 | async-start | bytes 196608 | tf_op jit(solution)/shard_map/all_to_all | solution.py:488
  80.0 16.1 %all-to-all-start.1 = ((bf16[16,24,768]{2,1,0:T(8,128)(2,1)}), bf16[16,24,768]{2,1,0:T(8,128)(2,1)S(1)}, u32[]{:S(2)}, u32[]{:S(2)}) async-start(bf16[16,24,768]{2,1,0:T(8,128)(2,1)} %one_part.1), calls=%async_computation.1 | async-start | bytes 1179648 | tf_op jit(solution)/shard_map/all_to_all | solution.py:487

commit v4 on v3

--- a/solution.py
+++ b/solution.py
@@ -466,26 +466,27 @@
 
     gp_next = lax.ppermute(gp, "frame", prev_perm)
     g = lax.all_to_all(gpt, "height", 0, 0, tiled=True)
-    pair2, _ = lax.optimization_barrier((pair2, gp_next))
+    ht_other, given = inside(ht), inside(give)
+    gp_next, pair2 = lax.optimization_barrier((gp_next, pair2))
+    g_next = lax.ppermute(g, "frame", prev_perm)
+    ht, pair2, gp_next, _ = lax.optimization_barrier((ht, pair2, gp_next, g))
+    two = two_part(ht, keep, ht_other, given)
+    pair2, _ = lax.optimization_barrier((pair2, two))
     pair3 = ring(pair2)
-    ht_other, given = inside(ht), inside(give)
+    two = lax.all_to_all(two, ("dp", "frame"), 0, 0, tiled=True)
+    far1, far2 = inside(pair1), inside(pair2)
+    pair3, gp_next, far1, far2 = lax.optimization_barrier((pair3, gp_next, far1, far2))
+    pair4, far3 = ring(pair3), inside(pair3)
     cross, inner = rows(gp, gp_next)
     cross, inner = across(cross), inside(inner)
-    g_next = lax.ppermute(g, "frame", prev_perm)
-    ht, _, _ = lax.optimization_barrier((ht, gp_next, g))
-    two = two_part(ht, keep, ht_other, given)
-    w1, two = lax.optimization_barrier((w1, two))
-    two = lax.all_to_all(two, ("dp", "frame"), 0, 0, tiled=True)
-    w1, pair3 = lax.optimization_barrier((load(w1), pair3))
-    pair4 = ring(pair3)
-    grad_in = latents_grad(gp, gp_next, cross, inner, w1)
-    far1, far2 = inside(pair1), inside(pair2)
-    pair3, far1, far2, _ = lax.optimization_barrier((pair3, far1, far2, grad_in))
-    blocks = (pair0, pair1, pair2, pair3, pair4, far1, far2, inside(pair3))
+    two, far3 = lax.optimization_barrier((two, far3))
+    two = lax.all_to_all(two_mid(two), "height", 0, 0, tiled=True)
+    blocks = (pair0, pair1, pair2, pair3, pair4, far1, far2, far3)
 
     one = one_part(g, g_next, blocks)
+    one, w1, cross, inner = lax.optimization_barrier((one, w1, cross, inner))
     one = lax.all_to_all(one, ("dp", "frame"), 0, 0, tiled=True)
-    two = lax.all_to_all(two_mid(two), "height", 0, 0, tiled=True)
+    grad_in = latents_grad(gp, gp_next, cross, inner, load(w1))
     one = final_one(one).reshape(3, 3, 3, 24, 24)
     two = jnp.swapaxes(final_two(two).reshape(3, 3, 12, 24), 2, 3)
     return (grad_in[None], one, two)

time: 97.5 us -> 98.9 us (1.014)
  starting transfers between devices: 42 us -> 45.8 us
  waiting for transfers between devices: 24.7 us -> 22.2 us
    all_to_all x1, waiting for transfers between devices: 11.8 us -> 4.69 us  [local(): one = lax.all_to_all(one, ('dp', 'frame'), 0, 0, tiled=True)]
    ppermute x1, waiting for transfers between devices: 0.01 us -> 3.76 us  [local(): gp_next = lax.ppermute(gp, 'frame', prev_perm)]
    ppermute x4, starting transfers between devices: 10.3 us -> 6.92 us  [ring(): return lax.ppermute(value, 'height', ring_perm)]
    all_to_all x1, starting transfers between devices: 3.92 us -> 6.84 us  [local(): two = lax.all_to_all(two_mid(two), 'height', 0, 0, tiled=True)]
    ppermute x8, starting transfers between devices: 8.83 us -> 11.6 us  [inside(): return lax.ppermute(value, 'height', inner_perm)]
    all_to_all x1, starting transfers between devices: 4.53 us -> 6.9 us  [local(): two = lax.all_to_all(two, ('dp', 'frame'), 0, 0, tiled=True)]
    all_to_all x1, waiting for transfers between devices: 3.77 us -> 5.47 us  [local(): two = lax.all_to_all(two, ('dp', 'frame'), 0, 0, tiled=True)]
  transfers between devices with their start and end apart: 21 -> 21, of which waited for: 7 -> 8; matrix products, arithmetic and copies ran while one was open for 0% -> 0% of each run, Pallas kernels for 27% -> 21%
where the time goes in v4:
time: 98.9 us; the launch traced here: 98.3 us
  starting transfers between devices  45.8 us (46%)
  Pallas kernels  27.6 us (28%)
  waiting for transfers between devices  22.2 us (22%)
  local copies, waits for them, and re-layouts  1.94 us (2%)
    ppermute x8, starting transfers between devices, inside(): return lax.ppermute(value, 'height', inner_perm)  11.6 us
    ppermute x4, starting transfers between devices, ring(): return lax.ppermute(value, 'height', ring_perm)  6.92 us
    all_to_all x1, starting transfers between devices, local(): two = lax.all_to_all(two, ('dp', 'frame'), 0, 0, tiled=True)  6.9 us
    all_to_all x1, starting transfers between devices, local(): two = lax.all_to_all(two_mid(two), 'height', 0, 0, tiled=True)  6.84 us
    pallas_call x2, Pallas kernels, load(): pl.pallas_call(load_kernel, in_specs=anywhere(1), out_specs=vmem(1)[0], o...  6.7 us
    pallas_call x1, Pallas kernels, one_part(): pl.pallas_call(one_kernel, in_specs=anywhere(10), out_specs=vmem(1)[0], o...  6.42 us
    pallas_call x1, Pallas kernels, forward(): pl.pallas_call(forward_kernel, in_specs=vmem(5) + anywhere(1) + vmem(1),...  5.79 us
    all_to_all x1, waiting for transfers between devices, local(): two = lax.all_to_all(two, ('dp', 'frame'), 0, 0, tiled=True)  5.47 us
  transfers between devices with their start and end apart: 21, of which 8 were waited for; matrix products, arithmetic and copies ran while one was open for 0% of the time, Pallas kernels for 21%

profile of v4, /device:TPU:1, one launch (start us, length us, event | category | flops | bytes accessed | tf_op | source)
XLA Modules:
  0.0 98.3 jit_solution(4649288473422472233)
XLA Ops:
  0.6 3.3 %collective-permute-start.1 = (bf16[2,2,64,384]{3,2,1,0:T(8,128)(2,1)}, bf16[2,2,64,384]{3,2,1,0:T(8,128)(2,1)S(1)}, u32[]{:S(2)}, u32[]{:S(2)}) collective-permute-start(bf16[2,2,64,384]{3,2,1,0:T(8,128)(2,1)} %bitcast.13), channel_id=1, source_target_pairs={{0,1},{1,0},{2,3},{3,2},{4,5},{5,4},{6,7},{7,6},{8,9},{9,8},{10,11... | collective-permute-start | bytes 589832 | tf_op jit(solution)/shard_map/ppermute | solution.py:445
  4.0 1.3 %collective-permute-done.1.other = bf16[2,2,64,384]{3,2,1,0:T(8,128)(2,1)S(1)} collective-permute-done((bf16[2,2,64,384]{3,2,1,0:T(8,128)(2,1)}, bf16[2,2,64,384]{3,2,1,0:T(8,128)(2,1)S(1)}, u32[]{:S(2)}, u32[]{:S(2)}) %collective-permute-start.1) | collective-permute-done | bytes 196640 | tf_op jit(solution)/shard_map/ppermute | solution.py:445
  5.2 0.9 copy-done
  6.2 1.0 %copy-done.2 = bf16[1,2,4,128,192]{3,4,2,1,0:T(8,128)(2,1)S(1)} copy-done((bf16[1,2,4,128,192]{3,4,2,1,0:T(8,128)(2,1)S(1)}, bf16[1,2,4,128,192]{3,4,2,1,0:T(8,128)(2,1)}, u32[]{:S(2)}) %copy-start.2) | copy-done | bytes 393240
  7.2 0.1 pair.1
  7.2 3.9 %collective-permute-start.2 = (bf16[2,2,2,64,384]{4,3,2,1,0:T(8,128)(2,1)S(1)}, bf16[2,2,2,64,384]{4,3,2,1,0:T(8,128)(2,1)S(1)}, u32[]{:S(2)}, u32[]{:S(2)}) collective-permute-start(bf16[2,2,2,64,384]{4,3,2,1,0:T(8,128)(2,1)S(1)} %get-tuple-element.38.rest_0_), channel_id=1, source_target_pairs={{0,2},{1,15},{2,4},{3,1},{4,6},{5,3},{6,8},{7,5},{8,10},{9,7},{10,... | collective-permute-start | bytes 1179656 | tf_op jit(solution)/shard_map/ppermute | solution.py:451
  11.2 0.7 collective-permute-done.prev
  11.8 0.1 edges.1
  11.9 0.0 copy-start.1
  11.9 0.0 copy-start.3
  11.9 0.0 copy-start.4
  11.9 0.7 collective-permute-start.3
  12.7 3.6 %collective-permute-start.4 = (bf16[6,64,384]{2,1,0:T(8,128)(2,1)S(1)}, bf16[6,64,384]{2,1,0:T(8,128)(2,1)S(1)}, u32[]{:S(2)}, u32[]{:S(2)}) collective-permute-start(bf16[6,64,384]{2,1,0:T(8,128)(2,1)S(1)} %get-tuple-element.45), channel_id=1, source_target_pairs={{0,1},{1,0},{2,3},{3,2},{4,5},{5,4},{6,7},{7,6},{8,9},{9,8},{10,11... | collective-permute-start | bytes 884744 | tf_op jit(solution)/shard_map/ppermute | solution.py:445
  16.3 3.3 %load.2.wv = bf16[27,384,384]{2,1,0:T(8,128)(2,1)S(1)} custom-call(bf16[27,384,384]{2,1,0:T(8,128)(2,1)} %bitcast.21), custom_call_target="tpu_custom_call" | custom-call | flops 2000 | bytes 16000000 | tf_op jit(solution)/shard_map/load/pallas_call | solution.py:86
  19.6 0.0 collective-permute-done.3.cross
  19.6 0.0 collective-permute-done.4.inner
  19.7 5.8 %forward.1 = (bf16[2,2,64,384]{3,2,1,0:T(8,128)(2,1)S(1)}, bf16[16,24,256]{2,1,0:T(8,128)(2,1)}, bf16[384,256]{1,0:T(8,128)(2,1)S(1)}, bf16[256,864]{1,0:T(8,128)(2,1)S(1)}, bf16[256,864]{1,0:T(8,128)(2,1)S(1)}) custom-call(bf16[2,2,64,384]{3,2,1,0:T(8,128)(2,1)S(1)} %bitcast.17, bf16[2,2,64,384]{3,2,1,0:T(8,128)(2,1)S(1)} %collective-permute-done.prev, ...), custom_call_target="tpu_custom_call" | custom-call | flops 2600000000 | bytes 12000000 | tf_op jit(solution)/shard_map/forward/pallas_call | solution.py:209
  25.5 1.2 %collective-permute-start.8 = (bf16[256,864]{1,0:T(8,128)(2,1)S(1)}, bf16[256,864]{1,0:T(8,128)(2,1)S(1)}, u32[]{:S(2)}, u32[]{:S(2)}) collective-permute-start(bf16[256,864]{1,0:T(8,128)(2,1)S(1)} %get-tuple-element.58), channel_id=1, source_target_pairs={{0,1},{1,0},{2,3},{3,2},{4,5},{5,4},{6,7},{7,6},{8,9},{9,8},{10,11... | collective-permute-start | bytes 1327112 | tf_op jit(solution)/shard_map/ppermute | solution.py:445
  26.7 2.6 %collective-permute-start.6 = (bf16[2,2,2,64,384]{4,3,2,1,0:T(8,128)(2,1)S(1)}, bf16[2,2,2,64,384]{4,3,2,1,0:T(8,128)(2,1)}, u32[]{:S(2)}, u32[]{:S(2)}) collective-permute-start(bf16[2,2,2,64,384]{4,3,2,1,0:T(8,128)(2,1)S(1)} %collective-permute-done.2.rest_1_), channel_id=1, source_target_pairs={{0,2},{1,15},{2,4},{3,1},{4,6},{5,3},{6,8},{7,5},{8,10},{9,7},{10,... | collective-permute-start | bytes 1179656 | tf_op jit(solution)/shard_map/ppermute | solution.py:451
  29.2 4.3 %all-to-all-start = ((bf16[16,24,256]{2,1,0:T(8,128)(2,1)}), bf16[16,24,256]{2,1,0:T(8,128)(2,1)S(1)}, u32[]{:S(2)}, u32[]{:S(2)}) async-start(bf16[16,24,256]{2,1,0:T(8,128)(2,1)} %get-tuple-element.54), calls=%async_computation | async-start | bytes 393216 | tf_op jit(solution)/shard_map/all_to_all | solution.py:468
  33.6 2.1 %collective-permute-start.5 = (bf16[2,2,64,384]{3,2,1,0:T(8,128)(2,1)S(1)}, bf16[2,2,64,384]{3,2,1,0:T(8,128)(2,1)S(1)}, u32[]{:S(2)}, u32[]{:S(2)}) collective-permute-start(bf16[2,2,64,384]{3,2,1,0:T(8,128)(2,1)S(1)} %get-tuple-element.49.own), channel_id=1, source_target_pairs={{16,0},{32,16},{48,32},{0,48},{17,1},{33,17},{49,33},{1,49},{18,2}... | collective-permute-start | bytes 589832 | tf_op jit(solution)/shard_map/ppermute | solution.py:467
  35.6 0.5 collective-permute-start.7
  36.1 0.1 collective-permute-start.10
  36.1 3.8 %collective-permute-done.5.after = bf16[2,2,64,384]{3,2,1,0:T(8,128)(2,1)S(1)} collective-permute-done((bf16[2,2,64,384]{3,2,1,0:T(8,128)(2,1)S(1)}, bf16[2,2,64,384]{3,2,1,0:T(8,128)(2,1)S(1)}, u32[]{:S(2)}, u32[]{:S(2)}) %collective-permute-start.5) | collective-permute-done | bytes 196640 | tf_op jit(solution)/shard_map/ppermute | solution.py:467
  39.9 4.0 %all-to-all-done.g_in = bf16[16,24,256]{2,1,0:T(8,128)(2,1)S(1)} async-done(((bf16[16,24,256]{2,1,0:T(8,128)(2,1)}), bf16[16,24,256]{2,1,0:T(8,128)(2,1)S(1)}, u32[]{:S(2)}, u32[]{:S(2)}) %all-to-all-start) | async-done | bytes 196640 | tf_op jit(solution)/shard_map/all_to_all | solution.py:468
  43.9 0.0 collective-permute-done.7.ht_other
  43.9 0.0 collective-permute-done.8.given
  43.9 1.4 %two_part.1 = bf16[16,24,864]{2,1,0:T(8,128)(2,1)} custom-call(bf16[384,256]{1,0:T(8,128)(2,1)S(1)} %get-tuple-element.56.ht, bf16[256,864]{1,0:T(8,128)(2,1)S(1)} %get-tuple-element.57.keep, bf16[384,256]{1,0:T(8,128)(2,1)S(1)} %collective-permute-done.7.ht_other, bf16[256,864]{1,0:T(8,128)(2,1)S(1)} %collective-permute-done.8.given), custom_call_target="tpu_custom_call" | custom-call | flops 340000000 | bytes 3000000 | tf_op jit(solution)/shard_map/two_part/pallas_call | solution.py:261
  45.3 0.0 collective-permute-start.11
  45.3 0.0 collective-permute-start.9
  45.3 6.9 %all-to-all-start.1 = ((bf16[16,24,864]{2,1,0:T(8,128)(2,1)}), bf16[16,24,864]{2,1,0:T(8,128)(2,1)S(1)}, u32[]{:S(2)}, u32[]{:S(2)}) async-start(bf16[16,24,864]{2,1,0:T(8,128)(2,1)} %two_part.1), calls=%async_computation.1 | async-start | bytes 1376256 | tf_op jit(solution)/shard_map/all_to_all | solution.py:476
  52.3 0.3 collective-permute-done.9.rest_3_
  52.6 2.6 %collective-permute-start.14 = (bf16[2,2,2,64,384]{4,3,2,1,0:T(8,128)(2,1)}, bf16[2,2,2,64,384]{4,3,2,1,0:T(8,128)(2,1)}, u32[]{:S(2)}, u32[]{:S(2)}) collective-permute-start(bf16[2,2,2,64,384]{4,3,2,1,0:T(8,128)(2,1)} %collective-permute-done.9.rest_3_), channel_id=1, source_target_pairs={{0,1},{1,0},{2,3},{3,2},{4,5},{5,4},{6,7},{7,6},{8,9},{9,8},{10,11... | collective-permute-start | bytes 1179656 | tf_op jit(solution)/shard_map/ppermute | solution.py:445
  55.2 0.4 collective-permute-start.13
  55.6 2.9 %collective-permute-start.12 = (bf16[16,24,256]{2,1,0:T(8,128)(2,1)S(1)}, bf16[16,24,256]{2,1,0:T(8,128)(2,1)S(1)}, u32[]{:S(2)}, u32[]{:S(2)}) collective-permute-start(bf16[16,24,256]{2,1,0:T(8,128)(2,1)S(1)} %all-to-all-done.g_in), channel_id=1, source_target_pairs={{16,0},{32,16},{48,32},{0,48},{17,1},{33,17},{49,33},{1,49},{18,2}... | collective-permute-start | bytes 589832 | tf_op jit(solution)/shard_map/ppermute | solution.py:471
  58.4 0.7 rows.1
  59.1 0.4 collective-permute-start.16
  59.5 5.5 %all-to-all-done.1.parts = bf16[16,24,864]{2,1,0:T(8,128)(2,1)S(1)} async-done(((bf16[16,24,864]{2,1,0:T(8,128)(2,1)}), bf16[16,24,864]{2,1,0:T(8,128)(2,1)S(1)}, u32[]{:S(2)}, u32[]{:S(2)}) %all-to-all-start.1) | async-done | bytes 663584 | tf_op jit(solution)/shard_map/all_to_all | solution.py:476
  65.0 0.9 two_mid.1
  65.9 6.8 %all-to-all-start.3 = ((bf16[16,24,128]{2,1,0:T(8,128)(2,1)}), bf16[16,24,128]{2,1,0:T(8,128)(2,1)S(1)}, u32[]{:S(2)}, u32[]{:S(2)}) async-start(bf16[16,24,128]{2,1,0:T(8,128)(2,1)} %two_mid.1), calls=%async_computation.3 | async-start | bytes 196608 | tf_op jit(solution)/shard_map/all_to_all | solution.py:483
  72.8 6.4 %one_part.1 = bf16[16,24,768]{2,1,0:T(8,128)(2,1)} custom-call(bf16[16,24,256]{2,1,0:T(8,128)(2,1)S(1)} %all-to-all-done.g_in, bf16[16,24,256]{2,1,0:T(8,128)(2,1)S(1)} %collective-permute-done.12.g_after_in, bf16[2,2,2,64,384]{4,3,2,1,0:T(8,128)(2,1)S(1)} %get-tuple-element.38.rest_0_, bf16[2,2,2,64,384]{4,3,2,1,0:T(8,128)(2,1)S(1)} %collective-permute-done.2.rest_1_, ...), custom_call_target="tpu_custom_call" | custom-call | flops 2040000000 | bytes 5000000 | tf_op jit(solution)/shard_map/one_part/pallas_call | solution.py:353
  79.2 2.0 %all-to-all-done.3.parts = bf16[16,24,128]{2,1,0:T(8,128)(2,1)S(1)} async-done(((bf16[16,24,128]{2,1,0:T(8,128)(2,1)}), bf16[16,24,128]{2,1,0:T(8,128)(2,1)S(1)}, u32[]{:S(2)}, u32[]{:S(2)}) %all-to-all-start.3) | async-done | bytes 98336 | tf_op jit(solution)/shard_map/all_to_all | solution.py:483
  81.2 3.6 %all-to-all-start.2 = ((bf16[16,24,768]{2,1,0:T(8,128)(2,1)}), bf16[16,24,768]{2,1,0:T(8,128)(2,1)S(1)}, u32[]{:S(2)}, u32[]{:S(2)}) async-start(bf16[16,24,768]{2,1,0:T(8,128)(2,1)} %one_part.1), calls=%async_computation.2 | async-start | bytes 1179648 | tf_op jit(solution)/shard_map/all_to_all | solution.py:488
  84.8 3.4 %load.3.wv = bf16[27,384,384]{2,1,0:T(8,128)(2,1)S(1)} custom-call(bf16[27,384,384]{2,1,0:T(8,128)(2,1)} %bitcast.22), custom_call_target="tpu_custom_call" | custom-call | flops 2000 | bytes 16000000 | tf_op jit(solution)/shard_map/load/pallas_call | solution.py:86
  88.2 3.8 %latents_grad.1 = bf16[2,2,64,384]{3,2,1,0:T(8,128)(2,1)} custom-call(bf16[2,2,64,384]{3,2,1,0:T(8,128)(2,1)S(1)} %get-tuple-element.49.own, bf16[2,2,64,384]{3,2,1,0:T(8,128)(2,1)S(1)} %collective-permute-done.5.after, bf16[4,64,384]{2,1,0:T(8,128)(2,1)S(1)} %collective-permute-done.15.cross, bf16[4,64,384]{2,1,0:T(8,128)(2,1)S(1)} %collective-permute-done.16.inner, ...), custom_call_target="tpu_custom_call" | custom-call | flops 2040000000 | bytes 10000000 | tf_op jit(solution)/shard_map/latents_grad/pallas_call | solution.py:287
  92.0 0.7 final_two.1
  92.7 4.7 %all-to-all-done.2.parts = bf16[16,24,768]{2,1,0:T(8,128)(2,1)S(1)} async-done(((bf16[16,24,768]{2,1,0:T(8,128)(2,1)}), bf16[16,24,768]{2,1,0:T(8,128)(2,1)S(1)}, u32[]{:S(2)}, u32[]{:S(2)}) %all-to-all-start.2) | async-done | bytes 589856 | tf_op jit(solution)/shard_map/all_to_all | solution.py:488
  97.4 0.9 final_one.1
  (16 shorter events, 0.0 us)
Async XLA Ops:
  0.6 4.6 %collective-permute-start.1 = (bf16[2,2,64,384]{3,2,1,0:T(8,128)(2,1)}, bf16[2,2,64,384]{3,2,1,0:T(8,128)(2,1)S(1)}, u32[]{:S(2)}, u32[]{:S(2)}) collective-permute-start(bf16[2,2,64,384]{3,2,1,0:T(8,128)(2,1)} %bitcast.13), channel_id=1, source_target_pairs={{0,1},{1,0},{2,3},{3,2},{4,5},{5,4},{6,7},{7,6},{8,9},{9,8},{10,11... | collective-permute-start | bytes 589832 | tf_op jit(solution)/shard_map/ppermute | solution.py:445
  4.0 7.9 %collective-permute-start = (bf16[2,2,64,384]{3,2,1,0:T(8,128)(2,1)}, bf16[2,2,64,384]{3,2,1,0:T(8,128)(2,1)S(1)}, u32[]{:S(2)}, u32[]{:S(2)}) collective-permute-start(bf16[2,2,64,384]{3,2,1,0:T(8,128)(2,1)} %bitcast.14), channel_id=1, source_target_pairs={{0,16},{16,32},{32,48},{48,0},{1,17},{17,33},{33,49},{49,1},{2,18}... | collective-permute-start | bytes 589832 | tf_op jit(solution)/shard_map/ppermute | solution.py:456
  5.2 0.9 copy-start
  6.2 1.0 %copy-start.2 = (bf16[1,2,4,128,192]{3,4,2,1,0:T(8,128)(2,1)S(1)}, bf16[1,2,4,128,192]{3,4,2,1,0:T(8,128)(2,1)}, u32[]{:S(2)}) copy-start(bf16[1,2,4,128,192]{3,4,2,1,0:T(8,128)(2,1)} %param.7) | copy-start | bytes 1179652
  7.2 12.4 %collective-permute-start.2 = (bf16[2,2,2,64,384]{4,3,2,1,0:T(8,128)(2,1)S(1)}, bf16[2,2,2,64,384]{4,3,2,1,0:T(8,128)(2,1)S(1)}, u32[]{:S(2)}, u32[]{:S(2)}) collective-permute-start(bf16[2,2,2,64,384]{4,3,2,1,0:T(8,128)(2,1)S(1)} %get-tuple-element.38.rest_0_), channel_id=1, source_target_pairs={{0,2},{1,15},{2,4},{3,1},{4,6},{5,3},{6,8},{7,5},{8,10},{9,7},{10,... | collective-permute-start | bytes 1179656 | tf_op jit(solution)/shard_map/ppermute | solution.py:451
  11.9 7.7 %copy-start.1 = (bf16[1,2,2,64,384]{4,3,2,1,0:T(8,128)(2,1)S(1)}, bf16[1,2,2,64,384]{4,3,2,1,0:T(8,128)(2,1)}, u32[]{:S(2)}) copy-start(bf16[1,2,2,64,384]{4,3,2,1,0:T(8,128)(2,1)} %param.4) | copy-start | bytes 589828
  11.9 7.7 %copy-start.3 = (bf16[1,2,4,128,192]{3,4,2,1,0:T(8,128)(2,1)S(1)}, bf16[1,2,4,128,192]{3,4,2,1,0:T(8,128)(2,1)}, u32[]{:S(2)}) copy-start(bf16[1,2,4,128,192]{3,4,2,1,0:T(8,128)(2,1)} %param.7) | copy-start | bytes 1179652
  11.9 7.7 %copy-start.4 = (bf16[3,3,384,192]{2,3,1,0:T(8,128)(2,1)S(1)}, bf16[3,3,384,192]{2,3,1,0:T(8,128)(2,1)}, u32[]{:S(2)}) copy-start(bf16[3,3,384,192]{2,3,1,0:T(8,128)(2,1)} %param.6) | copy-start | bytes 3981316
  11.9 7.7 %collective-permute-start.3 = (bf16[6,64,384]{2,1,0:T(8,128)(2,1)S(1)}, bf16[6,64,384]{2,1,0:T(8,128)(2,1)S(1)}, u32[]{:S(2)}, u32[]{:S(2)}) collective-permute-start(bf16[6,64,384]{2,1,0:T(8,128)(2,1)S(1)} %get-tuple-element.44), channel_id=1, source_target_pairs={{0,15},{1,2},{2,1},{3,4},{4,3},{5,6},{6,5},{7,8},{8,7},{9,10},{10,... | collective-permute-start | bytes 884744 | tf_op jit(solution)/shard_map/ppermute | solution.py:448
  12.7 6.9 %collective-permute-start.4 = (bf16[6,64,384]{2,1,0:T(8,128)(2,1)S(1)}, bf16[6,64,384]{2,1,0:T(8,128)(2,1)S(1)}, u32[]{:S(2)}, u32[]{:S(2)}) collective-permute-start(bf16[6,64,384]{2,1,0:T(8,128)(2,1)S(1)} %get-tuple-element.45), channel_id=1, source_target_pairs={{0,1},{1,0},{2,3},{3,2},{4,5},{5,4},{6,7},{7,6},{8,9},{9,8},{10,11... | collective-permute-start | bytes 884744 | tf_op jit(solution)/shard_map/ppermute | solution.py:445
  25.5 18.4 %collective-permute-start.8 = (bf16[256,864]{1,0:T(8,128)(2,1)S(1)}, bf16[256,864]{1,0:T(8,128)(2,1)S(1)}, u32[]{:S(2)}, u32[]{:S(2)}) collective-permute-start(bf16[256,864]{1,0:T(8,128)(2,1)S(1)} %get-tuple-element.58), channel_id=1, source_target_pairs={{0,1},{1,0},{2,3},{3,2},{4,5},{5,4},{6,7},{7,6},{8,9},{9,8},{10,11... | collective-permute-start | bytes 1327112 | tf_op jit(solution)/shard_map/ppermute | solution.py:445
  26.7 13.3 %collective-permute-start.6 = (bf16[2,2,2,64,384]{4,3,2,1,0:T(8,128)(2,1)S(1)}, bf16[2,2,2,64,384]{4,3,2,1,0:T(8,128)(2,1)}, u32[]{:S(2)}, u32[]{:S(2)}) collective-permute-start(bf16[2,2,2,64,384]{4,3,2,1,0:T(8,128)(2,1)S(1)} %collective-permute-done.2.rest_1_), channel_id=1, source_target_pairs={{0,2},{1,15},{2,4},{3,1},{4,6},{5,3},{6,8},{7,5},{8,10},{9,7},{10,... | collective-permute-start | bytes 1179656 | tf_op jit(solution)/shard_map/ppermute | solution.py:451
  29.2 14.7 %all-to-all-start = ((bf16[16,24,256]{2,1,0:T(8,128)(2,1)}), bf16[16,24,256]{2,1,0:T(8,128)(2,1)S(1)}, u32[]{:S(2)}, u32[]{:S(2)}) async-start(bf16[16,24,256]{2,1,0:T(8,128)(2,1)} %get-tuple-element.54), calls=%async_computation | async-start | bytes 393216 | tf_op jit(solution)/shard_map/all_to_all | solution.py:468
  33.6 6.3 %collective-permute-start.5 = (bf16[2,2,64,384]{3,2,1,0:T(8,128)(2,1)S(1)}, bf16[2,2,64,384]{3,2,1,0:T(8,128)(2,1)S(1)}, u32[]{:S(2)}, u32[]{:S(2)}) collective-permute-start(bf16[2,2,64,384]{3,2,1,0:T(8,128)(2,1)S(1)} %get-tuple-element.49.own), channel_id=1, source_target_pairs={{16,0},{32,16},{48,32},{0,48},{17,1},{33,17},{49,33},{1,49},{18,2}... | collective-permute-start | bytes 589832 | tf_op jit(solution)/shard_map/ppermute | solution.py:467
  35.6 8.3 %collective-permute-start.7 = (bf16[384,256]{1,0:T(8,128)(2,1)S(1)}, bf16[384,256]{1,0:T(8,128)(2,1)S(1)}, u32[]{:S(2)}, u32[]{:S(2)}) collective-permute-start(bf16[384,256]{1,0:T(8,128)(2,1)S(1)} %get-tuple-element.56.ht), channel_id=1, source_target_pairs={{0,1},{1,0},{2,3},{3,2},{4,5},{5,4},{6,7},{7,6},{8,9},{9,8},{10,11... | collective-permute-start | bytes 589832 | tf_op jit(solution)/shard_map/ppermute | solution.py:445
  36.1 16.2 %collective-permute-start.10 = (bf16[2,2,2,64,384]{4,3,2,1,0:T(8,128)(2,1)S(1)}, bf16[2,2,2,64,384]{4,3,2,1,0:T(8,128)(2,1)}, u32[]{:S(2)}, u32[]{:S(2)}) collective-permute-start(bf16[2,2,2,64,384]{4,3,2,1,0:T(8,128)(2,1)S(1)} %collective-permute-done.2.rest_1_), channel_id=1, source_target_pairs={{0,1},{1,0},{2,3},{3,2},{4,5},{5,4},{6,7},{7,6},{8,9},{9,8},{10,11... | collective-permute-start | bytes 1179656 | tf_op jit(solution)/shard_map/ppermute | solution.py:445
  45.3 6.9 %collective-permute-start.11 = (bf16[2,2,2,64,384]{4,3,2,1,0:T(8,128)(2,1)}, bf16[2,2,2,64,384]{4,3,2,1,0:T(8,128)(2,1)S(1)}, u32[]{:S(2)}, u32[]{:S(2)}) collective-permute-start(bf16[2,2,2,64,384]{4,3,2,1,0:T(8,128)(2,1)} %collective-permute-done.6.rest_2_), channel_id=1, source_target_pairs={{0,1},{1,0},{2,3},{3,2},{4,5},{5,4},{6,7},{7,6},{8,9},{9,8},{10,11... | collective-permute-start | bytes 1179656 | tf_op jit(solution)/shard_map/ppermute | solution.py:445
  45.3 7.2 %collective-permute-start.9 = (bf16[2,2,2,64,384]{4,3,2,1,0:T(8,128)(2,1)}, bf16[2,2,2,64,384]{4,3,2,1,0:T(8,128)(2,1)}, u32[]{:S(2)}, u32[]{:S(2)}) collective-permute-start(bf16[2,2,2,64,384]{4,3,2,1,0:T(8,128)(2,1)} %collective-permute-done.6.rest_2_), channel_id=1, source_target_pairs={{0,2},{1,15},{2,4},{3,1},{4,6},{5,3},{6,8},{7,5},{8,10},{9,7},{10,... | collective-permute-start | bytes 1179656 | tf_op jit(solution)/shard_map/ppermute | solution.py:451
  45.3 19.7 %all-to-all-start.1 = ((bf16[16,24,864]{2,1,0:T(8,128)(2,1)}), bf16[16,24,864]{2,1,0:T(8,128)(2,1)S(1)}, u32[]{:S(2)}, u32[]{:S(2)}) async-start(bf16[16,24,864]{2,1,0:T(8,128)(2,1)} %two_part.1), calls=%async_computation.1 | async-start | bytes 1376256 | tf_op jit(solution)/shard_map/all_to_all | solution.py:476
  52.6 12.4 %collective-permute-start.14 = (bf16[2,2,2,64,384]{4,3,2,1,0:T(8,128)(2,1)}, bf16[2,2,2,64,384]{4,3,2,1,0:T(8,128)(2,1)}, u32[]{:S(2)}, u32[]{:S(2)}) collective-permute-start(bf16[2,2,2,64,384]{4,3,2,1,0:T(8,128)(2,1)} %collective-permute-done.9.rest_3_), channel_id=1, source_target_pairs={{0,1},{1,0},{2,3},{3,2},{4,5},{5,4},{6,7},{7,6},{8,9},{9,8},{10,11... | collective-permute-start | bytes 1179656 | tf_op jit(solution)/shard_map/ppermute | solution.py:445
  55.2 17.6 %collective-permute-start.13 = (bf16[2,2,2,64,384]{4,3,2,1,0:T(8,128)(2,1)}, bf16[2,2,2,64,384]{4,3,2,1,0:T(8,128)(2,1)}, u32[]{:S(2)}, u32[]{:S(2)}) collective-permute-start(bf16[2,2,2,64,384]{4,3,2,1,0:T(8,128)(2,1)} %collective-permute-done.9.rest_3_), channel_id=1, source_target_pairs={{0,2},{1,15},{2,4},{3,1},{4,6},{5,3},{6,8},{7,5},{8,10},{9,7},{10,... | collective-permute-start | bytes 1179656 | tf_op jit(solution)/shard_map/ppermute | solution.py:451
  55.6 17.2 %collective-permute-start.12 = (bf16[16,24,256]{2,1,0:T(8,128)(2,1)S(1)}, bf16[16,24,256]{2,1,0:T(8,128)(2,1)S(1)}, u32[]{:S(2)}, u32[]{:S(2)}) collective-permute-start(bf16[16,24,256]{2,1,0:T(8,128)(2,1)S(1)} %all-to-all-done.g_in), channel_id=1, source_target_pairs={{16,0},{32,16},{48,32},{0,48},{17,1},{33,17},{49,33},{1,49},{18,2}... | collective-permute-start | bytes 589832 | tf_op jit(solution)/shard_map/ppermute | solution.py:471
  59.1 20.1 %collective-permute-start.15 = (bf16[4,64,384]{2,1,0:T(8,128)(2,1)}, bf16[4,64,384]{2,1,0:T(8,128)(2,1)S(1)}, u32[]{:S(2)}, u32[]{:S(2)}) collective-permute-start(bf16[4,64,384]{2,1,0:T(8,128)(2,1)} %get-tuple-element.66), channel_id=1, source_target_pairs={{0,15},{1,2},{2,1},{3,4},{4,3},{5,6},{6,5},{7,8},{8,7},{9,10},{10,... | collective-permute-start | bytes 589832 | tf_op jit(solution)/shard_map/ppermute | solution.py:448
  59.1 20.1 %collective-permute-start.16 = (bf16[4,64,384]{2,1,0:T(8,128)(2,1)S(1)}, bf16[4,64,384]{2,1,0:T(8,128)(2,1)S(1)}, u32[]{:S(2)}, u32[]{:S(2)}) collective-permute-start(bf16[4,64,384]{2,1,0:T(8,128)(2,1)S(1)} %get-tuple-element.67), channel_id=1, source_target_pairs={{0,1},{1,0},{2,3},{3,2},{4,5},{5,4},{6,7},{7,6},{8,9},{9,8},{10,11... | collective-permute-start | bytes 589832 | tf_op jit(solution)/shard_map/ppermute | solution.py:445
  65.9 15.3 %all-to-all-start.3 = ((bf16[16,24,128]{2,1,0:T(8,128)(2,1)}), bf16[16,24,128]{2,1,0:T(8,128)(2,1)S(1)}, u32[]{:S(2)}, u32[]{:S(2)}) async-start(bf16[16,24,128]{2,1,0:T(8,128)(2,1)} %two_mid.1), calls=%async_computation.3 | async-start | bytes 196608 | tf_op jit(solution)/shard_map/all_to_all | solution.py:483
  81.2 16.2 %all-to-all-start.2 = ((bf16[16,24,768]{2,1,0:T(8,128)(2,1)}), bf16[16,24,768]{2,1,0:T(8,128)(2,1)S(1)}, u32[]{:S(2)}, u32[]{:S(2)}) async-start(bf16[16,24,768]{2,1,0:T(8,128)(2,1)} %one_part.1), calls=%async_computation.2 | async-start | bytes 1179648 | tf_op jit(solution)/shard_map/all_to_all | solution.py:488

commit v5 on v3

--- a/solution.py
+++ b/solution.py
@@ -474,18 +474,18 @@
     g_next = lax.ppermute(g, "frame", prev_perm)
     ht, _, _ = lax.optimization_barrier((ht, gp_next, g))
     two = two_part(ht, keep, ht_other, given)
-    w1, two = lax.optimization_barrier((w1, two))
+    pair3, _ = lax.optimization_barrier((pair3, two))
     two = lax.all_to_all(two, ("dp", "frame"), 0, 0, tiled=True)
-    w1, pair3 = lax.optimization_barrier((load(w1), pair3))
     pair4 = ring(pair3)
-    grad_in = latents_grad(gp, gp_next, cross, inner, w1)
     far1, far2 = inside(pair1), inside(pair2)
-    pair3, far1, far2, _ = lax.optimization_barrier((pair3, far1, far2, grad_in))
+    two, far1, far2 = lax.optimization_barrier((two, far1, far2))
     blocks = (pair0, pair1, pair2, pair3, pair4, far1, far2, inside(pair3))
 
+    two = lax.all_to_all(two_mid(two), "height", 0, 0, tiled=True)
     one = one_part(g, g_next, blocks)
+    one, w1, cross, inner = lax.optimization_barrier((one, w1, cross, inner))
     one = lax.all_to_all(one, ("dp", "frame"), 0, 0, tiled=True)
-    two = lax.all_to_all(two_mid(two), "height", 0, 0, tiled=True)
+    grad_in = latents_grad(gp, gp_next, cross, inner, load(w1))
     one = final_one(one).reshape(3, 3, 3, 24, 24)
     two = jnp.swapaxes(final_two(two).reshape(3, 3, 12, 24), 2, 3)
     return (grad_in[None], one, two)

time: 97.5 us -> 97.4 us (level)
  waiting for transfers between devices: 24.7 us -> 18.3 us
  starting transfers between devices: 42 us -> 46.6 us
  local copies, waits for them, and re-layouts: 1.94 us -> 3.69 us
    all_to_all x1, waiting for transfers between devices: 11.8 us -> 3.97 us  [local(): one = lax.all_to_all(one, ('dp', 'frame'), 0, 0, tiled=True)]
    ppermute x1, waiting for transfers between devices: 0.01 us -> 3.81 us  [local(): gp_next = lax.ppermute(gp, 'frame', prev_perm)]
    all_to_all x1, waiting for transfers between devices: 4.64 us -> 1.59 us  [local(): g = lax.all_to_all(gpt, 'height', 0, 0, tiled=True)]
    all_to_all x1, waiting for transfers between devices: 3.77 us -> 5.84 us  [local(): two = lax.all_to_all(two, ('dp', 'frame'), 0, 0, tiled=True)]
    all_to_all x1, starting transfers between devices: 4.53 us -> 6.34 us  [local(): two = lax.all_to_all(two, ('dp', 'frame'), 0, 0, tiled=True)]
    unnamed x10 -> x14, local copies, waits for them, and re-layouts: 1.94 us -> 3.69 us
    all_to_all x1, starting transfers between devices: 3.58 us -> 4.77 us  [local(): one = lax.all_to_all(one, ('dp', 'frame'), 0, 0, tiled=True)]
    ppermute x2, starting transfers between devices: 1.24 us -> 2.36 us  [across(): return lax.ppermute(value, 'height', cross_perm)]
where the time goes in v5:
time: 97.4 us; the launch traced here: 96.8 us
  starting transfers between devices  46.6 us (48%)
  Pallas kernels  27.5 us (28%)
  waiting for transfers between devices  18.3 us (19%)
  local copies, waits for them, and re-layouts  3.69 us (4%)
    ppermute x4, starting transfers between devices, ring(): return lax.ppermute(value, 'height', ring_perm)  11 us
    ppermute x8, starting transfers between devices, inside(): return lax.ppermute(value, 'height', inner_perm)  8.32 us
    pallas_call x2, Pallas kernels, load(): pl.pallas_call(load_kernel, in_specs=anywhere(1), out_specs=vmem(1)[0], o...  6.7 us
    all_to_all x1, starting transfers between devices, local(): two = lax.all_to_all(two, ('dp', 'frame'), 0, 0, tiled=True)  6.34 us
    pallas_call x1, Pallas kernels, one_part(): pl.pallas_call(one_kernel, in_specs=anywhere(10), out_specs=vmem(1)[0], o...  6.33 us
    all_to_all x1, waiting for transfers between devices, local(): two = lax.all_to_all(two, ('dp', 'frame'), 0, 0, tiled=True)  5.84 us
    pallas_call x1, Pallas kernels, forward(): pl.pallas_call(forward_kernel, in_specs=vmem(5) + anywhere(1) + vmem(1),...  5.8 us
    all_to_all x1, starting transfers between devices, local(): one = lax.all_to_all(one, ('dp', 'frame'), 0, 0, tiled=True)  4.77 us
  transfers between devices with their start and end apart: 21, of which 7 were waited for; matrix products, arithmetic and copies ran while one was open for 0% of the time, Pallas kernels for 27%

profile of v5, /device:TPU:1, one launch (start us, length us, event | category | flops | bytes accessed | tf_op | source)
XLA Modules:
  0.0 96.8 jit_solution(7901911386567699357)
XLA Ops:
  0.6 3.3 %collective-permute-start.1 = (bf16[2,2,64,384]{3,2,1,0:T(8,128)(2,1)}, bf16[2,2,64,384]{3,2,1,0:T(8,128)(2,1)S(1)}, u32[]{:S(2)}, u32[]{:S(2)}) collective-permute-start(bf16[2,2,64,384]{3,2,1,0:T(8,128)(2,1)} %bitcast.13), channel_id=1, source_target_pairs={{0,1},{1,0},{2,3},{3,2},{4,5},{5,4},{6,7},{7,6},{8,9},{9,8},{10,11... | collective-permute-start | bytes 589832 | tf_op jit(solution)/shard_map/ppermute | solution.py:445
  4.0 0.0 collective-permute-start
  4.0 1.3 %collective-permute-done.1.other = bf16[2,2,64,384]{3,2,1,0:T(8,128)(2,1)S(1)} collective-permute-done((bf16[2,2,64,384]{3,2,1,0:T(8,128)(2,1)}, bf16[2,2,64,384]{3,2,1,0:T(8,128)(2,1)S(1)}, u32[]{:S(2)}, u32[]{:S(2)}) %collective-permute-start.1) | collective-permute-done | bytes 196640 | tf_op jit(solution)/shard_map/ppermute | solution.py:445
  5.2 0.9 copy-done
  6.2 1.0 %copy-done.2 = bf16[1,2,4,128,192]{3,4,2,1,0:T(8,128)(2,1)S(1)} copy-done((bf16[1,2,4,128,192]{3,4,2,1,0:T(8,128)(2,1)S(1)}, bf16[1,2,4,128,192]{3,4,2,1,0:T(8,128)(2,1)}, u32[]{:S(2)}) %copy-start.2) | copy-done | bytes 393240
  7.2 0.1 pair.1
  7.2 3.9 %collective-permute-start.2 = (bf16[2,2,2,64,384]{4,3,2,1,0:T(8,128)(2,1)S(1)}, bf16[2,2,2,64,384]{4,3,2,1,0:T(8,128)(2,1)S(1)}, u32[]{:S(2)}, u32[]{:S(2)}) collective-permute-start(bf16[2,2,2,64,384]{4,3,2,1,0:T(8,128)(2,1)S(1)} %get-tuple-element.32.rest_0_), channel_id=1, source_target_pairs={{0,2},{1,15},{2,4},{3,1},{4,6},{5,3},{6,8},{7,5},{8,10},{9,7},{10,... | collective-permute-start | bytes 1179656 | tf_op jit(solution)/shard_map/ppermute | solution.py:451
  11.2 0.7 collective-permute-done.prev
  11.8 0.1 edges.1
  11.9 0.0 copy-start.1
  11.9 0.0 copy-start.3
  11.9 0.0 copy-start.4
  11.9 0.7 collective-permute-start.3
  12.7 3.6 %collective-permute-start.4 = (bf16[6,64,384]{2,1,0:T(8,128)(2,1)S(1)}, bf16[6,64,384]{2,1,0:T(8,128)(2,1)S(1)}, u32[]{:S(2)}, u32[]{:S(2)}) collective-permute-start(bf16[6,64,384]{2,1,0:T(8,128)(2,1)S(1)} %get-tuple-element.39), channel_id=1, source_target_pairs={{0,1},{1,0},{2,3},{3,2},{4,5},{5,4},{6,7},{7,6},{8,9},{9,8},{10,11... | collective-permute-start | bytes 884744 | tf_op jit(solution)/shard_map/ppermute | solution.py:445
  16.3 3.3 %load.2.wv = bf16[27,384,384]{2,1,0:T(8,128)(2,1)S(1)} custom-call(bf16[27,384,384]{2,1,0:T(8,128)(2,1)} %bitcast.21), custom_call_target="tpu_custom_call" | custom-call | flops 2000 | bytes 16000000 | tf_op jit(solution)/shard_map/load/pallas_call | solution.py:86
  19.6 0.0 collective-permute-done.2.rest_1_
  19.6 3.6 %collective-permute-start.7 = (bf16[2,2,2,64,384]{4,3,2,1,0:T(8,128)(2,1)S(1)}, bf16[2,2,2,64,384]{4,3,2,1,0:T(8,128)(2,1)}, u32[]{:S(2)}, u32[]{:S(2)}) collective-permute-start(bf16[2,2,2,64,384]{4,3,2,1,0:T(8,128)(2,1)S(1)} %collective-permute-done.2.rest_1_), channel_id=1, source_target_pairs={{0,2},{1,15},{2,4},{3,1},{4,6},{5,3},{6,8},{7,5},{8,10},{9,7},{10,... | collective-permute-start | bytes 1179656 | tf_op jit(solution)/shard_map/ppermute | solution.py:451
  23.2 5.8 %forward.1 = (bf16[2,2,64,384]{3,2,1,0:T(8,128)(2,1)S(1)}, bf16[16,24,256]{2,1,0:T(8,128)(2,1)}, bf16[384,256]{1,0:T(8,128)(2,1)S(1)}, bf16[256,864]{1,0:T(8,128)(2,1)S(1)}, bf16[256,864]{1,0:T(8,128)(2,1)S(1)}) custom-call(bf16[2,2,64,384]{3,2,1,0:T(8,128)(2,1)S(1)} %bitcast.17, bf16[2,2,64,384]{3,2,1,0:T(8,128)(2,1)S(1)} %collective-permute-done.prev, ...), custom_call_target="tpu_custom_call" | custom-call | flops 2600000000 | bytes 12000000 | tf_op jit(solution)/shard_map/forward/pallas_call | solution.py:209
  29.0 0.1 collective-permute-start.10
  29.1 4.4 %all-to-all-start = ((bf16[16,24,256]{2,1,0:T(8,128)(2,1)}), bf16[16,24,256]{2,1,0:T(8,128)(2,1)S(1)}, u32[]{:S(2)}, u32[]{:S(2)}) async-start(bf16[16,24,256]{2,1,0:T(8,128)(2,1)} %get-tuple-element.44), calls=%async_computation | async-start | bytes 393216 | tf_op jit(solution)/shard_map/all_to_all | solution.py:468
  33.6 2.1 %collective-permute-start.5 = (bf16[2,2,64,384]{3,2,1,0:T(8,128)(2,1)S(1)}, bf16[2,2,64,384]{3,2,1,0:T(8,128)(2,1)S(1)}, u32[]{:S(2)}, u32[]{:S(2)}) collective-permute-start(bf16[2,2,64,384]{3,2,1,0:T(8,128)(2,1)S(1)} %get-tuple-element.43.own), channel_id=1, source_target_pairs={{16,0},{32,16},{48,32},{0,48},{17,1},{33,17},{49,33},{1,49},{18,2}... | collective-permute-start | bytes 589832 | tf_op jit(solution)/shard_map/ppermute | solution.py:467
  35.6 0.5 collective-permute-start.9
  36.1 3.8 %collective-permute-done.5.after = bf16[2,2,64,384]{3,2,1,0:T(8,128)(2,1)S(1)} collective-permute-done((bf16[2,2,64,384]{3,2,1,0:T(8,128)(2,1)S(1)}, bf16[2,2,64,384]{3,2,1,0:T(8,128)(2,1)S(1)}, u32[]{:S(2)}, u32[]{:S(2)}) %collective-permute-start.5) | collective-permute-done | bytes 196640 | tf_op jit(solution)/shard_map/ppermute | solution.py:467
  39.9 2.4 %collective-permute-start.8 = (bf16[2,2,2,64,384]{4,3,2,1,0:T(8,128)(2,1)}, bf16[2,2,2,64,384]{4,3,2,1,0:T(8,128)(2,1)}, u32[]{:S(2)}, u32[]{:S(2)}) collective-permute-start(bf16[2,2,2,64,384]{4,3,2,1,0:T(8,128)(2,1)} %collective-permute-done.7.rest_2_), channel_id=1, source_target_pairs={{0,2},{1,15},{2,4},{3,1},{4,6},{5,3},{6,8},{7,5},{8,10},{9,7},{10,... | collective-permute-start | bytes 1179656 | tf_op jit(solution)/shard_map/ppermute | solution.py:451
  42.3 1.6 %all-to-all-done.g_in = bf16[16,24,256]{2,1,0:T(8,128)(2,1)S(1)} async-done(((bf16[16,24,256]{2,1,0:T(8,128)(2,1)}), bf16[16,24,256]{2,1,0:T(8,128)(2,1)S(1)}, u32[]{:S(2)}, u32[]{:S(2)}) %all-to-all-start) | async-done | bytes 196640 | tf_op jit(solution)/shard_map/all_to_all | solution.py:468
  43.9 1.4 %two_part.1 = bf16[16,24,864]{2,1,0:T(8,128)(2,1)} custom-call(bf16[384,256]{1,0:T(8,128)(2,1)S(1)} %get-tuple-element.48.ht, bf16[256,864]{1,0:T(8,128)(2,1)S(1)} %get-tuple-element.49.keep, bf16[384,256]{1,0:T(8,128)(2,1)S(1)} %collective-permute-done.9.ht_other, bf16[256,864]{1,0:T(8,128)(2,1)S(1)} %collective-permute-done.10.given), custom_call_target="tpu_custom_call" | custom-call | flops 340000000 | bytes 3000000 | tf_op jit(solution)/shard_map/two_part/pallas_call | solution.py:261
  45.3 6.3 %all-to-all-start.1 = ((bf16[16,24,864]{2,1,0:T(8,128)(2,1)}), bf16[16,24,864]{2,1,0:T(8,128)(2,1)S(1)}, u32[]{:S(2)}, u32[]{:S(2)}) async-start(bf16[16,24,864]{2,1,0:T(8,128)(2,1)} %two_part.1), calls=%async_computation.1 | async-start | bytes 1376256 | tf_op jit(solution)/shard_map/all_to_all | solution.py:478
  51.7 0.1 collective-permute-start.12
  51.8 0.5 collective-permute-start.13
  52.3 0.1 collective-permute-start.14
  52.4 1.1 %collective-permute-start.11 = (bf16[2,2,2,64,384]{4,3,2,1,0:T(8,128)(2,1)}, bf16[2,2,2,64,384]{4,3,2,1,0:T(8,128)(2,1)}, u32[]{:S(2)}, u32[]{:S(2)}) collective-permute-start(bf16[2,2,2,64,384]{4,3,2,1,0:T(8,128)(2,1)} %collective-permute-done.8.rest_3_), channel_id=1, source_target_pairs={{0,2},{1,15},{2,4},{3,1},{4,6},{5,3},{6,8},{7,5},{8,10},{9,7},{10,... | collective-permute-start | bytes 1179656 | tf_op jit(solution)/shard_map/ppermute | solution.py:451
  53.5 2.8 %collective-permute-start.6 = (bf16[16,24,256]{2,1,0:T(8,128)(2,1)S(1)}, bf16[16,24,256]{2,1,0:T(8,128)(2,1)S(1)}, u32[]{:S(2)}, u32[]{:S(2)}) collective-permute-start(bf16[16,24,256]{2,1,0:T(8,128)(2,1)S(1)} %all-to-all-done.g_in), channel_id=1, source_target_pairs={{16,0},{32,16},{48,32},{0,48},{17,1},{33,17},{49,33},{1,49},{18,2}... | collective-permute-start | bytes 589832 | tf_op jit(solution)/shard_map/ppermute | solution.py:474
  56.3 0.7 rows.1
  57.0 1.6 %collective-permute-start.15 = (bf16[4,64,384]{2,1,0:T(8,128)(2,1)}, bf16[4,64,384]{2,1,0:T(8,128)(2,1)S(1)}, u32[]{:S(2)}, u32[]{:S(2)}) collective-permute-start(bf16[4,64,384]{2,1,0:T(8,128)(2,1)} %get-tuple-element.54), channel_id=1, source_target_pairs={{0,15},{1,2},{2,1},{3,4},{4,3},{5,6},{6,5},{7,8},{8,7},{9,10},{10,... | collective-permute-start | bytes 589832 | tf_op jit(solution)/shard_map/ppermute | solution.py:448
  58.6 0.8 copy-done.5
  59.4 0.2 collective-permute-start.16
  59.5 5.8 %all-to-all-done.1.parts = bf16[16,24,864]{2,1,0:T(8,128)(2,1)S(1)} async-done(((bf16[16,24,864]{2,1,0:T(8,128)(2,1)}), bf16[16,24,864]{2,1,0:T(8,128)(2,1)S(1)}, u32[]{:S(2)}, u32[]{:S(2)}) %all-to-all-start.1) | async-done | bytes 663584 | tf_op jit(solution)/shard_map/all_to_all | solution.py:478
  65.4 0.9 two_mid.1
  66.3 4.5 %all-to-all-start.3 = ((bf16[16,24,128]{2,1,0:T(8,128)(2,1)}), bf16[16,24,128]{2,1,0:T(8,128)(2,1)S(1)}, u32[]{:S(2)}, u32[]{:S(2)}) async-start(bf16[16,24,128]{2,1,0:T(8,128)(2,1)} %two_mid.1), calls=%async_computation.3 | async-start | bytes 196608 | tf_op jit(solution)/shard_map/all_to_all | solution.py:484
  70.8 1.0 %copy-done.6 = bf16[2,2,2,64,384]{4,3,2,1,0:T(8,128)(2,1)S(1)} copy-done((bf16[2,2,2,64,384]{4,3,2,1,0:T(8,128)(2,1)S(1)}, bf16[2,2,2,64,384]{4,3,2,1,0:T(8,128)(2,1)}, u32[]{:S(2)}) %copy-start.6) | copy-done | bytes 393240
  71.8 6.3 %one_part.1 = bf16[16,24,768]{2,1,0:T(8,128)(2,1)} custom-call(bf16[16,24,256]{2,1,0:T(8,128)(2,1)S(1)} %all-to-all-done.g_in, bf16[16,24,256]{2,1,0:T(8,128)(2,1)S(1)} %collective-permute-done.6.g_after_in, bf16[2,2,2,64,384]{4,3,2,1,0:T(8,128)(2,1)S(1)} %get-tuple-element.32.rest_0_, bf16[2,2,2,64,384]{4,3,2,1,0:T(8,128)(2,1)S(1)} %collective-permute-done.2.rest_1_, ...), custom_call_target="tpu_custom_call" | custom-call | flops 2040000000 | bytes 5000000 | tf_op jit(solution)/shard_map/one_part/pallas_call | solution.py:353
  78.1 1.1 %all-to-all-done.3.parts = bf16[16,24,128]{2,1,0:T(8,128)(2,1)S(1)} async-done(((bf16[16,24,128]{2,1,0:T(8,128)(2,1)}), bf16[16,24,128]{2,1,0:T(8,128)(2,1)S(1)}, u32[]{:S(2)}, u32[]{:S(2)}) %all-to-all-start.3) | async-done | bytes 98336 | tf_op jit(solution)/shard_map/all_to_all | solution.py:484
  79.2 4.8 %all-to-all-start.2 = ((bf16[16,24,768]{2,1,0:T(8,128)(2,1)}), bf16[16,24,768]{2,1,0:T(8,128)(2,1)S(1)}, u32[]{:S(2)}, u32[]{:S(2)}) async-start(bf16[16,24,768]{2,1,0:T(8,128)(2,1)} %one_part.1), calls=%async_computation.2 | async-start | bytes 1179648 | tf_op jit(solution)/shard_map/all_to_all | solution.py:487
  84.0 3.4 %load.3.wv = bf16[27,384,384]{2,1,0:T(8,128)(2,1)S(1)} custom-call(bf16[27,384,384]{2,1,0:T(8,128)(2,1)} %bitcast.22), custom_call_target="tpu_custom_call" | custom-call | flops 2000 | bytes 16000000 | tf_op jit(solution)/shard_map/load/pallas_call | solution.py:86
  87.4 3.8 %latents_grad.1 = bf16[2,2,64,384]{3,2,1,0:T(8,128)(2,1)} custom-call(bf16[2,2,64,384]{3,2,1,0:T(8,128)(2,1)S(1)} %get-tuple-element.43.own, bf16[2,2,64,384]{3,2,1,0:T(8,128)(2,1)S(1)} %collective-permute-done.5.after, bf16[4,64,384]{2,1,0:T(8,128)(2,1)S(1)} %collective-permute-done.15.cross, bf16[4,64,384]{2,1,0:T(8,128)(2,1)S(1)} %collective-permute-done.16.inner, ...), custom_call_target="tpu_custom_call" | custom-call | flops 2040000000 | bytes 10000000 | tf_op jit(solution)/shard_map/latents_grad/pallas_call | solution.py:287
  91.2 0.7 final_two.1
  91.9 4.0 %all-to-all-done.2.parts = bf16[16,24,768]{2,1,0:T(8,128)(2,1)S(1)} async-done(((bf16[16,24,768]{2,1,0:T(8,128)(2,1)}), bf16[16,24,768]{2,1,0:T(8,128)(2,1)S(1)}, u32[]{:S(2)}, u32[]{:S(2)}) %all-to-all-start.2) | async-done | bytes 589856 | tf_op jit(solution)/shard_map/all_to_all | solution.py:487
  95.9 0.9 final_one.1
  (20 shorter events, 0.0 us)
Async XLA Ops:
  0.6 4.6 %collective-permute-start.1 = (bf16[2,2,64,384]{3,2,1,0:T(8,128)(2,1)}, bf16[2,2,64,384]{3,2,1,0:T(8,128)(2,1)S(1)}, u32[]{:S(2)}, u32[]{:S(2)}) collective-permute-start(bf16[2,2,64,384]{3,2,1,0:T(8,128)(2,1)} %bitcast.13), channel_id=1, source_target_pairs={{0,1},{1,0},{2,3},{3,2},{4,5},{5,4},{6,7},{7,6},{8,9},{9,8},{10,11... | collective-permute-start | bytes 589832 | tf_op jit(solution)/shard_map/ppermute | solution.py:445
  4.0 7.9 %collective-permute-start = (bf16[2,2,64,384]{3,2,1,0:T(8,128)(2,1)}, bf16[2,2,64,384]{3,2,1,0:T(8,128)(2,1)S(1)}, u32[]{:S(2)}, u32[]{:S(2)}) collective-permute-start(bf16[2,2,64,384]{3,2,1,0:T(8,128)(2,1)} %bitcast.14), channel_id=1, source_target_pairs={{0,16},{16,32},{32,48},{48,0},{1,17},{17,33},{33,49},{49,1},{2,18}... | collective-permute-start | bytes 589832 | tf_op jit(solution)/shard_map/ppermute | solution.py:456
  5.2 0.9 copy-start
  6.2 1.0 %copy-start.2 = (bf16[1,2,4,128,192]{3,4,2,1,0:T(8,128)(2,1)S(1)}, bf16[1,2,4,128,192]{3,4,2,1,0:T(8,128)(2,1)}, u32[]{:S(2)}) copy-start(bf16[1,2,4,128,192]{3,4,2,1,0:T(8,128)(2,1)} %param.7) | copy-start | bytes 1179652
  7.2 12.4 %collective-permute-start.2 = (bf16[2,2,2,64,384]{4,3,2,1,0:T(8,128)(2,1)S(1)}, bf16[2,2,2,64,384]{4,3,2,1,0:T(8,128)(2,1)S(1)}, u32[]{:S(2)}, u32[]{:S(2)}) collective-permute-start(bf16[2,2,2,64,384]{4,3,2,1,0:T(8,128)(2,1)S(1)} %get-tuple-element.32.rest_0_), channel_id=1, source_target_pairs={{0,2},{1,15},{2,4},{3,1},{4,6},{5,3},{6,8},{7,5},{8,10},{9,7},{10,... | collective-permute-start | bytes 1179656 | tf_op jit(solution)/shard_map/ppermute | solution.py:451
  11.9 11.3 %copy-start.1 = (bf16[1,2,2,64,384]{4,3,2,1,0:T(8,128)(2,1)S(1)}, bf16[1,2,2,64,384]{4,3,2,1,0:T(8,128)(2,1)}, u32[]{:S(2)}) copy-start(bf16[1,2,2,64,384]{4,3,2,1,0:T(8,128)(2,1)} %param.4) | copy-start | bytes 589828
  11.9 11.3 %copy-start.3 = (bf16[1,2,4,128,192]{3,4,2,1,0:T(8,128)(2,1)S(1)}, bf16[1,2,4,128,192]{3,4,2,1,0:T(8,128)(2,1)}, u32[]{:S(2)}) copy-start(bf16[1,2,4,128,192]{3,4,2,1,0:T(8,128)(2,1)} %param.7) | copy-start | bytes 1179652
  11.9 11.3 %copy-start.4 = (bf16[3,3,384,192]{2,3,1,0:T(8,128)(2,1)S(1)}, bf16[3,3,384,192]{2,3,1,0:T(8,128)(2,1)}, u32[]{:S(2)}) copy-start(bf16[3,3,384,192]{2,3,1,0:T(8,128)(2,1)} %param.6) | copy-start | bytes 3981316
  11.9 7.7 %collective-permute-start.3 = (bf16[6,64,384]{2,1,0:T(8,128)(2,1)S(1)}, bf16[6,64,384]{2,1,0:T(8,128)(2,1)S(1)}, u32[]{:S(2)}, u32[]{:S(2)}) collective-permute-start(bf16[6,64,384]{2,1,0:T(8,128)(2,1)S(1)} %get-tuple-element.38), channel_id=1, source_target_pairs={{0,15},{1,2},{2,1},{3,4},{4,3},{5,6},{6,5},{7,8},{8,7},{9,10},{10,... | collective-permute-start | bytes 884744 | tf_op jit(solution)/shard_map/ppermute | solution.py:448
  12.7 6.9 %collective-permute-start.4 = (bf16[6,64,384]{2,1,0:T(8,128)(2,1)S(1)}, bf16[6,64,384]{2,1,0:T(8,128)(2,1)S(1)}, u32[]{:S(2)}, u32[]{:S(2)}) collective-permute-start(bf16[6,64,384]{2,1,0:T(8,128)(2,1)S(1)} %get-tuple-element.39), channel_id=1, source_target_pairs={{0,1},{1,0},{2,3},{3,2},{4,5},{5,4},{6,7},{7,6},{8,9},{9,8},{10,11... | collective-permute-start | bytes 884744 | tf_op jit(solution)/shard_map/ppermute | solution.py:445
  19.6 20.3 %collective-permute-start.7 = (bf16[2,2,2,64,384]{4,3,2,1,0:T(8,128)(2,1)S(1)}, bf16[2,2,2,64,384]{4,3,2,1,0:T(8,128)(2,1)}, u32[]{:S(2)}, u32[]{:S(2)}) collective-permute-start(bf16[2,2,2,64,384]{4,3,2,1,0:T(8,128)(2,1)S(1)} %collective-permute-done.2.rest_1_), channel_id=1, source_target_pairs={{0,2},{1,15},{2,4},{3,1},{4,6},{5,3},{6,8},{7,5},{8,10},{9,7},{10,... | collective-permute-start | bytes 1179656 | tf_op jit(solution)/shard_map/ppermute | solution.py:451
  29.0 14.9 %collective-permute-start.10 = (bf16[256,864]{1,0:T(8,128)(2,1)S(1)}, bf16[256,864]{1,0:T(8,128)(2,1)S(1)}, u32[]{:S(2)}, u32[]{:S(2)}) collective-permute-start(bf16[256,864]{1,0:T(8,128)(2,1)S(1)} %get-tuple-element.50), channel_id=1, source_target_pairs={{0,1},{1,0},{2,3},{3,2},{4,5},{5,4},{6,7},{7,6},{8,9},{9,8},{10,11... | collective-permute-start | bytes 1327112 | tf_op jit(solution)/shard_map/ppermute | solution.py:445
  29.1 14.8 %all-to-all-start = ((bf16[16,24,256]{2,1,0:T(8,128)(2,1)}), bf16[16,24,256]{2,1,0:T(8,128)(2,1)S(1)}, u32[]{:S(2)}, u32[]{:S(2)}) async-start(bf16[16,24,256]{2,1,0:T(8,128)(2,1)} %get-tuple-element.44), calls=%async_computation | async-start | bytes 393216 | tf_op jit(solution)/shard_map/all_to_all | solution.py:468
  33.6 6.3 %collective-permute-start.5 = (bf16[2,2,64,384]{3,2,1,0:T(8,128)(2,1)S(1)}, bf16[2,2,64,384]{3,2,1,0:T(8,128)(2,1)S(1)}, u32[]{:S(2)}, u32[]{:S(2)}) collective-permute-start(bf16[2,2,64,384]{3,2,1,0:T(8,128)(2,1)S(1)} %get-tuple-element.43.own), channel_id=1, source_target_pairs={{16,0},{32,16},{48,32},{0,48},{17,1},{33,17},{49,33},{1,49},{18,2}... | collective-permute-start | bytes 589832 | tf_op jit(solution)/shard_map/ppermute | solution.py:467
  35.6 8.3 %collective-permute-start.9 = (bf16[384,256]{1,0:T(8,128)(2,1)S(1)}, bf16[384,256]{1,0:T(8,128)(2,1)S(1)}, u32[]{:S(2)}, u32[]{:S(2)}) collective-permute-start(bf16[384,256]{1,0:T(8,128)(2,1)S(1)} %get-tuple-element.48.ht), channel_id=1, source_target_pairs={{0,1},{1,0},{2,3},{3,2},{4,5},{5,4},{6,7},{7,6},{8,9},{9,8},{10,11... | collective-permute-start | bytes 589832 | tf_op jit(solution)/shard_map/ppermute | solution.py:445
  39.9 12.4 %collective-permute-start.8 = (bf16[2,2,2,64,384]{4,3,2,1,0:T(8,128)(2,1)}, bf16[2,2,2,64,384]{4,3,2,1,0:T(8,128)(2,1)}, u32[]{:S(2)}, u32[]{:S(2)}) collective-permute-start(bf16[2,2,2,64,384]{4,3,2,1,0:T(8,128)(2,1)} %collective-permute-done.7.rest_2_), channel_id=1, source_target_pairs={{0,2},{1,15},{2,4},{3,1},{4,6},{5,3},{6,8},{7,5},{8,10},{9,7},{10,... | collective-permute-start | bytes 1179656 | tf_op jit(solution)/shard_map/ppermute | solution.py:451
  45.3 20.0 %all-to-all-start.1 = ((bf16[16,24,864]{2,1,0:T(8,128)(2,1)}), bf16[16,24,864]{2,1,0:T(8,128)(2,1)S(1)}, u32[]{:S(2)}, u32[]{:S(2)}) async-start(bf16[16,24,864]{2,1,0:T(8,128)(2,1)} %two_part.1), calls=%async_computation.1 | async-start | bytes 1376256 | tf_op jit(solution)/shard_map/all_to_all | solution.py:478
  51.7 5.3 %collective-permute-start.12 = (bf16[2,2,2,64,384]{4,3,2,1,0:T(8,128)(2,1)S(1)}, bf16[2,2,2,64,384]{4,3,2,1,0:T(8,128)(2,1)S(1)}, u32[]{:S(2)}, u32[]{:S(2)}) collective-permute-start(bf16[2,2,2,64,384]{4,3,2,1,0:T(8,128)(2,1)S(1)} %collective-permute-done.2.rest_1_), channel_id=1, source_target_pairs={{0,1},{1,0},{2,3},{3,2},{4,5},{5,4},{6,7},{7,6},{8,9},{9,8},{10,11... | collective-permute-start | bytes 1179656 | tf_op jit(solution)/shard_map/ppermute | solution.py:445
  51.8 6.8 %collective-permute-start.13 = (bf16[2,2,2,64,384]{4,3,2,1,0:T(8,128)(2,1)}, bf16[2,2,2,64,384]{4,3,2,1,0:T(8,128)(2,1)S(1)}, u32[]{:S(2)}, u32[]{:S(2)}) collective-permute-start(bf16[2,2,2,64,384]{4,3,2,1,0:T(8,128)(2,1)} %collective-permute-done.7.rest_2_), channel_id=1, source_target_pairs={{0,1},{1,0},{2,3},{3,2},{4,5},{5,4},{6,7},{7,6},{8,9},{9,8},{10,11... | collective-permute-start | bytes 1179656 | tf_op jit(solution)/shard_map/ppermute | solution.py:445
  52.3 18.5 %collective-permute-start.14 = (bf16[2,2,2,64,384]{4,3,2,1,0:T(8,128)(2,1)}, bf16[2,2,2,64,384]{4,3,2,1,0:T(8,128)(2,1)}, u32[]{:S(2)}, u32[]{:S(2)}) collective-permute-start(bf16[2,2,2,64,384]{4,3,2,1,0:T(8,128)(2,1)} %collective-permute-done.8.rest_3_), channel_id=1, source_target_pairs={{0,1},{1,0},{2,3},{3,2},{4,5},{5,4},{6,7},{7,6},{8,9},{9,8},{10,11... | collective-permute-start | bytes 1179656 | tf_op jit(solution)/shard_map/ppermute | solution.py:445
  52.4 18.4 %collective-permute-start.11 = (bf16[2,2,2,64,384]{4,3,2,1,0:T(8,128)(2,1)}, bf16[2,2,2,64,384]{4,3,2,1,0:T(8,128)(2,1)}, u32[]{:S(2)}, u32[]{:S(2)}) collective-permute-start(bf16[2,2,2,64,384]{4,3,2,1,0:T(8,128)(2,1)} %collective-permute-done.8.rest_3_), channel_id=1, source_target_pairs={{0,2},{1,15},{2,4},{3,1},{4,6},{5,3},{6,8},{7,5},{8,10},{9,7},{10,... | collective-permute-start | bytes 1179656 | tf_op jit(solution)/shard_map/ppermute | solution.py:451
  53.5 17.3 %collective-permute-start.6 = (bf16[16,24,256]{2,1,0:T(8,128)(2,1)S(1)}, bf16[16,24,256]{2,1,0:T(8,128)(2,1)S(1)}, u32[]{:S(2)}, u32[]{:S(2)}) collective-permute-start(bf16[16,24,256]{2,1,0:T(8,128)(2,1)S(1)} %all-to-all-done.g_in), channel_id=1, source_target_pairs={{16,0},{32,16},{48,32},{0,48},{17,1},{33,17},{49,33},{1,49},{18,2}... | collective-permute-start | bytes 589832 | tf_op jit(solution)/shard_map/ppermute | solution.py:474
  57.0 21.1 %collective-permute-start.15 = (bf16[4,64,384]{2,1,0:T(8,128)(2,1)}, bf16[4,64,384]{2,1,0:T(8,128)(2,1)S(1)}, u32[]{:S(2)}, u32[]{:S(2)}) collective-permute-start(bf16[4,64,384]{2,1,0:T(8,128)(2,1)} %get-tuple-element.54), channel_id=1, source_target_pairs={{0,15},{1,2},{2,1},{3,4},{4,3},{5,6},{6,5},{7,8},{8,7},{9,10},{10,... | collective-permute-start | bytes 589832 | tf_op jit(solution)/shard_map/ppermute | solution.py:448
  58.6 0.8 copy-start.5
  59.4 18.8 %collective-permute-start.16 = (bf16[4,64,384]{2,1,0:T(8,128)(2,1)S(1)}, bf16[4,64,384]{2,1,0:T(8,128)(2,1)S(1)}, u32[]{:S(2)}, u32[]{:S(2)}) collective-permute-start(bf16[4,64,384]{2,1,0:T(8,128)(2,1)S(1)} %get-tuple-element.55), channel_id=1, source_target_pairs={{0,1},{1,0},{2,3},{3,2},{4,5},{5,4},{6,7},{7,6},{8,9},{9,8},{10,11... | collective-permute-start | bytes 589832 | tf_op jit(solution)/shard_map/ppermute | solution.py:445
  66.3 13.0 %all-to-all-start.3 = ((bf16[16,24,128]{2,1,0:T(8,128)(2,1)}), bf16[16,24,128]{2,1,0:T(8,128)(2,1)S(1)}, u32[]{:S(2)}, u32[]{:S(2)}) async-start(bf16[16,24,128]{2,1,0:T(8,128)(2,1)} %two_mid.1), calls=%async_computation.3 | async-start | bytes 196608 | tf_op jit(solution)/shard_map/all_to_all | solution.py:484
  70.8 1.0 %copy-start.6 = (bf16[2,2,2,64,384]{4,3,2,1,0:T(8,128)(2,1)S(1)}, bf16[2,2,2,64,384]{4,3,2,1,0:T(8,128)(2,1)}, u32[]{:S(2)}) copy-start(bf16[2,2,2,64,384]{4,3,2,1,0:T(8,128)(2,1)} %copy-done.5) | copy-start | bytes 1179652
  79.2 16.7 %all-to-all-start.2 = ((bf16[16,24,768]{2,1,0:T(8,128)(2,1)}), bf16[16,24,768]{2,1,0:T(8,128)(2,1)S(1)}, u32[]{:S(2)}, u32[]{:S(2)}) async-start(bf16[16,24,768]{2,1,0:T(8,128)(2,1)} %one_part.1), calls=%async_computation.2 | async-start | bytes 1179648 | tf_op jit(solution)/shard_map/all_to_all | solution.py:487
